TPU v7x, 256 devices: a whole 4x4x8 slice. The times are simulated.
256 devices in a mesh: rep: 4 (over y), ep: 64 (over z, x, core).
Axes of the slice: x: 4, y: 4, z: 8, core: 2. Of those that a mesh axis runs over, the one named last changes fastest.
Arguments:
- tokens: bfloat16 [4096, 3584], P(('rep', 'ep')), may hold values from -6 to 6
- chosen_expert_index: int32 [4096, 8], P(('rep', 'ep')), may hold values from 0 to 127, all different within a row; in each aligned block of 16 rows (0 to 15, 16 to 31, ...) at most 2 rows name the same one
- expert_mixing_weight: bfloat16 [4096, 8], P(('rep', 'ep')), may hold values from 0.099609375 to 0.59765625
- row_adapter_index: int32 [4096], P(('rep', 'ep')), may hold values from 0 to 7
- gate_weight: bfloat16 [128, 3584, 1024], P('ep', None, 'rep'), may hold values from -0.09375 to 0.09375
- up_weight: bfloat16 [128, 3584, 1024], P('ep', None, 'rep'), may hold values from -0.09375 to 0.09375
- down_weight: bfloat16 [128, 1024, 3584], P('ep', None, 'rep'), may hold values from -0.1875 to 0.1875
- adapter_down_factor: bfloat16 [3584, 128], replicated, may hold values from -0.09375 to 0.09375
- adapter_up_factor: bfloat16 [128, 1024], P(None, 'rep'), may hold values from -0.75 to 0.75
Outputs:
- mixed: bfloat16 [4096, 3584], P(('rep', 'ep'))
Inputs may be any that keep to these rules, and one draw needn't show every extreme that they name: `chosen_expert_index`: each row names 8 different experts. Among the rows of one device no expert is named more than 2 times, a bound that some block reaches.
All inputs are finite; a program needn't handle non-finite values.
Results may differ from a plain program's by a relative error of at most 0.0059.
Values may be sent and summed in bfloat16 or wider, within the bound.
No kernel may reach another device: no remote copies, remote signals or barrier semaphores. Data moves between devices by JAX's collectives and lax.ppermute only.
A program may use at most 128 MiB of HBM per device.

v0:
```python
import jax
import jax.numpy as jnp
from jax import lax
from jax.sharding import PartitionSpec as P

ADAPTER_RANK = 16


def per_device(
    tokens,
    chosen_expert_index,
    expert_mixing_weight,
    row_adapter_index,
    gate_weight,
    up_weight,
    down_weight,
    adapter_down_factor,
    adapter_up_factor,
):
    row_count, width = tokens.shape
    top_count = chosen_expert_index.shape[1]
    owners = lax.axis_size("ep")
    groups = lax.axis_size("rep")
    local_count = gate_weight.shape[0]
    experts = local_count * owners
    capacity = max(2, 2 * row_count * top_count // experts)
    slot_count = experts * capacity
    owner_slots = local_count * capacity
    adapter_row_count = adapter_down_factor.shape[1]
    lane_adapter = lax.iota(jnp.int32, adapter_row_count) // ADAPTER_RANK
    adapter_row_mask = (row_adapter_index[:, None] == lane_adapter[None, :]).astype(jnp.float32)
    lowrank_product = (
        jnp.dot(tokens, adapter_down_factor, preferred_element_type=jnp.float32) * adapter_row_mask
    ).astype(jnp.bfloat16)
    flat_ids = chosen_expert_index.reshape(-1)
    one_hot = (flat_ids[:, None] == lax.iota(jnp.int32, experts)[None, :]).astype(jnp.int32)
    before = jnp.cumsum(one_hot, axis=0) - one_hot
    position = jnp.sum(before * one_hot, axis=1)
    slot_index = (flat_ids * capacity + position).reshape(row_count, top_count)
    matches = slot_index[:, :, None] == lax.iota(jnp.int32, slot_count)[None, None, :]
    routing = jnp.any(matches, axis=1).astype(jnp.bfloat16)
    combiner = jnp.sum(
        jnp.where(matches, expert_mixing_weight.astype(jnp.float32)[:, :, None], jnp.float32(0.0)),
        axis=1,
    ).astype(jnp.bfloat16)
    got_rows, got_low, got_route = (
        lax.all_gather(tokens[None], "rep", axis=0, tiled=True),
        lax.all_gather(lowrank_product[None], "rep", axis=0, tiled=True),
        lax.all_gather(routing[None], "rep", axis=0, tiled=True),
    )
    packed = jnp.einsum(
        "gri,grd->gid", got_route, got_rows, preferred_element_type=jnp.float32
    ).astype(jnp.bfloat16)
    packed_low = jnp.einsum(
        "gri,grl->gil", got_route, got_low, preferred_element_type=jnp.float32
    ).astype(jnp.bfloat16)
    packed = packed.reshape(groups, owners, owner_slots, width)
    packed_low = packed_low.reshape(groups, owners, owner_slots, adapter_row_count)
    assembled, gathered_lowrank = (
        lax.all_to_all(packed, "ep", split_axis=1, concat_axis=1, tiled=True),
        lax.all_to_all(packed_low, "ep", split_axis=1, concat_axis=1, tiled=True),
    )
    source_count = groups * owners
    assembled = assembled.reshape(source_count, local_count, capacity, width)
    gathered_lowrank = gathered_lowrank.reshape(
        source_count, local_count, capacity, adapter_row_count
    )
    gate_value = jnp.einsum(
        "mjcd,jdf->mjcf", assembled, gate_weight, preferred_element_type=jnp.float32
    )
    up_projection_value = jnp.einsum(
        "mjcd,jdf->mjcf", assembled, up_weight, preferred_element_type=jnp.float32
    )
    up_projection_value = up_projection_value + jnp.einsum(
        "roqi,ih->roqh", gathered_lowrank, adapter_up_factor, preferred_element_type=jnp.float32
    )
    hidden = (jax.nn.silu(gate_value) * up_projection_value).astype(jnp.bfloat16)
    summed = jnp.einsum(
        "mjcf,jfd->mjcd",
        lax.all_gather(hidden, "rep", axis=3, tiled=True),
        down_weight,
        preferred_element_type=jnp.float32,
    )
    outputs = summed.astype(jnp.bfloat16).reshape(groups, owners, owner_slots, down_weight.shape[2])
    returned = lax.all_to_all(outputs, "ep", split_axis=1, concat_axis=1, tiled=True)
    returned = lax.all_to_all(returned, "rep", split_axis=0, concat_axis=3, tiled=True)
    result = returned.reshape(slot_count, width)
    return jnp.dot(combiner, result, preferred_element_type=jnp.float32).astype(jnp.bfloat16)


def solution(mesh):
    placed = (
        P(("rep", "ep"), None),
        P(("rep", "ep"), None),
        P(("rep", "ep"), None),
        P(("rep", "ep")),
        P("ep", None, "rep"),
        P("ep", None, "rep"),
        P("ep", None, "rep"),
        P(),
        P(None, "rep"),
    )
    return jax.shard_map(
        per_device, mesh=mesh, in_specs=placed, out_specs=P(("rep", "ep"), None), check_vma=False
    )
```

profile of v0, /device:TPU:1, one launch (start us, length us, event | category | flops | bytes accessed | tf_op | source)
XLA Modules:
  0.0 407.3 jit_solution(15059793992752468185)
XLA Ops:
  6.5 0.8 copy.38
  8.2 10.4 %all-gather = bf16[64,256]{1,0:T(8,128)(2,1)S(1)} all-gather(bf16[16,256]{1,0:T(8,128)(2,1)S(1)} %convert_element_type.56), channel_id=2, replica_groups=mesh['rep'=4,'ep'=64] {'rep'}, dimensions={0}, use_global_device_ids=true | all-gather | bytes 40960 | tf_op jit(solution)/shard_map/all_gather | solution.py:49
  18.5 1.1 fusion.17
  19.7 9.0 %all-gather.2 = bf16[64,128]{1,0:T(8,128)(2,1)S(1)} all-gather(bf16[16,128]{1,0:T(8,128)(2,1)S(1)} %fusion.17), channel_id=4, replica_groups=mesh['rep'=4,'ep'=64] {'rep'}, dimensions={0}, use_global_device_ids=true | all-gather | bytes 20480 | tf_op jit(solution)/shard_map/all_gather | solution.py:48
  29.8 17.9 %all-to-all-start.1 = ((bf16[4,64,4,128]{3,2,0,1:T(4,128)(2,1)}), bf16[4,64,4,128]{3,2,0,1:T(4,128)(2,1)S(1)}, u32[]{:S(2)}, u32[]{:S(2)}) async-start(bf16[4,64,4,128]{3,2,0,1:T(4,128)(2,1)} %copy.43), calls=%async_computation.1 | async-start | bytes 524288 | tf_op jit(solution)/shard_map/all_to_all | solution.py:61
  47.7 11.1 %all-gather.1 = bf16[64,3584]{1,0:T(8,128)(2,1)S(1)} all-gather(bf16[16,3584]{1,0:T(8,128)(2,1)} %param.9), channel_id=3, replica_groups=mesh['rep'=4,'ep'=64] {'rep'}, dimensions={0}, use_global_device_ids=true | all-gather | bytes 573440 | tf_op jit(solution)/shard_map/all_gather | solution.py:47
  58.8 5.0 %convolution_convert_fusion = bf16[4,256,3584]{2,1,0:T(8,128)(2,1)} fusion(bf16[4,16,256]{2,1,0:T(8,128)(2,1)S(1)} %bitcast.66, bf16[4,16,3584]{2,1,0:T(8,128)(2,1)S(1)} %bitcast.63), kind=kOutput, calls=%fused_computation | convolution fusion | flops 121110528 | bytes 7831552 | tf_op jit(solution)/shard_map/gri,grd->gid/dot_general | solution.py:51
  63.9 12.6 %reshape.51 = bf16[4,64,4,3584]{3,2,1,0:T(4,128)(2,1)} reshape(bf16[4,256,3584]{2,1,0:T(8,128)(2,1)} %convolution_convert_fusion) | data formatting | bytes 14680064 | tf_op jit(solution)/shard_map/reshape | solution.py:57
  76.5 10.1 %copy.41 = bf16[4,64,4,3584]{3,2,0,1:T(4,128)(2,1)} copy(bf16[4,64,4,3584]{3,2,1,0:T(4,128)(2,1)} %reshape.51) | data formatting | bytes 14680064 | tf_op jit(solution)/shard_map/reshape | solution.py:57
  86.6 12.2 %all-to-all-start = ((bf16[4,64,4,3584]{3,2,0,1:T(4,128)(2,1)}), bf16[4,64,4,3584]{3,2,0,1:T(4,128)(2,1)}, u32[]{:S(2)}, u32[]{:S(2)}) async-start(bf16[4,64,4,3584]{3,2,0,1:T(4,128)(2,1)} %copy.41), calls=%async_computation | async-start | bytes 14680064 | tf_op jit(solution)/shard_map/all_to_all | solution.py:60
  99.1 160.0 %all-to-all-done = bf16[4,64,4,3584]{3,2,0,1:T(4,128)(2,1)} async-done(((bf16[4,64,4,3584]{3,2,0,1:T(4,128)(2,1)}), bf16[4,64,4,3584]{3,2,0,1:T(4,128)(2,1)}, u32[]{:S(2)}, u32[]{:S(2)}) %all-to-all-start) | async-done | bytes 7340064 | tf_op jit(solution)/shard_map/all_to_all | solution.py:60
  259.1 7.2 %copy.42 = bf16[4,64,4,3584]{3,1,0,2:T(8,128)(2,1)S(1)} copy(bf16[4,64,4,3584]{3,2,0,1:T(4,128)(2,1)} %all-to-all-done) | data formatting | bytes 14680064 | tf_op jit(solution)/shard_map/all_to_all | solution.py:60
  266.4 2.1 fusion.12
  268.5 2.1 fusion.9
  270.5 1.2 fusion.16
  271.8 36.0 %all-gather.5.cloned.1.call-done = bf16[256,2,2,1024]{3,0,2,1:T(8,128)(2,1)} async-done(((bf16[256,2,2,256]{3,0,2,1:T(8,128)(2,1)}), bf16[256,2,2,1024]{3,0,2,1:T(8,128)(2,1)}) %all-gather.5.cloned.1.call-update) | async-done | bytes 2097168 | tf_op jit(solution)/shard_map/all_gather | solution.py:80
  307.8 5.0 %fusion.6 = bf16[2,256,2,896]{3,1,2,0:T(8,128)(2,1)S(1)} fusion(bf16[256,2,2,1024]{3,0,2,1:T(8,128)(2,1)} %all-gather.5.cloned.1.call-done, bf16[2,1024,896]{2,1,0:T(8,128)(2,1)} %param.15), kind=kOutput, calls=%fused_computation.8 | convolution fusion | flops 1879965696 | bytes 7602176 | tf_op jit(solution)/shard_map/mjcf,jfd->mjcd/dot_general | solution.py:78
  312.8 1.4 copy.45
  314.3 55.6 %all_to_all.30 = bf16[4,64,4,896]{3,2,0,1:T(4,128)(2,1)S(1)} all-to-all(bf16[4,64,4,896]{3,2,0,1:T(4,128)(2,1)S(1)} %copy.45), channel_id=1, replica_groups=mesh['rep'=4,'ep'=64] {'ep'}, dimensions={1} | all-to-all | bytes 3670016 | tf_op jit(solution)/shard_map/all_to_all | solution.py:85
  369.9 1.9 copy.46
  371.7 3.7 all-to-all-start.3
  375.7 21.1 %all-to-all-done.3 = bf16[4,64,4,896]{3,2,1,0:T(4,128)(2,1)S(1)} async-done(((bf16[4,64,4,896]{3,2,1,0:T(4,128)(2,1)}), bf16[4,64,4,896]{3,2,1,0:T(4,128)(2,1)S(1)}, u32[]{:S(2)}, u32[]{:S(2)}) %all-to-all-start.3) | async-done | bytes 1835040 | tf_op jit(solution)/shard_map/all_to_all | solution.py:86
  396.8 2.4 copy.47
  399.4 1.0 convolution_convert_fusion.1
  (30 shorter events, 2.6 us)
Async XLA Ops:
  6.5 12.0 %copy-start = (bf16[3584,128]{1,0:T(8,128)(2,1)S(1)}, bf16[3584,128]{1,0:T(8,128)(2,1)}, u32[]{:S(2)}) copy-start(bf16[3584,128]{1,0:T(8,128)(2,1)} %param.16) | copy-start | bytes 2752516
  29.8 56.8 %all-to-all-start.1 = ((bf16[4,64,4,128]{3,2,0,1:T(4,128)(2,1)}), bf16[4,64,4,128]{3,2,0,1:T(4,128)(2,1)S(1)}, u32[]{:S(2)}, u32[]{:S(2)}) async-start(bf16[4,64,4,128]{3,2,0,1:T(4,128)(2,1)} %copy.43), calls=%async_computation.1 | async-start | bytes 524288 | tf_op jit(solution)/shard_map/all_to_all | solution.py:61
  86.6 172.6 %all-to-all-start = ((bf16[4,64,4,3584]{3,2,0,1:T(4,128)(2,1)}), bf16[4,64,4,3584]{3,2,0,1:T(4,128)(2,1)}, u32[]{:S(2)}, u32[]{:S(2)}) async-start(bf16[4,64,4,3584]{3,2,0,1:T(4,128)(2,1)} %copy.41), calls=%async_computation | async-start | bytes 14680064 | tf_op jit(solution)/shard_map/all_to_all | solution.py:60
  98.8 209.0 %all-gather.5.cloned.1.call-start = ((), (), s32[]{:S(2)}) async-start(), calls=%async_computation.4 | async-start | bytes 2621440 | tf_op jit(solution)/shard_map/all_gather | solution.py:80
  259.1 7.3 %copy-start.3 = (bf16[2,3584,256]{2,1,0:T(8,128)(2,1)S(1)}, bf16[2,3584,256]{2,1,0:T(8,128)(2,1)}, u32[]{:S(2)}) copy-start(bf16[2,3584,256]{2,1,0:T(8,128)(2,1)} %param.14) | copy-start | bytes 11010052
  266.4 2.1 copy-start.4
  268.5 2.1 copy-start.5
  369.9 5.6 %copy-start.2 = (bf16[16,8]{0,1:T(8,128)(2,1)S(1)}, bf16[16,8]{0,1:T(8,128)(2,1)}, u32[]{:S(2)}) copy-start(bf16[16,8]{0,1:T(8,128)(2,1)} %param.11) | copy-start | bytes 772
  371.7 25.1 %all-to-all-start.3 = ((bf16[4,64,4,896]{3,2,1,0:T(4,128)(2,1)}), bf16[4,64,4,896]{3,2,1,0:T(4,128)(2,1)S(1)}, u32[]{:S(2)}, u32[]{:S(2)}) async-start(bf16[4,64,4,896]{3,2,1,0:T(4,128)(2,1)} %copy.46), calls=%async_computation.3 | async-start | bytes 3670016 | tf_op jit(solution)/shard_map/all_to_all | solution.py:86
  396.8 3.6 copy-start.1
Sparse Core Ops, SparseCore 0:
  271.9 35.8 all-gather.4
where the time goes:
time: 410 us; the launch traced here: 407 us
  waiting for transfers between devices  217 us (53%)
  blocking collectives  86.1 us (21%)
  local copies, waits for them, and re-layouts  37.8 us (9%)
  starting transfers between devices  34.1 us (8%)
  matrix products  17.8 us (4%)
  between operations  13.6 us (3%)
    all_to_all x1, waiting for transfers between devices, per_device(): lax.all_to_all(packed, 'ep', split_axis=1, concat_axis=1, tiled=True)  160 us
    all_to_all x1, blocking collectives, per_device(): lax.all_to_all(outputs, 'ep', split_axis=1, concat_axis=1, tiled=True)  55.6 us
    all_gather x1, waiting for transfers between devices, per_device(): lax.all_gather(hidden, 'rep', axis=3, tiled=True)  36 us
    reshape x2, local copies, waits for them, and re-layouts, per_device(): packed = packed.reshape(groups, owners, owner_slots, width)  22.7 us
    all_to_all x1, waiting for transfers between devices, per_device(): lax.all_to_all(returned, 'rep', split_axis=0, concat_axis=3, tiled=True)  21.1 us
    all_to_all x1, starting transfers between devices, per_device(): lax.all_to_all(packed_low, 'ep', split_axis=1, concat_axis=1, tiled=True)  17.9 us
    all_to_all x1, starting transfers between devices, per_device(): lax.all_to_all(packed, 'ep', split_axis=1, concat_axis=1, tiled=True)  12.2 us
    all_gather x1, blocking collectives, per_device(): lax.all_gather(tokens[None], 'rep', axis=0, tiled=True)  11.1 us
  transfers between devices with their start and end apart: 4, of which 3 were waited for; matrix products, arithmetic and copies ran while one was open for 7% of the time, Pallas kernels for 0%

commit v1 on v0

v1 whole, which is shorter than its diff:
```python
import jax
import jax.numpy as jnp
from jax import lax
from jax.sharding import PartitionSpec as P

ADAPTER_RANK = 16


def per_device(
    tokens,
    chosen_expert_index,
    expert_mixing_weight,
    row_adapter_index,
    gate_weight,
    up_weight,
    down_weight,
    adapter_down_factor,
    adapter_up_factor,
):
    row_count, width = tokens.shape
    owners = lax.axis_size("ep")
    groups = lax.axis_size("rep")
    local_count = gate_weight.shape[0]
    experts = local_count * owners
    capacity = 2
    share = down_weight.shape[2]
    f32 = jnp.float32
    bf16 = jnp.bfloat16

    flat_ids = chosen_expert_index.reshape(-1)
    one_hot = (flat_ids[:, None] == lax.iota(jnp.int32, experts)[None, :]).astype(jnp.int32)
    before = jnp.cumsum(one_hot, axis=0) - one_hot
    position = jnp.sum(before * one_hot, axis=1).reshape(chosen_expert_index.shape)
    local = chosen_expert_index % local_count
    owner = chosen_expert_index // local_count

    adapters = adapter_down_factor.shape[1]
    lane_adapter = lax.iota(jnp.int32, adapters) // ADAPTER_RANK
    adapter_mask = (row_adapter_index[:, None] == lane_adapter[None, :]).astype(f32)
    low = (
        jnp.dot(tokens, adapter_down_factor, preferred_element_type=f32) * adapter_mask
    ).astype(bf16)
    rows = jnp.concatenate([tokens, low], axis=1)

    slots = owners * capacity
    slot = owner * capacity + position
    mixing = expert_mixing_weight.astype(f32)
    received, combiners = [], []
    for j in range(local_count):
        matches = (slot[:, :, None] == lax.iota(jnp.int32, slots)[None, None, :]) & (
            local == j
        )[:, :, None]
        routing = jnp.any(matches, axis=1).astype(bf16)
        combiners.append(
            jnp.sum(jnp.where(matches, mixing[:, :, None], f32(0.0)), axis=1).astype(bf16)
        )
        packed = jnp.einsum("ri,rd->id", routing, rows, preferred_element_type=f32).astype(bf16)
        packed = packed.reshape(owners, capacity, width + adapters)
        received.append(lax.all_to_all(packed, "ep", split_axis=0, concat_axis=0, tiled=True))
    combiner = lax.all_gather(jnp.stack(combiners), "rep", axis=0)

    total = jnp.zeros((groups, row_count, share), f32)
    for j in range(local_count):
        mine = received[j].reshape(slots, width + adapters)
        every = lax.all_gather(mine, "rep", axis=0, tiled=True)
        row_part, low_part = every[:, :width], every[:, width:]
        gate = jnp.dot(row_part, gate_weight[j], preferred_element_type=f32)
        up = jnp.dot(row_part, up_weight[j], preferred_element_type=f32) + jnp.dot(
            low_part, adapter_up_factor, preferred_element_type=f32
        )
        hidden = (jax.nn.silu(gate) * up).astype(bf16)
        hidden = lax.all_gather(hidden, "rep", axis=1, tiled=True)
        out = jnp.dot(hidden, down_weight[j], preferred_element_type=f32).astype(bf16)
        out = out.reshape(groups, owners, capacity, share).transpose(1, 0, 2, 3)
        back = lax.all_to_all(out, "ep", split_axis=0, concat_axis=0, tiled=True)
        back = back.transpose(1, 0, 2, 3).reshape(groups, slots, share)
        total = total + jnp.einsum(
            "gri,gid->grd", combiner[:, j], back, preferred_element_type=f32
        )
    mixed = total.astype(bf16)
    mixed = lax.all_to_all(mixed, "rep", split_axis=0, concat_axis=0, tiled=True)
    return mixed.transpose(1, 0, 2).reshape(row_count, width)


def solution(mesh):
    placed = (
        P(("rep", "ep"), None),
        P(("rep", "ep"), None),
        P(("rep", "ep"), None),
        P(("rep", "ep")),
        P("ep", None, "rep"),
        P("ep", None, "rep"),
        P("ep", None, "rep"),
        P(),
        P(None, "rep"),
    )
    return jax.shard_map(
        per_device, mesh=mesh, in_specs=placed, out_specs=P(("rep", "ep"), None), check_vma=False
    )
```

time: 410 us -> 273 us (0.67)
  waiting for transfers between devices: 217 us -> 104 us
  local copies, waits for them, and re-layouts: 37.8 us -> 21.1 us
  starting transfers between devices: 34.1 us -> 20.3 us
  matrix products: 17.8 us -> 22.5 us
    all_to_all x3 -> x2, waiting for transfers between devices: 181 us -> 14 us  [per_device(): back = lax.all_to_all(out, 'ep', split_axis=0, concat_axis=0, tiled=True)]
    all_gather x1 -> x4, waiting for transfers between devices: 36 us -> 90.4 us  [the longest x2 53.1 us: per_device(): every = lax.all_gather(mine, 'rep', axis=0, tiled=True)]
    all_to_all x1 -> x3, blocking collectives: 55.6 us -> 79.2 us  [the longest x2 71 us: per_device(): lax.all_to_all(packed, 'ep', split_axis=0, concat_axis=0, tiled=True)]
    all_gather x3 -> x1, blocking collectives: 30.5 us -> 9.81 us  [per_device(): combiner = lax.all_gather(jnp.stack(combiners), 'rep', axis=0)]
    all_to_all x3 -> x2, starting transfers between devices: 33.9 us -> 20.2 us  [per_device(): back = lax.all_to_all(out, 'ep', split_axis=0, concat_axis=0, tiled=True)]
    all_to_all x4 -> x0, local copies, waits for them, and re-layouts: 11.6 us -> none  [the longest x1 7.25 us: per_device(): lax.all_to_all(packed, 'ep', split_axis=1, concat_axis=1, tiled=True)]
    reshape x4 -> x12, local copies, waits for them, and re-layouts: 24.9 us -> 15 us  [the longest x4 5.87 us: per_device(): out = out.reshape(groups, owners, capacity, share).transpose(1, 0, 2, 3)]
    dot_general x8 -> x13, matrix products: 17.8 us -> 22.5 us  [the longest x2 7.72 us: per_device(): jnp.dot(row_part, up_weight[j], preferred_element_type=f32)]
  transfers between devices with their start and end apart: 4 -> 6, of which waited for: 3 -> 6; matrix products, arithmetic and copies ran while one was open for 7% -> 12% of each run, Pallas kernels for 0% -> 0%
where the time goes in v1:
time: 273 us; the launch traced here: 272 us
  waiting for transfers between devices  104 us (38%)
  blocking collectives  89.1 us (33%)
  matrix products  22.5 us (8%)
  local copies, waits for them, and re-layouts  21.1 us (8%)
  starting transfers between devices  20.3 us (7%)
  between operations  13.4 us (5%)
    all_to_all x2, blocking collectives, per_device(): lax.all_to_all(packed, 'ep', split_axis=0, concat_axis=0, tiled=True)  71 us
    all_gather x2, waiting for transfers between devices, per_device(): every = lax.all_gather(mine, 'rep', axis=0, tiled=True)  53.1 us
    all_gather x2, waiting for transfers between devices, per_device(): hidden = lax.all_gather(hidden, 'rep', axis=1, tiled=True)  37.2 us
    all_to_all x2, starting transfers between devices, per_device(): back = lax.all_to_all(out, 'ep', split_axis=0, concat_axis=0, tiled=True)  20.2 us
    all_to_all x2, waiting for transfers between devices, per_device(): back = lax.all_to_all(out, 'ep', split_axis=0, concat_axis=0, tiled=True)  14 us
    all_gather x1, blocking collectives, per_device(): combiner = lax.all_gather(jnp.stack(combiners), 'rep', axis=0)  9.81 us
    all_to_all x1, blocking collectives, per_device(): lax.all_to_all(mixed, 'rep', split_axis=0, concat_axis=0, tiled=True)  8.24 us
    dot_general x2, matrix products, per_device(): jnp.dot(row_part, up_weight[j], preferred_element_type=f32)  7.72 us
  transfers between devices with their start and end apart: 6, of which 6 were waited for; matrix products, arithmetic and copies ran while one was open for 12% of the time, Pallas kernels for 0%

profile of v1, /device:TPU:1, one launch (start us, length us, event | category | flops | bytes accessed | tf_op | source)
XLA Modules:
  0.0 271.6 jit_solution(13068860921193433796)
XLA Ops:
  9.3 1.4 convolution_convert_fusion.1
  11.1 38.8 %all_to_all.25 = bf16[64,2,3712]{2,1,0:T(2,128)(2,1)S(1)} all-to-all(bf16[64,2,3712]{2,1,0:T(2,128)(2,1)S(1)} %reshape.66), channel_id=1, replica_groups=mesh['rep'=4,'ep'=64] {'ep'}, dimensions={0} | all-to-all | bytes 1900544 | tf_op jit(solution)/shard_map/all_to_all | solution.py:59
  52.2 32.2 %all_to_all.26 = bf16[64,2,3712]{2,1,0:T(2,128)(2,1)S(1)} all-to-all(bf16[64,2,3712]{2,1,0:T(2,128)(2,1)S(1)} %reshape.70), channel_id=1, replica_groups=mesh['rep'=4,'ep'=64] {'ep'}, dimensions={0} | all-to-all | bytes 1900544 | tf_op jit(solution)/shard_map/all_to_all | solution.py:59
  85.9 10.4 %all-gather.6.cloned.1.call-done = bf16[512,3712]{1,0:T(8,128)(2,1)} async-done(((bf16[128,3712]{1,0:T(8,128)(2,1)}), bf16[512,3712]{1,0:T(8,128)(2,1)}) %all-gather.6.cloned.1.call-update) | async-done | bytes 3801104 | tf_op jit(solution)/shard_map/all_gather | solution.py:65
  96.3 3.9 %fusion.4 = f32[512,256]{1,0:T(8,128)S(1)} fusion(bf16[512,3712]{1,0:T(8,128)(2,1)} %all-gather.6.cloned.1.call-done, bf16[2,3584,256]{2,1,0:T(8,128)(2,1)} %param.14), kind=kOutput, calls=%fused_computation.6 | convolution fusion | flops 939524096 | bytes 6029312 | tf_op jit(solution)/shard_map/dot_general | solution.py:68
  103.4 42.7 %all-gather.10.cloned.1.call-done = bf16[512,3712]{1,0:T(8,128)(2,1)} async-done(((bf16[128,3712]{1,0:T(8,128)(2,1)}), bf16[512,3712]{1,0:T(8,128)(2,1)}) %all-gather.10.cloned.1.call-update) | async-done | bytes 3801104 | tf_op jit(solution)/shard_map/all_gather | solution.py:65
  146.0 3.9 %fusion = f32[512,256]{1,0:T(8,128)S(1)} fusion(bf16[512,3712]{1,0:T(8,128)(2,1)} %all-gather.10.cloned.1.call-done, bf16[2,3584,256]{2,1,0:T(8,128)(2,1)} %param.14), kind=kOutput, calls=%fused_computation.2 | convolution fusion | flops 939524096 | bytes 6029312 | tf_op jit(solution)/shard_map/dot_general | solution.py:68
  153.0 22.7 %all-gather.8.cloned.1.call-done = bf16[512,1024]{1,0:T(8,128)(2,1)} async-done(((bf16[512,256]{1,0:T(8,128)(2,1)}), bf16[512,1024]{1,0:T(8,128)(2,1)}) %all-gather.8.cloned.1.call-update) | async-done | bytes 1048592 | tf_op jit(solution)/shard_map/all_gather | solution.py:72
  175.7 3.1 %fusion.22 = bf16[512,896]{1,0:T(8,128)(2,1)S(1)} fusion(bf16[512,1024]{1,0:T(8,128)(2,1)} %all-gather.8.cloned.1.call-done, bf16[2,1024,896]{2,1,0:T(8,128)(2,1)} %param.15), kind=kOutput, calls=%fused_computation.24 | convolution fusion | flops 939982848 | bytes 3801088 | tf_op jit(solution)/shard_map/dot_general | solution.py:73
  179.2 1.6 copy.57
  180.8 11.5 %all-to-all-start.1 = ((bf16[64,4,2,896]{3,2,1,0:T(2,128)(2,1)}), bf16[64,4,2,896]{3,2,1,0:T(2,128)(2,1)S(1)}, u32[]{:S(2)}, u32[]{:S(2)}) async-start(bf16[64,4,2,896]{3,2,1,0:T(2,128)(2,1)} %bitcast.59), calls=%async_computation.1 | async-start | bytes 1835008 | tf_op jit(solution)/shard_map/all_to_all | solution.py:75
  192.3 14.5 %all-gather.12.cloned.1.call-done = bf16[512,1024]{1,0:T(8,128)(2,1)} async-done(((bf16[512,256]{1,0:T(8,128)(2,1)}), bf16[512,1024]{1,0:T(8,128)(2,1)}) %all-gather.12.cloned.1.call-update) | async-done | bytes 1048592 | tf_op jit(solution)/shard_map/all_gather | solution.py:72
  206.9 4.0 %fusion.25 = bf16[512,896]{1,0:T(8,128)(2,1)} fusion(bf16[512,1024]{1,0:T(8,128)(2,1)} %all-gather.12.cloned.1.call-done, bf16[2,1024,896]{2,1,0:T(8,128)(2,1)} %param.15), kind=kOutput, calls=%fused_computation.25 | convolution fusion | flops 939982848 | bytes 3801088 | tf_op jit(solution)/shard_map/dot_general | solution.py:73
  210.9 2.3 reshape.72
  213.2 1.6 copy.56
  214.8 2.8 %all-to-all-done.1 = bf16[64,4,2,896]{3,2,1,0:T(2,128)(2,1)S(1)} async-done(((bf16[64,4,2,896]{3,2,1,0:T(2,128)(2,1)}), bf16[64,4,2,896]{3,2,1,0:T(2,128)(2,1)S(1)}, u32[]{:S(2)}, u32[]{:S(2)}) %all-to-all-start.1) | async-done | bytes 917536 | tf_op jit(solution)/shard_map/all_to_all | solution.py:75
  217.6 8.7 %all-to-all-start.3 = ((bf16[64,4,2,896]{3,2,1,0:T(2,128)(2,1)}), bf16[64,4,2,896]{3,2,1,0:T(2,128)(2,1)S(1)}, u32[]{:S(2)}, u32[]{:S(2)}) async-start(bf16[64,4,2,896]{3,2,1,0:T(2,128)(2,1)} %bitcast.58), calls=%async_computation.3 | async-start | bytes 1835008 | tf_op jit(solution)/shard_map/all_to_all | solution.py:75
  226.6 9.8 %all-gather = bf16[8,16,128]{2,1,0:T(8,128)(2,1)S(1)} all-gather(bf16[2,16,128]{2,1,0:T(8,128)(2,1)S(1)} %pad_maximum_fusion.3), channel_id=2, replica_groups=mesh['rep'=4,'ep'=64] {'rep'}, dimensions={0}, use_global_device_ids=true | all-gather | bytes 40960 | tf_op jit(solution)/shard_map/all_gather | solution.py:60
  236.4 1.6 copy.46
  238.0 2.5 reshape.69
  240.4 11.2 %all-to-all-done.3 = bf16[64,4,2,896]{3,2,1,0:T(2,128)(2,1)S(1)} async-done(((bf16[64,4,2,896]{3,2,1,0:T(2,128)(2,1)}), bf16[64,4,2,896]{3,2,1,0:T(2,128)(2,1)S(1)}, u32[]{:S(2)}, u32[]{:S(2)}) %all-to-all-start.3) | async-done | bytes 917536 | tf_op jit(solution)/shard_map/all_to_all | solution.py:75
  251.6 1.6 copy.49
  253.2 2.5 reshape.73
  256.1 8.2 %all_to_all.27 = bf16[4,16,896]{2,1,0:T(8,128)(2,1)S(1)} all-to-all(bf16[4,16,896]{2,1,0:T(8,128)(2,1)S(1)} %fusion.32), channel_id=1, replica_groups=mesh['rep'=4,'ep'=64] {'rep'}, dimensions={0} | all-to-all | bytes 229376 | tf_op jit(solution)/shard_map/all_to_all | solution.py:81
  (51 shorter events, 14.8 us)
Async XLA Ops:
  6.5 1.7 copy-start
  6.5 89.8 %all-gather.6.cloned.1.call-start = ((), (), s32[]{:S(2)}) async-start(), calls=%async_computation.5 | async-start | bytes 4751360 | tf_op jit(solution)/shard_map/all_gather | solution.py:65
  9.3 42.0 %copy-start.1 = (bf16[16,3584]{1,0:T(8,128)(2,1)S(1)}, bf16[16,3584]{1,0:T(8,128)(2,1)}, u32[]{:S(2)}) copy-start(bf16[16,3584]{1,0:T(8,128)(2,1)} %param.9) | copy-start | bytes 344068
  51.3 94.7 %all-gather.10.cloned.1.call-start = ((), (), s32[]{:S(2)}) async-start(), calls=%async_computation.7 | async-start | bytes 4751360 | tf_op jit(solution)/shard_map/all_gather | solution.py:65
  85.8 89.9 %all-gather.8.cloned.1.call-start = ((), (), s32[]{:S(2)}) async-start(), calls=%async_computation.6 | async-start | bytes 1310720 | tf_op jit(solution)/shard_map/all_gather | solution.py:72
  96.3 3.9 %copy-start.3 = (bf16[512,3712]{1,0:T(8,128)(2,1)S(1)}, bf16[512,3712]{1,0:T(8,128)(2,1)}, u32[]{:S(2)}) copy-start(bf16[512,3712]{1,0:T(8,128)(2,1)} %all-gather.6.cloned.1.call-done) | copy-start | bytes 11403268
  96.3 4.8 %copy-start.5 = (bf16[2,3584,256]{2,1,0:T(8,128)(2,1)S(1)}, bf16[2,3584,256]{2,1,0:T(8,128)(2,1)}, u32[]{:S(2)}) copy-start(bf16[2,3584,256]{2,1,0:T(8,128)(2,1)} %param.13) | copy-start | bytes 11010052
  101.2 1.1 copy-start.7
  103.3 103.5 %all-gather.12.cloned.1.call-start = ((), (), s32[]{:S(2)}) async-start(), calls=%async_computation.8 | async-start | bytes 1310720 | tf_op jit(solution)/shard_map/all_gather | solution.py:72
  146.0 3.9 %copy-start.4 = (bf16[512,3712]{1,0:T(8,128)(2,1)S(1)}, bf16[512,3712]{1,0:T(8,128)(2,1)}, u32[]{:S(2)}) copy-start(bf16[512,3712]{1,0:T(8,128)(2,1)} %all-gather.10.cloned.1.call-done) | copy-start | bytes 11403268
  146.0 4.8 %copy-start.6 = (bf16[2,3584,256]{2,1,0:T(8,128)(2,1)S(1)}, bf16[2,3584,256]{2,1,0:T(8,128)(2,1)}, u32[]{:S(2)}) copy-start(bf16[2,3584,256]{2,1,0:T(8,128)(2,1)} %param.13) | copy-start | bytes 11010052
  180.8 36.8 %all-to-all-start.1 = ((bf16[64,4,2,896]{3,2,1,0:T(2,128)(2,1)}), bf16[64,4,2,896]{3,2,1,0:T(2,128)(2,1)S(1)}, u32[]{:S(2)}, u32[]{:S(2)}) async-start(bf16[64,4,2,896]{3,2,1,0:T(2,128)(2,1)} %bitcast.59), calls=%async_computation.1 | async-start | bytes 1835008 | tf_op jit(solution)/shard_map/all_to_all | solution.py:75
  210.9 15.5 %copy-start.2 = (bf16[16,8]{0,1:T(8,128)(2,1)S(1)}, bf16[16,8]{0,1:T(8,128)(2,1)}, u32[]{:S(2)}) copy-start(bf16[16,8]{0,1:T(8,128)(2,1)} %param.11) | copy-start | bytes 772
  217.6 34.0 %all-to-all-start.3 = ((bf16[64,4,2,896]{3,2,1,0:T(2,128)(2,1)}), bf16[64,4,2,896]{3,2,1,0:T(2,128)(2,1)S(1)}, u32[]{:S(2)}, u32[]{:S(2)}) async-start(bf16[64,4,2,896]{3,2,1,0:T(2,128)(2,1)} %bitcast.58), calls=%async_computation.3 | async-start | bytes 1835008 | tf_op jit(solution)/shard_map/all_to_all | solution.py:75
Sparse Core Ops, SparseCore 0:
  51.4 44.8 all-gather.5
  98.1 47.8 all-gather.9
  147.8 27.8 all-gather.7
  177.4 29.4 all-gather.11

commit v2 on v1

--- a/solution.py
+++ b/solution.py
@@ -1,9 +1,116 @@
+import functools
+
 import jax
 import jax.numpy as jnp
 from jax import lax
+from jax.experimental import pallas as pl
+from jax.experimental.pallas import tpu as pltpu
 from jax.sharding import PartitionSpec as P
 
 ADAPTER_RANK = 16
+VMEM_LIMIT = 40 * 1024 * 1024
+
+
+def gate_up_kernel(parts, *refs):
+    rows = refs[:parts]
+    lows = refs[parts : 2 * parts]
+    gate_ref, up_ref, factor_ref, _, hidden_ref, gate_sum, up_sum = refs[2 * parts :]
+    step = pl.program_id(0)
+    x = jnp.concatenate([r[...] for r in rows], axis=0) if parts > 1 else rows[0][...]
+    gate = jnp.dot(x, gate_ref[0], preferred_element_type=jnp.float32)
+    up = jnp.dot(x, up_ref[0], preferred_element_type=jnp.float32)
+
+    @pl.when(step == 0)
+    def _():
+        low = jnp.concatenate([r[...] for r in lows], axis=0) if parts > 1 else lows[0][...]
+        gate_sum[...] = gate
+        up_sum[...] = up + jnp.dot(low, factor_ref[...], preferred_element_type=jnp.float32)
+
+    @pl.when(step > 0)
+    def _():
+        gate_sum[...] += gate
+        up_sum[...] += up
+
+    @pl.when(step == pl.num_programs(0) - 1)
+    def _():
+        g = gate_sum[...]
+        hidden_ref[...] = (g / (1.0 + jnp.exp(-g)) * up_sum[...]).astype(hidden_ref.dtype)
+
+
+def gate_up(rows, gate_weight, up_weight, factor, expert, after):
+    width, units = gate_weight.shape[1:]
+    adapters = factor.shape[0]
+    steps = 4
+    depth = width // steps
+    count = sum(r.shape[0] for r in rows)
+    weight = pl.BlockSpec((1, depth, units), lambda k: (expert, k, 0))
+    return pl.pallas_call(
+        functools.partial(gate_up_kernel, len(rows)),
+        grid=(steps,),
+        in_specs=[pl.BlockSpec((r.shape[0], depth), lambda k: (0, k)) for r in rows]
+        + [pl.BlockSpec((r.shape[0], adapters), lambda k: (0, width // adapters)) for r in rows]
+        + [weight, weight, pl.BlockSpec((adapters, units), lambda k: (0, 0))]
+        + [pl.BlockSpec(memory_space=pl.ANY)],
+        out_specs=pl.BlockSpec((count, units), lambda k: (0, 0)),
+        out_shape=jax.ShapeDtypeStruct((count, units), jnp.bfloat16),
+        scratch_shapes=[pltpu.VMEM((count, units), jnp.float32)] * 2,
+        compiler_params=pltpu.CompilerParams(vmem_limit_bytes=VMEM_LIMIT),
+        cost_estimate=pl.CostEstimate(
+            flops=4 * count * width * units,
+            bytes_accessed=2 * (count * width + 2 * width * units + count * units),
+            transcendentals=count * units,
+        ),
+        name="gate_up",
+    )(*rows, *rows, gate_weight, up_weight, factor, after)
+
+
+def down_kernel(groups, _, *refs):
+    hidden, weights, out_ref = refs[:groups], refs[groups : 2 * groups], refs[2 * groups]
+    out_ref[...] = sum(
+        jnp.dot(h[...], w[0], preferred_element_type=jnp.float32)
+        for h, w in zip(hidden, weights)
+    ).astype(out_ref.dtype)
+
+
+def down(hidden, down_weight, me, expert, turned):
+    groups = len(hidden)
+    count, units = hidden[0].shape
+    share = down_weight.shape[2]
+    block = count // groups
+    if turned:
+        from_at = [lambda i, m, s=s: ((i + groups - s) % groups, 0) for s in range(groups)]
+        to_at = lambda i, m: ((m[0] + i) % groups, 0)
+    else:
+        from_at = [lambda i, m: (i, 0)] * groups
+        to_at = lambda i, m: (i, 0)
+    return pl.pallas_call(
+        functools.partial(down_kernel, groups),
+        grid_spec=pltpu.PrefetchScalarGridSpec(
+            num_scalar_prefetch=1,
+            grid=(groups,),
+            in_specs=[pl.BlockSpec((block, units), at) for at in from_at]
+            + [
+                pl.BlockSpec(
+                    (1, units, share), lambda i, m, s=s: (expert, (m[0] + s) % groups, 0)
+                )
+                for s in range(groups)
+            ],
+            out_specs=pl.BlockSpec((block, share), to_at),
+        ),
+        out_shape=jax.ShapeDtypeStruct((count, share), jnp.bfloat16),
+        compiler_params=pltpu.CompilerParams(vmem_limit_bytes=VMEM_LIMIT),
+        cost_estimate=pl.CostEstimate(
+            flops=2 * count * units * groups * share,
+            bytes_accessed=2 * (groups * count * units + groups * units * share + count * share),
+            transcendentals=0,
+        ),
+        name="down",
+    )(me, *hidden, *([down_weight] * groups))
+
+
+def from_further(x, by):
+    n = lax.axis_size("rep")
+    return lax.ppermute(x, "rep", [(i, (i - by) % n) for i in range(n)])
 
 
 def per_device(
@@ -56,30 +163,33 @@
         )
         packed = jnp.einsum("ri,rd->id", routing, rows, preferred_element_type=f32).astype(bf16)
         packed = packed.reshape(owners, capacity, width + adapters)
-        received.append(lax.all_to_all(packed, "ep", split_axis=0, concat_axis=0, tiled=True))
-    combiner = lax.all_gather(jnp.stack(combiners), "rep", axis=0)
-
-    total = jnp.zeros((groups, row_count, share), f32)
+        sent = lax.all_to_all(packed, "ep", split_axis=0, concat_axis=0, tiled=True)
+        received.append(sent.reshape(slots, width + adapters))
+
+    me = lax.axis_index("rep").astype(jnp.int32).reshape(1)
+    total = jnp.zeros((row_count, groups, share), f32)
+    after = adapter_up_factor
     for j in range(local_count):
-        mine = received[j].reshape(slots, width + adapters)
-        every = lax.all_gather(mine, "rep", axis=0, tiled=True)
-        row_part, low_part = every[:, :width], every[:, width:]
-        gate = jnp.dot(row_part, gate_weight[j], preferred_element_type=f32)
-        up = jnp.dot(row_part, up_weight[j], preferred_element_type=f32) + jnp.dot(
-            low_part, adapter_up_factor, preferred_element_type=f32
+        mine = received[j]
+        last = j == local_count - 1
+        if last:
+            half = slots // 2
+            before_me, after_me = from_further(mine, -1), from_further(mine, 1)
+            across = [from_further(before_me[:half], -1), from_further(after_me[half:], 1)]
+            every = [mine, after_me, *across, before_me]
+        else:
+            every = [lax.all_gather(mine, "rep", axis=0, tiled=True)]
+        hidden = gate_up(every, gate_weight, up_weight, adapter_up_factor, j, after)
+        hidden = [hidden] + [from_further(hidden, s) for s in range(1, groups)]
+        out = down(hidden, down_weight, me, j, last)
+        after = out[:16, :128]
+        out = out.reshape(groups * owners, capacity, share)
+        back = lax.all_to_all(out, ("rep", "ep"), split_axis=0, concat_axis=0, tiled=True)
+        back = back.reshape(groups, slots, share)
+        total = total + jnp.einsum(
+            "ri,gid->rgd", combiners[j], back, preferred_element_type=f32
         )
-        hidden = (jax.nn.silu(gate) * up).astype(bf16)
-        hidden = lax.all_gather(hidden, "rep", axis=1, tiled=True)
-        out = jnp.dot(hidden, down_weight[j], preferred_element_type=f32).astype(bf16)
-        out = out.reshape(groups, owners, capacity, share).transpose(1, 0, 2, 3)
-        back = lax.all_to_all(out, "ep", split_axis=0, concat_axis=0, tiled=True)
-        back = back.transpose(1, 0, 2, 3).reshape(groups, slots, share)
-        total = total + jnp.einsum(
-            "gri,gid->grd", combiner[:, j], back, preferred_element_type=f32
-        )
-    mixed = total.astype(bf16)
-    mixed = lax.all_to_all(mixed, "rep", split_axis=0, concat_axis=0, tiled=True)
-    return mixed.transpose(1, 0, 2).reshape(row_count, width)
+    return total.astype(bf16).reshape(row_count, width)
 
 
 def solution(mesh):

time: 273 us -> 248 us (0.908)
  blocking collectives: 89.1 us -> 38.8 us
  starting transfers between devices: 20.3 us -> 50.6 us
  matrix products: 22.5 us -> 4.66 us
  Pallas kernels: 0 us -> 14.2 us
  waiting for transfers between devices: 104 us -> 96.9 us
  local copies, waits for them, and re-layouts: 21.1 us -> 28.1 us
    all_gather x4 -> x1, waiting for transfers between devices: 90.4 us -> 36.8 us  [per_device(): every = [lax.all_gather(mine, 'rep', axis=0, tiled=True)]]
    all_to_all x3 -> x1, blocking collectives: 79.2 us -> 38.8 us  [per_device(): sent = lax.all_to_all(packed, 'ep', split_axis=0, concat_axis=0, tiled=True)]
    ppermute x0 -> x10, waiting for transfers between devices: none -> 34.6 us  [from_further(): return lax.ppermute(x, 'rep', [(i, (i - by) % n) for i in range(n)])]
    dot_general x10 -> x2, matrix products: 19.5 us -> 1.64 us  [per_device(): jnp.einsum('ri,gid->rgd', combiners[j], back, preferred_element_type=f32)]
    all_to_all x2 -> x3, starting transfers between devices: 20.2 us -> 36.5 us  [the longest x2 30 us: per_device(): lax.all_to_all(out, ('rep', 'ep'), split_axis=0, concat_axis=0, tiled=True)]
    pallas_call x0 -> x4, Pallas kernels: none -> 14.2 us  [the longest x2 9.14 us: gate_up(): pl.pallas_call(functools.partial(gate_up_kernel, len(rows)), grid=(steps,...]
    ppermute x0 -> x10, starting transfers between devices: none -> 14.1 us  [from_further(): return lax.ppermute(x, 'rep', [(i, (i - by) % n) for i in range(n)])]
    all_to_all x2 -> x3, waiting for transfers between devices: 14 us -> 25.6 us  [the longest x2 25.6 us: per_device(): lax.all_to_all(out, ('rep', 'ep'), split_axis=0, concat_axis=0, tiled=True)]
  transfers between devices with their start and end apart: 6 -> 14, of which waited for: 6 -> 10; matrix products, arithmetic and copies ran while one was open for 12% -> 4% of each run, Pallas kernels for 0% -> 6%
where the time goes in v2:
time: 248 us
  waiting for transfers between devices  96.9 us (39%)
  starting transfers between devices  50.6 us (20%)
  blocking collectives  38.8 us (16%)
  local copies, waits for them, and re-layouts  28.1 us (11%)
  Pallas kernels  14.2 us (6%)
  between operations  13.6 us (5%)
  matrix products  4.66 us (2%)
    all_to_all x1, blocking collectives, per_device(): sent = lax.all_to_all(packed, 'ep', split_axis=0, concat_axis=0, tiled=True)  38.8 us
    all_gather x1, waiting for transfers between devices, per_device(): every = [lax.all_gather(mine, 'rep', axis=0, tiled=True)]  36.8 us
    ppermute x10, waiting for transfers between devices, from_further(): return lax.ppermute(x, 'rep', [(i, (i - by) % n) for i in range(n)])  34.6 us
    all_to_all x2, starting transfers between devices, per_device(): lax.all_to_all(out, ('rep', 'ep'), split_axis=0, concat_axis=0, tiled=True)  30 us
    all_to_all x2, waiting for transfers between devices, per_device(): lax.all_to_all(out, ('rep', 'ep'), split_axis=0, concat_axis=0, tiled=True)  25.6 us
    ppermute x10, starting transfers between devices, from_further(): return lax.ppermute(x, 'rep', [(i, (i - by) % n) for i in range(n)])  14.1 us
    unnamed x25, local copies, waits for them, and re-layouts  14 us
    pallas_call x2, Pallas kernels, gate_up(): pl.pallas_call(functools.partial(gate_up_kernel, len(rows)), grid=(steps,...  9.14 us
  transfers between devices with their start and end apart: 14, of which 10 were waited for; matrix products, arithmetic and copies ran while one was open for 4% of the time, Pallas kernels for 6%

profile of v2, /device:TPU:1, one launch (start us, length us, event | category | flops | bytes accessed | tf_op | source)
XLA Modules:
  0.0 247.6 jit_solution(15788508898461253523)
XLA Ops:
  11.1 38.8 %all_to_all.20 = bf16[64,2,3712]{2,1,0:T(2,128)(2,1)S(1)} all-to-all(bf16[64,2,3712]{2,1,0:T(2,128)(2,1)S(1)} %reshape.54), channel_id=1, replica_groups=mesh['rep'=4,'ep'=64] {'ep'}, dimensions={0} | all-to-all | bytes 1900544 | tf_op jit(solution)/shard_map/all_to_all | solution.py:166
  53.0 6.5 %all-to-all-start.2 = ((bf16[64,2,3712]{2,1,0:T(2,128)(2,1)}), bf16[64,2,3712]{2,1,0:T(2,128)(2,1)S(1)}, u32[]{:S(2)}, u32[]{:S(2)}) async-start(bf16[64,2,3712]{2,1,0:T(2,128)(2,1)} %reshape.58), calls=%async_computation.2 | async-start | bytes 1900544 | tf_op jit(solution)/shard_map/all_to_all | solution.py:166
  59.5 36.8 %all-gather.2.cloned.1.call-done.refs_0_.refs_1_ = bf16[512,3712]{1,0:T(8,128)(2,1)} async-done(((bf16[128,3712]{1,0:T(8,128)(2,1)}), bf16[512,3712]{1,0:T(8,128)(2,1)}) %all-gather.2.cloned.1.call-update) | async-done | bytes 3801104 | tf_op jit(solution)/shard_map/all_gather | solution.py:181
  96.3 2.1 copy-done.3
  98.3 2.0 copy-done.4
  102.4 4.1 %gate_up.2.refs_0_ = bf16[512,256]{1,0:T(8,128)(2,1)S(1)} custom-call(bf16[512,3712]{1,0:T(8,128)(2,1)S(1)} %copy-done.3, bf16[512,3712]{1,0:T(8,128)(2,1)S(1)} %copy-done.3, bf16[2,3584,256]{2,1,0:T(8,128)(2,1)S(1)} %copy-done.4, bf16[2,3584,256]{2,1,0:T(8,128)(2,1)S(1)} %copy-done.6, bf16[128,256]{1,0:T(8,128)(2,1)S(1)} %copy-done.9, ...), custom_call_target="tpu_custom_call" | custom-call | flops 1879048192 | bytes 7602176 | tf_op jit(solution)/shard_map/gate_up/pallas_call | solution.py:47
  110.8 2.7 %collective-permute-start.3 = (bf16[128,3712]{1,0:T(8,128)(2,1)S(1)}, bf16[128,3712]{1,0:T(8,128)(2,1)}, u32[]{:S(2)}, u32[]{:S(2)}) collective-permute-start(bf16[128,3712]{1,0:T(8,128)(2,1)S(1)} %reshape.59.refs_0_.refs_5_), channel_id=1, source_target_pairs={{0,192},{64,0},{128,64},{192,128},{1,193},{65,1},{129,65},{193,129... | collective-permute-start | bytes 2850824 | tf_op jit(solution)/shard_map/ppermute | solution.py:113
  113.5 2.4 collective-permute-done.2.refs_3_
  115.9 3.9 %collective-permute-done.1.refs_2_ = bf16[512,256]{1,0:T(8,128)(2,1)} collective-permute-done((bf16[512,256]{1,0:T(8,128)(2,1)S(1)}, bf16[512,256]{1,0:T(8,128)(2,1)}, u32[]{:S(2)}, u32[]{:S(2)}) %collective-permute-start.1) | collective-permute-done | bytes 262176 | tf_op jit(solution)/shard_map/ppermute | solution.py:113
  121.2 2.0 copy-done.1
  123.2 3.2 %down.2 = bf16[512,896]{1,0:T(8,128)(2,1)S(1)} custom-call(s32[1]{0:T(128)} %bitcast.1._, bf16[512,256]{1,0:T(8,128)(2,1)S(1)} %gate_up.2.refs_0_, bf16[512,256]{1,0:T(8,128)(2,1)} %collective-permute-done.refs_1_, bf16[512,256]{1,0:T(8,128)(2,1)} %collective-permute-done.1.refs_2_, bf16[512,256]{1,0:T(8,128)(2,1)S(1)} %collective-permute-done.2.refs_3_, ...), custom_call_target="tpu_custom_call" | custom-call | flops 939524096 | bytes 3801088 | tf_op jit(solution)/shard_map/down/pallas_call | solution.py:86
  127.3 3.1 %reshape.56 = bf16[256,2,896]{2,1,0:T(2,128)(2,1)} reshape(bf16[512,896]{1,0:T(8,128)(2,1)} %copy-done.8) | data formatting | bytes 1835008 | tf_op jit(solution)/shard_map/reshape | solution.py:186
  130.4 15.5 %all-to-all-start.1 = ((bf16[256,2,896]{2,1,0:T(2,128)(2,1)}), bf16[256,2,896]{2,1,0:T(2,128)(2,1)}, u32[]{:S(2)}, u32[]{:S(2)}) async-start(bf16[256,2,896]{2,1,0:T(2,128)(2,1)} %reshape.56), calls=%async_computation.1 | async-start | bytes 1835008 | tf_op jit(solution)/shard_map/all_to_all | solution.py:187
  150.5 14.8 %collective-permute-done.5.refs_2_.refs_7_ = bf16[64,3712]{1,0:T(8,128)(2,1)S(1)} collective-permute-done((bf16[64,3712]{1,0:T(8,128)(2,1)S(1)}, bf16[64,3712]{1,0:T(8,128)(2,1)S(1)}, u32[]{:S(2)}, u32[]{:S(2)}) %collective-permute-start.5) | collective-permute-done | bytes 475168 | tf_op jit(solution)/shard_map/ppermute | solution.py:113
  165.3 2.5 collective-permute-done.6.refs_3_.refs_8_
  167.7 2.0 copy-done.5
  169.8 2.0 copy-done.7
  171.8 5.1 %gate_up.3.refs_0_ = bf16[512,256]{1,0:T(8,128)(2,1)S(1)} custom-call(bf16[128,3712]{1,0:T(8,128)(2,1)S(1)} %reshape.59.refs_0_.refs_5_, bf16[128,3712]{1,0:T(8,128)(2,1)} %collective-permute-done.3.refs_1_.refs_6_, bf16[64,3712]{1,0:T(8,128)(2,1)S(1)} %collective-permute-done.5.refs_2_.refs_7_, bf16[64,3712]{1,0:T(8,128)(2,1)S(1)} %collective-permute-done.6.refs_3_.refs_8_, ...), custom_call_target="tpu_custom_call" | custom-call | flops 1879048192 | bytes 7602176 | tf_op jit(solution)/shard_map/gate_up/pallas_call | solution.py:47
  181.6 3.9 %collective-permute-done.9.refs_3_ = bf16[512,256]{1,0:T(8,128)(2,1)S(1)} collective-permute-done((bf16[512,256]{1,0:T(8,128)(2,1)S(1)}, bf16[512,256]{1,0:T(8,128)(2,1)S(1)}, u32[]{:S(2)}, u32[]{:S(2)}) %collective-permute-start.9) | collective-permute-done | bytes 262176 | tf_op jit(solution)/shard_map/ppermute | solution.py:113
  185.5 3.2 %collective-permute-done.8.refs_2_ = bf16[512,256]{1,0:T(8,128)(2,1)S(1)} collective-permute-done((bf16[512,256]{1,0:T(8,128)(2,1)S(1)}, bf16[512,256]{1,0:T(8,128)(2,1)S(1)}, u32[]{:S(2)}, u32[]{:S(2)}) %collective-permute-start.8) | collective-permute-done | bytes 262176 | tf_op jit(solution)/shard_map/ppermute | solution.py:113
  188.7 2.5 %collective-permute-done.7.refs_1_ = bf16[512,256]{1,0:T(8,128)(2,1)S(1)} collective-permute-done((bf16[512,256]{1,0:T(8,128)(2,1)S(1)}, bf16[512,256]{1,0:T(8,128)(2,1)S(1)}, u32[]{:S(2)}, u32[]{:S(2)}) %collective-permute-start.7) | collective-permute-done | bytes 262176 | tf_op jit(solution)/shard_map/ppermute | solution.py:113
  194.3 14.6 %all-to-all-start.3 = ((bf16[256,2,896]{2,1,0:T(2,128)(2,1)}), bf16[256,2,896]{2,1,0:T(2,128)(2,1)S(1)}, u32[]{:S(2)}, u32[]{:S(2)}) async-start(bf16[256,2,896]{2,1,0:T(2,128)(2,1)} %reshape.60), calls=%async_computation.3 | async-start | bytes 1835008 | tf_op jit(solution)/shard_map/all_to_all | solution.py:187
  209.1 2.5 reshape.57
  211.6 25.6 %all-to-all-done.3 = bf16[256,2,896]{2,1,0:T(2,128)(2,1)S(1)} async-done(((bf16[256,2,896]{2,1,0:T(2,128)(2,1)}), bf16[256,2,896]{2,1,0:T(2,128)(2,1)S(1)}, u32[]{:S(2)}, u32[]{:S(2)}) %all-to-all-start.3) | async-done | bytes 917536 | tf_op jit(solution)/shard_map/all_to_all | solution.py:187
  (63 shorter events, 32.5 us)
Async XLA Ops:
  6.5 89.7 %all-gather.2.cloned.1.call-start = ((), (), s32[]{:S(2)}) async-start(), calls=%async_computation.4 | async-start | bytes 4751360 | tf_op jit(solution)/shard_map/all_gather | solution.py:181
  9.3 41.9 %copy-start.10 = (bf16[16,3584]{1,0:T(8,128)(2,1)S(1)}, bf16[16,3584]{1,0:T(8,128)(2,1)}, u32[]{:S(2)}) copy-start(bf16[16,3584]{1,0:T(8,128)(2,1)} %param.9) | copy-start | bytes 344068
  49.9 46.4 %copy-start.9 = (bf16[128,256]{1,0:T(8,128)(2,1)S(1)}, bf16[128,256]{1,0:T(8,128)(2,1)}, u32[]{:S(2)}) copy-start(bf16[128,256]{1,0:T(8,128)(2,1)} %refs_12_.1) | copy-start | bytes 196612
  53.0 57.3 %all-to-all-start.2 = ((bf16[64,2,3712]{2,1,0:T(2,128)(2,1)}), bf16[64,2,3712]{2,1,0:T(2,128)(2,1)S(1)}, u32[]{:S(2)}, u32[]{:S(2)}) async-start(bf16[64,2,3712]{2,1,0:T(2,128)(2,1)} %reshape.58), calls=%async_computation.2 | async-start | bytes 1900544 | tf_op jit(solution)/shard_map/all_to_all | solution.py:166
  96.3 2.1 copy-start.3
  98.3 2.0 copy-start.4
  100.4 2.0 copy-start.6
  106.5 9.4 %collective-permute-start.2 = (bf16[512,256]{1,0:T(8,128)(2,1)S(1)}, bf16[512,256]{1,0:T(8,128)(2,1)S(1)}, u32[]{:S(2)}, u32[]{:S(2)}) collective-permute-start(bf16[512,256]{1,0:T(8,128)(2,1)S(1)} %gate_up.2.refs_0_), channel_id=1, source_target_pairs={{0,64},{64,128},{128,192},{192,0},{1,65},{65,129},{129,193},{193,1... | collective-permute-start | bytes 786440 | tf_op jit(solution)/shard_map/ppermute | solution.py:113
  107.0 12.7 %collective-permute-start.1 = (bf16[512,256]{1,0:T(8,128)(2,1)S(1)}, bf16[512,256]{1,0:T(8,128)(2,1)}, u32[]{:S(2)}, u32[]{:S(2)}) collective-permute-start(bf16[512,256]{1,0:T(8,128)(2,1)S(1)} %gate_up.2.refs_0_), channel_id=1, source_target_pairs={{0,128},{64,192},{128,0},{192,64},{1,129},{65,193},{129,1},{193,65... | collective-permute-start | bytes 786440 | tf_op jit(solution)/shard_map/ppermute | solution.py:113
  108.4 12.8 %collective-permute-start = (bf16[512,256]{1,0:T(8,128)(2,1)S(1)}, bf16[512,256]{1,0:T(8,128)(2,1)}, u32[]{:S(2)}, u32[]{:S(2)}) collective-permute-start(bf16[512,256]{1,0:T(8,128)(2,1)S(1)} %gate_up.2.refs_0_), channel_id=1, source_target_pairs={{0,192},{64,0},{128,64},{192,128},{1,193},{65,1},{129,65},{193,129... | collective-permute-start | bytes 786440 | tf_op jit(solution)/shard_map/ppermute | solution.py:113
  110.7 35.1 %collective-permute-start.4 = (bf16[128,3712]{1,0:T(8,128)(2,1)S(1)}, bf16[128,3712]{1,0:T(8,128)(2,1)S(1)}, u32[]{:S(2)}, u32[]{:S(2)}) collective-permute-start(bf16[128,3712]{1,0:T(8,128)(2,1)S(1)} %reshape.59.refs_0_.refs_5_), channel_id=1, source_target_pairs={{0,64},{64,128},{128,192},{192,0},{1,65},{65,129},{129,193},{193,1... | collective-permute-start | bytes 2850824 | tf_op jit(solution)/shard_map/ppermute | solution.py:113
  110.8 36.6 %collective-permute-start.3 = (bf16[128,3712]{1,0:T(8,128)(2,1)S(1)}, bf16[128,3712]{1,0:T(8,128)(2,1)}, u32[]{:S(2)}, u32[]{:S(2)}) collective-permute-start(bf16[128,3712]{1,0:T(8,128)(2,1)S(1)} %reshape.59.refs_0_.refs_5_), channel_id=1, source_target_pairs={{0,192},{64,0},{128,64},{192,128},{1,193},{65,1},{129,65},{193,129... | collective-permute-start | bytes 2850824 | tf_op jit(solution)/shard_map/ppermute | solution.py:113
  121.2 2.0 copy-start.1
  130.4 64.0 %all-to-all-start.1 = ((bf16[256,2,896]{2,1,0:T(2,128)(2,1)}), bf16[256,2,896]{2,1,0:T(2,128)(2,1)}, u32[]{:S(2)}, u32[]{:S(2)}) async-start(bf16[256,2,896]{2,1,0:T(2,128)(2,1)} %reshape.56), calls=%async_computation.1 | async-start | bytes 1835008 | tf_op jit(solution)/shard_map/all_to_all | solution.py:187
  145.9 19.4 %collective-permute-start.5 = (bf16[64,3712]{1,0:T(8,128)(2,1)S(1)}, bf16[64,3712]{1,0:T(8,128)(2,1)S(1)}, u32[]{:S(2)}, u32[]{:S(2)}) collective-permute-start(bf16[64,3712]{1,0:T(8,128)(2,1)S(1)} %slice.12), channel_id=1, source_target_pairs={{0,64},{64,128},{128,192},{192,0},{1,65},{65,129},{129,193},{193,1... | collective-permute-start | bytes 1425416 | tf_op jit(solution)/shard_map/ppermute | solution.py:113
  148.4 19.3 %collective-permute-start.6 = (bf16[64,3712]{1,0:T(8,128)(2,1)S(1)}, bf16[64,3712]{1,0:T(8,128)(2,1)S(1)}, u32[]{:S(2)}, u32[]{:S(2)}) collective-permute-start(bf16[64,3712]{1,0:T(8,128)(2,1)S(1)} %slice.13), channel_id=1, source_target_pairs={{0,192},{64,0},{128,64},{192,128},{1,193},{65,1},{129,65},{193,129... | collective-permute-start | bytes 1425416 | tf_op jit(solution)/shard_map/ppermute | solution.py:113
  150.5 40.7 %copy-start.2 = (bf16[2,1024,896]{2,1,0:T(8,128)(2,1)S(1)}, bf16[2,1024,896]{2,1,0:T(8,128)(2,1)}, u32[]{:S(2)}) copy-start(bf16[2,1024,896]{2,1,0:T(8,128)(2,1)} %refs_7_.3) | copy-start | bytes 11010052
  167.7 2.0 copy-start.5
  169.8 2.0 copy-start.7
  176.9 8.6 %collective-permute-start.9 = (bf16[512,256]{1,0:T(8,128)(2,1)S(1)}, bf16[512,256]{1,0:T(8,128)(2,1)S(1)}, u32[]{:S(2)}, u32[]{:S(2)}) collective-permute-start(bf16[512,256]{1,0:T(8,128)(2,1)S(1)} %gate_up.3.refs_0_), channel_id=1, source_target_pairs={{0,64},{64,128},{128,192},{192,0},{1,65},{65,129},{129,193},{193,1... | collective-permute-start | bytes 786440 | tf_op jit(solution)/shard_map/ppermute | solution.py:113
  178.6 10.1 %collective-permute-start.8 = (bf16[512,256]{1,0:T(8,128)(2,1)S(1)}, bf16[512,256]{1,0:T(8,128)(2,1)S(1)}, u32[]{:S(2)}, u32[]{:S(2)}) collective-permute-start(bf16[512,256]{1,0:T(8,128)(2,1)S(1)} %gate_up.3.refs_0_), channel_id=1, source_target_pairs={{0,128},{64,192},{128,0},{192,64},{1,129},{65,193},{129,1},{193,65... | collective-permute-start | bytes 786440 | tf_op jit(solution)/shard_map/ppermute | solution.py:113
  179.6 11.6 %collective-permute-start.7 = (bf16[512,256]{1,0:T(8,128)(2,1)S(1)}, bf16[512,256]{1,0:T(8,128)(2,1)S(1)}, u32[]{:S(2)}, u32[]{:S(2)}) collective-permute-start(bf16[512,256]{1,0:T(8,128)(2,1)S(1)} %gate_up.3.refs_0_), channel_id=1, source_target_pairs={{0,192},{64,0},{128,64},{192,128},{1,193},{65,1},{129,65},{193,129... | collective-permute-start | bytes 786440 | tf_op jit(solution)/shard_map/ppermute | solution.py:113
  193.0 15.8 %copy-start.11 = (bf16[16,8]{0,1:T(8,128)(2,1)S(1)}, bf16[16,8]{0,1:T(8,128)(2,1)}, u32[]{:S(2)}) copy-start(bf16[16,8]{0,1:T(8,128)(2,1)} %param.11) | copy-start | bytes 772
  194.3 42.8 %all-to-all-start.3 = ((bf16[256,2,896]{2,1,0:T(2,128)(2,1)}), bf16[256,2,896]{2,1,0:T(2,128)(2,1)S(1)}, u32[]{:S(2)}, u32[]{:S(2)}) async-start(bf16[256,2,896]{2,1,0:T(2,128)(2,1)} %reshape.60), calls=%async_computation.3 | async-start | bytes 1835008 | tf_op jit(solution)/shard_map/all_to_all | solution.py:187
  (2 other events, 2.6 us)
Sparse Core Ops, SparseCore 0:
  51.4 44.8 all-gather.1

commit v3 on v1

--- a/solution.py
+++ b/solution.py
@@ -1,9 +1,178 @@
+import functools
+
 import jax
 import jax.numpy as jnp
 from jax import lax
+from jax.experimental import pallas as pl
+from jax.experimental.pallas import tpu as pltpu
 from jax.sharding import PartitionSpec as P
 
 ADAPTER_RANK = 16
+VMEM_LIMIT = 57 * 1024 * 1024
+
+
+def gate_up_kernel(parts, expert, chunks, *refs):
+    rows = refs[:parts]
+    gate_ref, up_ref, factor_ref = refs[parts : parts + 3]
+    hidden_ref, x, gate_at, up_at, factor_at, sems = refs[-6:]
+    width, adapters = gate_ref.shape[1], factor_ref.shape[0]
+    depth = width // chunks
+    copies = []
+    for c in range(chunks):
+        here = pl.ds(c * depth, depth)
+        wide = here if c < chunks - 1 else pl.ds(c * depth, depth + adapters)
+        pairs, row = [], 0
+        for part in rows:
+            count = part.shape[0]
+            pairs.append((part.at[:, wide], x.at[pl.ds(row, count), wide]))
+            row += count
+        pairs.append((gate_ref.at[expert, here], gate_at.at[here]))
+        pairs.append((up_ref.at[expert, here], up_at.at[here]))
+        if c == 0:
+            pairs.append((factor_ref, factor_at))
+        started = [
+            pltpu.make_async_copy(src, dst, sems.at[c, i]) for i, (src, dst) in enumerate(pairs)
+        ]
+        for copy in started:
+            copy.start()
+        copies.append(started)
+    gate = up = 0.0
+    for c in range(chunks):
+        for copy in copies[c]:
+            copy.wait()
+        here = slice(c * depth, (c + 1) * depth)
+        gate += jnp.dot(x[:, here], gate_at[here], preferred_element_type=jnp.float32)
+        up += jnp.dot(x[:, here], up_at[here], preferred_element_type=jnp.float32)
+    up += jnp.dot(x[:, width:], factor_at[...], preferred_element_type=jnp.float32)
+    hidden_ref[...] = (gate / (1.0 + jnp.exp(-gate)) * up).astype(hidden_ref.dtype)
+
+
+def gate_up(rows, gate_weight, up_weight, factor, expert, after):
+    width, units = gate_weight.shape[1:]
+    adapters = factor.shape[0]
+    chunks = 7
+    parts = len(rows)
+    count = sum(r.shape[0] for r in rows)
+    anywhere = pl.BlockSpec(memory_space=pl.ANY)
+    return pl.pallas_call(
+        functools.partial(gate_up_kernel, parts, expert, chunks),
+        in_specs=[anywhere] * (parts + 3 + len(after)),
+        out_shape=jax.ShapeDtypeStruct((count, units), jnp.bfloat16),
+        scratch_shapes=[
+            pltpu.VMEM((count, width + adapters), jnp.bfloat16),
+            pltpu.VMEM((width, units), jnp.bfloat16),
+            pltpu.VMEM((width, units), jnp.bfloat16),
+            pltpu.VMEM((adapters, units), jnp.bfloat16),
+            pltpu.SemaphoreType.DMA((chunks, parts + 3)),
+        ],
+        compiler_params=pltpu.CompilerParams(vmem_limit_bytes=VMEM_LIMIT),
+        cost_estimate=pl.CostEstimate(flops=1000, bytes_accessed=1000, transcendentals=0),
+        name="gate_up",
+    )(*rows, gate_weight, up_weight, factor, *after)
+
+
+def down_kernel(groups, experts, me_ref, *refs):
+    hidden = [refs[e * groups : (e + 1) * groups] for e in range(experts)]
+    weight_ref = refs[experts * groups]
+    out_ref, x, weight_at, sems = refs[-4:]
+    count, units = hidden[0][0].shape
+    block = count // groups
+    me = me_ref[0]
+    copies = []
+    for e in range(experts):
+        started = []
+        for s in range(groups):
+            owner = lax.rem(me + s, groups)
+            started.append(
+                pltpu.make_async_copy(
+                    weight_ref.at[e, pl.ds(pl.multiple_of(owner * units, units), units)],
+                    weight_at.at[e, pl.ds(s * units, units)],
+                    sems.at[e, s, groups],
+                )
+            )
+            for i in range(groups):
+                started.append(
+                    pltpu.make_async_copy(
+                        hidden[e][s].at[pl.ds((i - s) % groups * block, block)],
+                        x.at[e, pl.ds(i * block, block), pl.ds(s * units, units)],
+                        sems.at[e, s, i],
+                    )
+                )
+        for copy in started:
+            copy.start()
+        copies.append(started)
+    for e in range(experts):
+        for copy in copies[e]:
+            copy.wait()
+        out = jnp.dot(x[e], weight_at[e], preferred_element_type=jnp.float32)
+        out = out.astype(out_ref.dtype)
+        senders = block // out_ref.shape[2]
+        for i in range(groups):
+            at = pl.ds(lax.rem(me + i, groups) * senders, senders)
+            rows = out[i * block : (i + 1) * block]
+            out_ref[at, e] = rows.reshape((senders,) + out_ref.shape[2:])
+
+
+def down(hidden, down_weight, me, capacity):
+    experts, groups = len(hidden), len(hidden[0])
+    count, units = hidden[0][0].shape
+    share = down_weight.shape[2]
+    anywhere = pl.BlockSpec(memory_space=pl.ANY)
+    return pl.pallas_call(
+        functools.partial(down_kernel, groups, experts),
+        in_specs=[pl.BlockSpec(memory_space=pltpu.SMEM)]
+        + [anywhere] * (groups * experts + 1),
+        out_shape=jax.ShapeDtypeStruct((count // capacity, experts, capacity, share), jnp.bfloat16),
+        scratch_shapes=[
+            pltpu.VMEM((experts, count, groups * units), jnp.bfloat16),
+            pltpu.VMEM((experts, groups * units, share), jnp.bfloat16),
+            pltpu.SemaphoreType.DMA((experts, groups, groups + 1)),
+        ],
+        compiler_params=pltpu.CompilerParams(vmem_limit_bytes=VMEM_LIMIT),
+        cost_estimate=pl.CostEstimate(flops=1000, bytes_accessed=1000, transcendentals=0),
+        name="down",
+    )(me, *[h for of_expert in hidden for h in of_expert], down_weight)
+
+
+def relayout_kernel(x_ref, *refs):
+    refs[-1][...] = x_ref[...].reshape(refs[-1].shape)
+
+
+def relayout(x, shape, after):
+    return pl.pallas_call(
+        relayout_kernel,
+        in_specs=[pl.BlockSpec(memory_space=pltpu.VMEM)]
+        + [pl.BlockSpec(memory_space=pl.ANY)] * len(after),
+        out_shape=jax.ShapeDtypeStruct(shape, x.dtype),
+        compiler_params=pltpu.CompilerParams(vmem_limit_bytes=VMEM_LIMIT),
+        cost_estimate=pl.CostEstimate(flops=1000, bytes_accessed=1000, transcendentals=0),
+        name="relayout",
+    )(x, *after)
+
+
+def halves_kernel(half, before_ref, after_ref, *refs):
+    top_ref, bottom_ref = refs[-2:]
+    top_ref[...] = before_ref[:half]
+    bottom_ref[...] = after_ref[half:]
+
+
+def halves(before_me, after_me, after):
+    count, width = before_me.shape
+    half = count // 2
+    vmem = pl.BlockSpec(memory_space=pltpu.VMEM)
+    return pl.pallas_call(
+        functools.partial(halves_kernel, half),
+        in_specs=[vmem, vmem] + [pl.BlockSpec(memory_space=pl.ANY)] * len(after),
+        out_shape=[jax.ShapeDtypeStruct((half, width), before_me.dtype)] * 2,
+        compiler_params=pltpu.CompilerParams(vmem_limit_bytes=VMEM_LIMIT),
+        cost_estimate=pl.CostEstimate(flops=1000, bytes_accessed=1000, transcendentals=0),
+        name="halves",
+    )(before_me, after_me, *after)
+
+
+def from_further(x, by):
+    n = lax.axis_size("rep")
+    return lax.ppermute(x, "rep", [(i, (i - by) % n) for i in range(n)])
 
 
 def per_device(
@@ -56,30 +225,27 @@
         )
         packed = jnp.einsum("ri,rd->id", routing, rows, preferred_element_type=f32).astype(bf16)
         packed = packed.reshape(owners, capacity, width + adapters)
-        received.append(lax.all_to_all(packed, "ep", split_axis=0, concat_axis=0, tiled=True))
-    combiner = lax.all_gather(jnp.stack(combiners), "rep", axis=0)
-
-    total = jnp.zeros((groups, row_count, share), f32)
-    for j in range(local_count):
-        mine = received[j].reshape(slots, width + adapters)
-        every = lax.all_gather(mine, "rep", axis=0, tiled=True)
-        row_part, low_part = every[:, :width], every[:, width:]
-        gate = jnp.dot(row_part, gate_weight[j], preferred_element_type=f32)
-        up = jnp.dot(row_part, up_weight[j], preferred_element_type=f32) + jnp.dot(
-            low_part, adapter_up_factor, preferred_element_type=f32
-        )
-        hidden = (jax.nn.silu(gate) * up).astype(bf16)
-        hidden = lax.all_gather(hidden, "rep", axis=1, tiled=True)
-        out = jnp.dot(hidden, down_weight[j], preferred_element_type=f32).astype(bf16)
-        out = out.reshape(groups, owners, capacity, share).transpose(1, 0, 2, 3)
-        back = lax.all_to_all(out, "ep", split_axis=0, concat_axis=0, tiled=True)
-        back = back.transpose(1, 0, 2, 3).reshape(groups, slots, share)
-        total = total + jnp.einsum(
-            "gri,gid->grd", combiner[:, j], back, preferred_element_type=f32
-        )
-    mixed = total.astype(bf16)
-    mixed = lax.all_to_all(mixed, "rep", split_axis=0, concat_axis=0, tiled=True)
-    return mixed.transpose(1, 0, 2).reshape(row_count, width)
+        sent = lax.all_to_all(packed, "ep", split_axis=0, concat_axis=0, tiled=True)
+        received.append(sent)
+
+    me = lax.axis_index("rep").astype(jnp.int32).reshape(1)
+    half = slots // 2
+    hidden = []
+    for j, sent in enumerate(received):
+        mine = relayout(sent, (slots, width + adapters), [])
+        before_me, after_me = from_further(mine, -1), from_further(mine, 1)
+        across = [from_further(before_me[:half], -1), from_further(after_me[half:], 1)]
+        every = [mine, after_me, *across, before_me]
+        units = gate_up(every, gate_weight, up_weight, adapter_up_factor, j, [])
+        hidden.append([units] + [from_further(units, s) for s in range(1, groups)])
+    back = down(hidden, down_weight, me, capacity)
+    back = lax.all_to_all(back, ("rep", "ep"), split_axis=0, concat_axis=0, tiled=True)
+    back = back.reshape(groups, owners * local_count * capacity, share)
+    combiner = jnp.stack([c.reshape(row_count, owners, capacity) for c in combiners], axis=2)
+    total = jnp.einsum(
+        "ri,gid->rgd", combiner.reshape(row_count, -1), back, preferred_element_type=f32
+    )
+    return total.astype(bf16).reshape(row_count, width)
 
 
 def solution(mesh):

time: 273 us -> 216 us (0.79)
  blocking collectives: 89.1 us -> 0 us
  starting transfers between devices: 20.3 us -> 48.7 us
  waiting for transfers between devices: 104 us -> 128 us
  Pallas kernels: 0 us -> 21.4 us
  matrix products: 22.5 us -> 4.82 us
  between operations: 13.4 us -> 0.33 us
  local copies, waits for them, and re-layouts: 21.1 us -> 11.2 us
    all_gather x4 -> x0, waiting for transfers between devices: 90.4 us -> none  [the longest x2 53.1 us: per_device(): every = lax.all_gather(mine, 'rep', axis=0, tiled=True)]
    all_to_all x3 -> x0, blocking collectives: 79.2 us -> none  [the longest x2 71 us: per_device(): lax.all_to_all(packed, 'ep', split_axis=0, concat_axis=0, tiled=True)]
    all_to_all x2 -> x3, waiting for transfers between devices: 14 us -> 92.4 us  [the longest x1 47.2 us: per_device(): lax.all_to_all(back, ('rep', 'ep'), split_axis=0, concat_axis=0, tiled=True)]
    ppermute x0 -> x14, waiting for transfers between devices: none -> 35.2 us  [from_further(): return lax.ppermute(x, 'rep', [(i, (i - by) % n) for i in range(n)])]
    pallas_call x0 -> x5, Pallas kernels: none -> 21.4 us  [the longest x2 11 us: gate_up(): pl.pallas_call(functools.partial(gate_up_kernel, parts, expert, chunks),...]
    dot_general x10 -> x1, matrix products: 19.5 us -> 1.87 us  [per_device(): jnp.einsum('ri,gid->rgd', combiner.reshape(row_count, -1), back, preferre...]
    ppermute x0 -> x14, starting transfers between devices: none -> 16.8 us  [from_further(): return lax.ppermute(x, 'rep', [(i, (i - by) % n) for i in range(n)])]
    reshape x9 -> x2, local copies, waits for them, and re-layouts: 14.2 us -> 2.34 us  [the longest x1 1.68 us: per_device(): back = back.reshape(groups, owners * local_count * capacity, share)]
  transfers between devices with their start and end apart: 6 -> 17, of which waited for: 6 -> 10; matrix products, arithmetic and copies ran while one was open for 12% -> 2% of each run, Pallas kernels for 0% -> 7%
where the time goes in v3:
time: 216 us; the launch traced here: 215 us
  waiting for transfers between devices  128 us (59%)
  starting transfers between devices  48.7 us (23%)
  Pallas kernels  21.4 us (10%)
  local copies, waits for them, and re-layouts  11.2 us (5%)
  matrix products  4.82 us (2%)
    all_to_all x1, waiting for transfers between devices, per_device(): lax.all_to_all(back, ('rep', 'ep'), split_axis=0, concat_axis=0, tiled=True)  47.2 us
    all_to_all x2, waiting for transfers between devices, per_device(): sent = lax.all_to_all(packed, 'ep', split_axis=0, concat_axis=0, tiled=True)  45.2 us
    ppermute x14, waiting for transfers between devices, from_further(): return lax.ppermute(x, 'rep', [(i, (i - by) % n) for i in range(n)])  35.2 us
    all_to_all x2, starting transfers between devices, per_device(): sent = lax.all_to_all(packed, 'ep', split_axis=0, concat_axis=0, tiled=True)  19.4 us
    ppermute x14, starting transfers between devices, from_further(): return lax.ppermute(x, 'rep', [(i, (i - by) % n) for i in range(n)])  16.8 us
    all_to_all x1, starting transfers between devices, per_device(): lax.all_to_all(back, ('rep', 'ep'), split_axis=0, concat_axis=0, tiled=True)  12.5 us
    pallas_call x2, Pallas kernels, gate_up(): pl.pallas_call(functools.partial(gate_up_kernel, parts, expert, chunks),...  11 us
    pallas_call x1, Pallas kernels, down(): pl.pallas_call(functools.partial(down_kernel, groups, experts), in_specs=...  5.9 us
  transfers between devices with their start and end apart: 17, of which 10 were waited for; matrix products, arithmetic and copies ran while one was open for 2% of the time, Pallas kernels for 7%

profile of v3, /device:TPU:1, one launch (start us, length us, event | category | flops | bytes accessed | tf_op | source)
XLA Modules:
  0.0 215.0 jit_solution(10748729813274659468)
XLA Ops:
  2.8 1.4 convolution_convert_fusion
  5.5 13.0 %all-to-all-start.1 = ((bf16[64,2,3712]{2,1,0:T(2,128)(2,1)}), bf16[64,2,3712]{2,1,0:T(2,128)(2,1)S(1)}, u32[]{:S(2)}, u32[]{:S(2)}) async-start(bf16[64,2,3712]{2,1,0:T(2,128)(2,1)} %reshape.66), calls=%async_computation.1 | async-start | bytes 1900544 | tf_op jit(solution)/shard_map/all_to_all | solution.py:228
  20.3 24.2 %all-to-all-done.1.x_ref = bf16[64,2,3712]{2,1,0:T(2,128)(2,1)S(1)} async-done(((bf16[64,2,3712]{2,1,0:T(2,128)(2,1)}), bf16[64,2,3712]{2,1,0:T(2,128)(2,1)S(1)}, u32[]{:S(2)}, u32[]{:S(2)}) %all-to-all-start.1) | async-done | bytes 950304 | tf_op jit(solution)/shard_map/all_to_all | solution.py:228
  44.5 6.5 %all-to-all-start = ((bf16[64,2,3712]{2,1,0:T(2,128)(2,1)}), bf16[64,2,3712]{2,1,0:T(2,128)(2,1)S(1)}, u32[]{:S(2)}, u32[]{:S(2)}) async-start(bf16[64,2,3712]{2,1,0:T(2,128)(2,1)} %reshape.65), calls=%async_computation | async-start | bytes 1900544 | tf_op jit(solution)/shard_map/all_to_all | solution.py:228
  51.0 2.3 %relayout.3.refs_0_ = bf16[128,3712]{1,0:T(8,128)(2,1)} custom-call(bf16[64,2,3712]{2,1,0:T(2,128)(2,1)} %copy-done.1), custom_call_target="tpu_custom_call" | custom-call | flops 1000 | bytes 1000 | tf_op jit(solution)/shard_map/relayout/pallas_call | solution.py:142
  53.2 2.7 %collective-permute-start.7 = (bf16[128,3712]{1,0:T(8,128)(2,1)}, bf16[128,3712]{1,0:T(8,128)(2,1)S(1)}, u32[]{:S(2)}, u32[]{:S(2)}) collective-permute-start(bf16[128,3712]{1,0:T(8,128)(2,1)} %relayout.3.refs_0_), channel_id=1, source_target_pairs={{0,192},{64,0},{128,64},{192,128},{1,193},{65,1},{129,65},{193,129... | collective-permute-start | bytes 2850824 | tf_op jit(solution)/shard_map/ppermute | solution.py:175
  55.9 21.0 %all-to-all-done.x_ref = bf16[64,2,3712]{2,1,0:T(2,128)(2,1)S(1)} async-done(((bf16[64,2,3712]{2,1,0:T(2,128)(2,1)}), bf16[64,2,3712]{2,1,0:T(2,128)(2,1)S(1)}, u32[]{:S(2)}, u32[]{:S(2)}) %all-to-all-start) | async-done | bytes 950304 | tf_op jit(solution)/shard_map/all_to_all | solution.py:228
  77.9 2.3 %relayout.2.refs_0_ = bf16[128,3712]{1,0:T(8,128)(2,1)} custom-call(bf16[64,2,3712]{2,1,0:T(2,128)(2,1)} %copy-done.2), custom_call_target="tpu_custom_call" | custom-call | flops 1000 | bytes 1000 | tf_op jit(solution)/shard_map/relayout/pallas_call | solution.py:142
  81.4 1.4 collective-permute-start
  82.9 1.5 collective-permute-start.10
  85.6 17.4 %collective-permute-done.1.refs_4_ = bf16[128,3712]{1,0:T(8,128)(2,1)S(1)} collective-permute-done((bf16[128,3712]{1,0:T(8,128)(2,1)}, bf16[128,3712]{1,0:T(8,128)(2,1)S(1)}, u32[]{:S(2)}, u32[]{:S(2)}) %collective-permute-start.1) | collective-permute-done | bytes 950304 | tf_op jit(solution)/shard_map/ppermute | solution.py:175
  103.2 2.9 %collective-permute-start.3 = (bf16[64,3712]{1,0:T(8,128)(2,1)S(1)}, bf16[64,3712]{1,0:T(8,128)(2,1)S(1)}, u32[]{:S(2)}, u32[]{:S(2)}) collective-permute-start(bf16[64,3712]{1,0:T(8,128)(2,1)S(1)} %slice.17), channel_id=1, source_target_pairs={{0,192},{64,0},{128,64},{192,128},{1,193},{65,1},{129,65},{193,129... | collective-permute-start | bytes 1425416 | tf_op jit(solution)/shard_map/ppermute | solution.py:175
  106.1 6.9 %collective-permute-done.10.refs_3_ = bf16[64,3712]{1,0:T(8,128)(2,1)S(1)} collective-permute-done((bf16[64,3712]{1,0:T(8,128)(2,1)S(1)}, bf16[64,3712]{1,0:T(8,128)(2,1)S(1)}, u32[]{:S(2)}, u32[]{:S(2)}) %collective-permute-start.10) | collective-permute-done | bytes 475168 | tf_op jit(solution)/shard_map/ppermute | solution.py:175
  113.7 5.5 %gate_up.3.refs_4_ = bf16[512,256]{1,0:T(8,128)(2,1)} custom-call(bf16[128,3712]{1,0:T(8,128)(2,1)} %relayout.3.refs_0_, bf16[128,3712]{1,0:T(8,128)(2,1)} %copy-done.5, bf16[64,3712]{1,0:T(8,128)(2,1)} %collective-permute-done.9.refs_2_, bf16[64,3712]{1,0:T(8,128)(2,1)} %copy-done.9, bf16[128,3712]{1,0:T(8,128)(2,1)} %collective-permute-done.8.refs_4_, ...), custom_call_target="tpu_custom_call" | custom-call | flops 1000 | bytes 1000 | tf_op jit(solution)/shard_map/gate_up/pallas_call | solution.py:57
  119.3 2.7 %collective-permute-start.11 = (bf16[512,256]{1,0:T(8,128)(2,1)}, bf16[512,256]{1,0:T(8,128)(2,1)S(1)}, u32[]{:S(2)}, u32[]{:S(2)}) collective-permute-start(bf16[512,256]{1,0:T(8,128)(2,1)} %gate_up.3.refs_4_), channel_id=1, source_target_pairs={{0,192},{64,0},{128,64},{192,128},{1,193},{65,1},{129,65},{193,129... | collective-permute-start | bytes 786440 | tf_op jit(solution)/shard_map/ppermute | solution.py:175
  124.9 5.5 %gate_up.2.refs_0_ = bf16[512,256]{1,0:T(8,128)(2,1)} custom-call(bf16[128,3712]{1,0:T(8,128)(2,1)} %relayout.2.refs_0_, bf16[128,3712]{1,0:T(8,128)(2,1)} %copy-done.4, bf16[64,3712]{1,0:T(8,128)(2,1)} %copy-done.7, bf16[64,3712]{1,0:T(8,128)(2,1)} %copy-done.8, bf16[128,3712]{1,0:T(8,128)(2,1)} %copy-done.3, bf16[2,3584,256]{2,1,0:T(8,128)(2,1)} %refs_5_.3, ...), custom_call_target="tpu_custom_call" | custom-call | flops 1000 | bytes 1000 | tf_op jit(solution)/shard_map/gate_up/pallas_call | solution.py:57
  130.4 1.9 collective-permute-start.4
  133.6 6.0 %collective-permute-done.4.refs_1_ = bf16[512,256]{1,0:T(8,128)(2,1)S(1)} collective-permute-done((bf16[512,256]{1,0:T(8,128)(2,1)}, bf16[512,256]{1,0:T(8,128)(2,1)S(1)}, u32[]{:S(2)}, u32[]{:S(2)}) %collective-permute-start.4) | collective-permute-done | bytes 262176 | tf_op jit(solution)/shard_map/ppermute | solution.py:175
  140.3 3.4 %collective-permute-done.6.refs_3_ = bf16[512,256]{1,0:T(8,128)(2,1)S(1)} collective-permute-done((bf16[512,256]{1,0:T(8,128)(2,1)}, bf16[512,256]{1,0:T(8,128)(2,1)S(1)}, u32[]{:S(2)}, u32[]{:S(2)}) %collective-permute-start.6) | collective-permute-done | bytes 262176 | tf_op jit(solution)/shard_map/ppermute | solution.py:175
  144.4 5.9 %down.1 = bf16[256,2,2,896]{3,2,1,0:T(2,128)(2,1)} custom-call(s32[1]{0:T(128)} %bitcast.4.me_ref, bf16[512,256]{1,0:T(8,128)(2,1)} %gate_up.2.refs_0_, bf16[512,256]{1,0:T(8,128)(2,1)} %copy-done.13, bf16[512,256]{1,0:T(8,128)(2,1)} %copy-done.14, bf16[512,256]{1,0:T(8,128)(2,1)} %copy-done.15, bf16[512,256]{1,0:T(8,128)(2,1)} %gate_up.3.refs_4_, ...), custom_call_target="tpu_custom_call" | custom-call | flops 1000 | bytes 1000 | tf_op jit(solution)/shard_map/down/pallas_call | solution.py:121
  150.3 12.5 %all-to-all-start.2 = ((bf16[256,2,2,896]{3,2,1,0:T(2,128)(2,1)}), bf16[256,2,2,896]{3,2,1,0:T(2,128)(2,1)S(1)}, u32[]{:S(2)}, u32[]{:S(2)}) async-start(bf16[256,2,2,896]{3,2,1,0:T(2,128)(2,1)} %down.1), calls=%async_computation.2 | async-start | bytes 3670016 | tf_op jit(solution)/shard_map/all_to_all | solution.py:242
  163.6 47.2 %all-to-all-done.2 = bf16[256,2,2,896]{3,2,1,0:T(2,128)(2,1)S(1)} async-done(((bf16[256,2,2,896]{3,2,1,0:T(2,128)(2,1)}), bf16[256,2,2,896]{3,2,1,0:T(2,128)(2,1)S(1)}, u32[]{:S(2)}, u32[]{:S(2)}) %all-to-all-start.2) | async-done | bytes 1835040 | tf_op jit(solution)/shard_map/all_to_all | solution.py:242
  210.8 1.7 reshape.67
  212.5 1.9 fusion
  (77 shorter events, 17.2 us)
Async XLA Ops:
  4.2 14.3 %copy-start.6 = (bf16[16,3584]{1,0:T(8,128)(2,1)S(1)}, bf16[16,3584]{1,0:T(8,128)(2,1)}, u32[]{:S(2)}) copy-start(bf16[16,3584]{1,0:T(8,128)(2,1)} %param.9) | copy-start | bytes 344068
  5.5 39.0 %all-to-all-start.1 = ((bf16[64,2,3712]{2,1,0:T(2,128)(2,1)}), bf16[64,2,3712]{2,1,0:T(2,128)(2,1)S(1)}, u32[]{:S(2)}, u32[]{:S(2)}) async-start(bf16[64,2,3712]{2,1,0:T(2,128)(2,1)} %reshape.66), calls=%async_computation.1 | async-start | bytes 1900544 | tf_op jit(solution)/shard_map/all_to_all | solution.py:228
  44.5 32.4 %all-to-all-start = ((bf16[64,2,3712]{2,1,0:T(2,128)(2,1)}), bf16[64,2,3712]{2,1,0:T(2,128)(2,1)S(1)}, u32[]{:S(2)}, u32[]{:S(2)}) async-start(bf16[64,2,3712]{2,1,0:T(2,128)(2,1)} %reshape.65), calls=%async_computation | async-start | bytes 1900544 | tf_op jit(solution)/shard_map/all_to_all | solution.py:228
  53.2 29.7 %collective-permute-start.7 = (bf16[128,3712]{1,0:T(8,128)(2,1)}, bf16[128,3712]{1,0:T(8,128)(2,1)S(1)}, u32[]{:S(2)}, u32[]{:S(2)}) collective-permute-start(bf16[128,3712]{1,0:T(8,128)(2,1)} %relayout.3.refs_0_), channel_id=1, source_target_pairs={{0,192},{64,0},{128,64},{192,128},{1,193},{65,1},{129,65},{193,129... | collective-permute-start | bytes 2850824 | tf_op jit(solution)/shard_map/ppermute | solution.py:175
  55.9 28.5 %collective-permute-start.8 = (bf16[128,3712]{1,0:T(8,128)(2,1)}, bf16[128,3712]{1,0:T(8,128)(2,1)}, u32[]{:S(2)}, u32[]{:S(2)}) collective-permute-start(bf16[128,3712]{1,0:T(8,128)(2,1)} %relayout.3.refs_0_), channel_id=1, source_target_pairs={{0,64},{64,128},{128,192},{192,0},{1,65},{65,129},{129,193},{193,1... | collective-permute-start | bytes 2850824 | tf_op jit(solution)/shard_map/ppermute | solution.py:175
  80.1 22.8 %collective-permute-start.1 = (bf16[128,3712]{1,0:T(8,128)(2,1)}, bf16[128,3712]{1,0:T(8,128)(2,1)S(1)}, u32[]{:S(2)}, u32[]{:S(2)}) collective-permute-start(bf16[128,3712]{1,0:T(8,128)(2,1)} %relayout.2.refs_0_), channel_id=1, source_target_pairs={{0,64},{64,128},{128,192},{192,0},{1,65},{65,129},{129,193},{193,1... | collective-permute-start | bytes 2850824 | tf_op jit(solution)/shard_map/ppermute | solution.py:175
  81.4 21.7 %collective-permute-start = (bf16[128,3712]{1,0:T(8,128)(2,1)}, bf16[128,3712]{1,0:T(8,128)(2,1)S(1)}, u32[]{:S(2)}, u32[]{:S(2)}) collective-permute-start(bf16[128,3712]{1,0:T(8,128)(2,1)} %relayout.2.refs_0_), channel_id=1, source_target_pairs={{0,192},{64,0},{128,64},{192,128},{1,193},{65,1},{129,65},{193,129... | collective-permute-start | bytes 2850824 | tf_op jit(solution)/shard_map/ppermute | solution.py:175
  82.9 20.3 %copy-start.5 = (bf16[128,3712]{1,0:T(8,128)(2,1)}, bf16[128,3712]{1,0:T(8,128)(2,1)S(1)}, u32[]{:S(2)}) copy-start(bf16[128,3712]{1,0:T(8,128)(2,1)S(1)} %collective-permute-done.7.refs_1_) | copy-start | bytes 2850820
  82.9 30.0 %collective-permute-start.10 = (bf16[64,3712]{1,0:T(8,128)(2,1)S(1)}, bf16[64,3712]{1,0:T(8,128)(2,1)S(1)}, u32[]{:S(2)}, u32[]{:S(2)}) collective-permute-start(bf16[64,3712]{1,0:T(8,128)(2,1)S(1)} %slice.19), channel_id=1, source_target_pairs={{0,192},{64,0},{128,64},{192,128},{1,193},{65,1},{129,65},{193,129... | collective-permute-start | bytes 1425416 | tf_op jit(solution)/shard_map/ppermute | solution.py:175
  85.5 27.7 %collective-permute-start.9 = (bf16[64,3712]{1,0:T(8,128)(2,1)S(1)}, bf16[64,3712]{1,0:T(8,128)(2,1)}, u32[]{:S(2)}, u32[]{:S(2)}) collective-permute-start(bf16[64,3712]{1,0:T(8,128)(2,1)S(1)} %slice.18), channel_id=1, source_target_pairs={{0,64},{64,128},{128,192},{192,0},{1,65},{65,129},{129,193},{193,1... | collective-permute-start | bytes 1425416 | tf_op jit(solution)/shard_map/ppermute | solution.py:175
  103.0 16.3 %copy-start.3 = (bf16[128,3712]{1,0:T(8,128)(2,1)}, bf16[128,3712]{1,0:T(8,128)(2,1)S(1)}, u32[]{:S(2)}) copy-start(bf16[128,3712]{1,0:T(8,128)(2,1)S(1)} %collective-permute-done.1.refs_4_) | copy-start | bytes 2850820
  103.0 20.3 %collective-permute-start.2 = (bf16[64,3712]{1,0:T(8,128)(2,1)S(1)}, bf16[64,3712]{1,0:T(8,128)(2,1)S(1)}, u32[]{:S(2)}, u32[]{:S(2)}) collective-permute-start(bf16[64,3712]{1,0:T(8,128)(2,1)S(1)} %slice.16), channel_id=1, source_target_pairs={{0,64},{64,128},{128,192},{192,0},{1,65},{65,129},{129,193},{193,1... | collective-permute-start | bytes 1425416 | tf_op jit(solution)/shard_map/ppermute | solution.py:175
  103.1 16.1 %copy-start.4 = (bf16[128,3712]{1,0:T(8,128)(2,1)}, bf16[128,3712]{1,0:T(8,128)(2,1)S(1)}, u32[]{:S(2)}) copy-start(bf16[128,3712]{1,0:T(8,128)(2,1)S(1)} %collective-permute-done.refs_1_) | copy-start | bytes 2850820
  103.2 20.2 %collective-permute-start.3 = (bf16[64,3712]{1,0:T(8,128)(2,1)S(1)}, bf16[64,3712]{1,0:T(8,128)(2,1)S(1)}, u32[]{:S(2)}, u32[]{:S(2)}) collective-permute-start(bf16[64,3712]{1,0:T(8,128)(2,1)S(1)} %slice.17), channel_id=1, source_target_pairs={{0,192},{64,0},{128,64},{192,128},{1,193},{65,1},{129,65},{193,129... | collective-permute-start | bytes 1425416 | tf_op jit(solution)/shard_map/ppermute | solution.py:175
  119.3 14.3 %collective-permute-start.11 = (bf16[512,256]{1,0:T(8,128)(2,1)}, bf16[512,256]{1,0:T(8,128)(2,1)S(1)}, u32[]{:S(2)}, u32[]{:S(2)}) collective-permute-start(bf16[512,256]{1,0:T(8,128)(2,1)} %gate_up.3.refs_4_), channel_id=1, source_target_pairs={{0,192},{64,0},{128,64},{192,128},{1,193},{65,1},{129,65},{193,129... | collective-permute-start | bytes 786440 | tf_op jit(solution)/shard_map/ppermute | solution.py:175
  122.0 11.6 %collective-permute-start.12 = (bf16[512,256]{1,0:T(8,128)(2,1)}, bf16[512,256]{1,0:T(8,128)(2,1)S(1)}, u32[]{:S(2)}, u32[]{:S(2)}) collective-permute-start(bf16[512,256]{1,0:T(8,128)(2,1)} %gate_up.3.refs_4_), channel_id=1, source_target_pairs={{0,128},{64,192},{128,0},{192,64},{1,129},{65,193},{129,1},{193,65... | collective-permute-start | bytes 786440 | tf_op jit(solution)/shard_map/ppermute | solution.py:175
  122.4 11.2 %collective-permute-start.13 = (bf16[512,256]{1,0:T(8,128)(2,1)}, bf16[512,256]{1,0:T(8,128)(2,1)S(1)}, u32[]{:S(2)}, u32[]{:S(2)}) collective-permute-start(bf16[512,256]{1,0:T(8,128)(2,1)} %gate_up.3.refs_4_), channel_id=1, source_target_pairs={{0,64},{64,128},{128,192},{192,0},{1,65},{65,129},{129,193},{193,1... | collective-permute-start | bytes 786440 | tf_op jit(solution)/shard_map/ppermute | solution.py:175
  130.4 9.2 %collective-permute-start.4 = (bf16[512,256]{1,0:T(8,128)(2,1)}, bf16[512,256]{1,0:T(8,128)(2,1)S(1)}, u32[]{:S(2)}, u32[]{:S(2)}) collective-permute-start(bf16[512,256]{1,0:T(8,128)(2,1)} %gate_up.2.refs_0_), channel_id=1, source_target_pairs={{0,192},{64,0},{128,64},{192,128},{1,193},{65,1},{129,65},{193,129... | collective-permute-start | bytes 786440 | tf_op jit(solution)/shard_map/ppermute | solution.py:175
  132.3 8.1 %collective-permute-start.5 = (bf16[512,256]{1,0:T(8,128)(2,1)}, bf16[512,256]{1,0:T(8,128)(2,1)S(1)}, u32[]{:S(2)}, u32[]{:S(2)}) collective-permute-start(bf16[512,256]{1,0:T(8,128)(2,1)} %gate_up.2.refs_0_), channel_id=1, source_target_pairs={{0,128},{64,192},{128,0},{192,64},{1,129},{65,193},{129,1},{193,65... | collective-permute-start | bytes 786440 | tf_op jit(solution)/shard_map/ppermute | solution.py:175
  133.6 10.2 %copy-start.10 = (bf16[512,256]{1,0:T(8,128)(2,1)}, bf16[512,256]{1,0:T(8,128)(2,1)S(1)}, u32[]{:S(2)}) copy-start(bf16[512,256]{1,0:T(8,128)(2,1)S(1)} %collective-permute-done.11.refs_5_) | copy-start | bytes 786436
  133.6 10.2 %collective-permute-start.6 = (bf16[512,256]{1,0:T(8,128)(2,1)}, bf16[512,256]{1,0:T(8,128)(2,1)S(1)}, u32[]{:S(2)}, u32[]{:S(2)}) collective-permute-start(bf16[512,256]{1,0:T(8,128)(2,1)} %gate_up.2.refs_0_), channel_id=1, source_target_pairs={{0,64},{64,128},{128,192},{192,0},{1,65},{65,129},{129,193},{193,1... | collective-permute-start | bytes 786440 | tf_op jit(solution)/shard_map/ppermute | solution.py:175
  133.6 10.2 %copy-start.11 = (bf16[512,256]{1,0:T(8,128)(2,1)}, bf16[512,256]{1,0:T(8,128)(2,1)S(1)}, u32[]{:S(2)}) copy-start(bf16[512,256]{1,0:T(8,128)(2,1)S(1)} %collective-permute-done.12.refs_6_) | copy-start | bytes 786436
  150.3 12.5 %copy-start.16 = (bf16[16,8]{0,1:T(8,128)(2,1)S(1)}, bf16[16,8]{0,1:T(8,128)(2,1)}, u32[]{:S(2)}) copy-start(bf16[16,8]{0,1:T(8,128)(2,1)} %param.11) | copy-start | bytes 772
  150.3 60.4 %all-to-all-start.2 = ((bf16[256,2,2,896]{3,2,1,0:T(2,128)(2,1)}), bf16[256,2,2,896]{3,2,1,0:T(2,128)(2,1)S(1)}, u32[]{:S(2)}, u32[]{:S(2)}) async-start(bf16[256,2,2,896]{3,2,1,0:T(2,128)(2,1)} %down.1), calls=%async_computation.2 | async-start | bytes 3670016 | tf_op jit(solution)/shard_map/all_to_all | solution.py:242
  (10 other events, 29.8 us)

commit v4 on v3

--- a/solution.py
+++ b/solution.py
@@ -8,7 +8,7 @@
 from jax.sharding import PartitionSpec as P
 
 ADAPTER_RANK = 16
-VMEM_LIMIT = 57 * 1024 * 1024
+VMEM_LIMIT = 16 * 1024 * 1024
 
 
 def gate_up_kernel(parts, expert, chunks, *refs):
@@ -71,67 +71,108 @@
     )(*rows, gate_weight, up_weight, factor, *after)
 
 
-def down_kernel(groups, experts, me_ref, *refs):
-    hidden = [refs[e * groups : (e + 1) * groups] for e in range(experts)]
-    weight_ref = refs[experts * groups]
-    out_ref, x, weight_at, sems = refs[-4:]
-    count, units = hidden[0][0].shape
+def down_kernel(groups, expert, me_ref, *refs):
+    hidden, weight_ref = refs[:groups], refs[groups]
+    out_ref, x, weight_at, made, sems = refs[-5:]
+    count, units = hidden[0].shape
     block = count // groups
     me = me_ref[0]
     copies = []
-    for e in range(experts):
-        started = []
-        for s in range(groups):
-            owner = lax.rem(me + s, groups)
-            started.append(
+    for s in range(groups):
+        owner = lax.rem(me + s, groups)
+        copies.append(
+            pltpu.make_async_copy(
+                weight_ref.at[expert, pl.ds(pl.multiple_of(owner * units, units), units)],
+                weight_at.at[pl.ds(s * units, units)],
+                sems.at[s, groups],
+            )
+        )
+        for i in range(groups):
+            copies.append(
                 pltpu.make_async_copy(
-                    weight_ref.at[e, pl.ds(pl.multiple_of(owner * units, units), units)],
-                    weight_at.at[e, pl.ds(s * units, units)],
-                    sems.at[e, s, groups],
+                    hidden[s].at[pl.ds((i - s) % groups * block, block)],
+                    x.at[pl.ds(i * block, block), pl.ds(s * units, units)],
+                    sems.at[s, i],
                 )
             )
-            for i in range(groups):
-                started.append(
-                    pltpu.make_async_copy(
-                        hidden[e][s].at[pl.ds((i - s) % groups * block, block)],
-                        x.at[e, pl.ds(i * block, block), pl.ds(s * units, units)],
-                        sems.at[e, s, i],
-                    )
-                )
-        for copy in started:
-            copy.start()
-        copies.append(started)
-    for e in range(experts):
-        for copy in copies[e]:
-            copy.wait()
-        out = jnp.dot(x[e], weight_at[e], preferred_element_type=jnp.float32)
-        out = out.astype(out_ref.dtype)
-        senders = block // out_ref.shape[2]
-        for i in range(groups):
-            at = pl.ds(lax.rem(me + i, groups) * senders, senders)
-            rows = out[i * block : (i + 1) * block]
-            out_ref[at, e] = rows.reshape((senders,) + out_ref.shape[2:])
-
-
-def down(hidden, down_weight, me, capacity):
-    experts, groups = len(hidden), len(hidden[0])
-    count, units = hidden[0][0].shape
-    share = down_weight.shape[2]
+    for copy in copies:
+        copy.start()
+    for copy in copies:
+        copy.wait()
+    out = jnp.dot(x[...], weight_at[...], preferred_element_type=jnp.float32)
+    out = out.astype(made.dtype)
+    stored = []
+    for i in range(groups):
+        senders = block // made.shape[1]
+        made[i * senders : (i + 1) * senders] = out[i * block : (i + 1) * block].reshape(
+            (senders,) + made.shape[1:]
+        )
+        to = pl.ds(lax.rem(me + i, groups) * senders, senders)
+        copy = pltpu.make_async_copy(
+            made.at[pl.ds(i * senders, senders)], out_ref.at[to, expert], sems.at[groups, i]
+        )
+        copy.start()
+        stored.append(copy)
+    for copy in stored:
+        copy.wait()
+
+
+def down(hidden, down_weight, me, expert, capacity, outputs):
+    groups = len(hidden)
+    count, units = hidden[0].shape
+    experts, share = down_weight.shape[0], down_weight.shape[2]
     anywhere = pl.BlockSpec(memory_space=pl.ANY)
-    return pl.pallas_call(
-        functools.partial(down_kernel, groups, experts),
+    held = [] if outputs is None else [outputs]
+    return pl.pallas_call(
+        functools.partial(down_kernel, groups, expert),
         in_specs=[pl.BlockSpec(memory_space=pltpu.SMEM)]
-        + [anywhere] * (groups * experts + 1),
+        + [anywhere] * (groups + 1 + len(held)),
+        out_specs=anywhere,
         out_shape=jax.ShapeDtypeStruct((count // capacity, experts, capacity, share), jnp.bfloat16),
         scratch_shapes=[
-            pltpu.VMEM((experts, count, groups * units), jnp.bfloat16),
-            pltpu.VMEM((experts, groups * units, share), jnp.bfloat16),
-            pltpu.SemaphoreType.DMA((experts, groups, groups + 1)),
+            pltpu.VMEM((count, groups * units), jnp.bfloat16),
+            pltpu.VMEM((groups * units, share), jnp.bfloat16),
+            pltpu.VMEM((count // capacity, capacity, share), jnp.bfloat16),
+            pltpu.SemaphoreType.DMA((groups + 1, groups + 1)),
         ],
+        input_output_aliases={groups + 2: 0} if held else {},
         compiler_params=pltpu.CompilerParams(vmem_limit_bytes=VMEM_LIMIT),
         cost_estimate=pl.CostEstimate(flops=1000, bytes_accessed=1000, transcendentals=0),
         name="down",
-    )(me, *[h for of_expert in hidden for h in of_expert], down_weight)
+    )(me, *hidden, down_weight, *held)
+
+
+def combine_kernel(groups, combiner_ref, back_ref, mixed_ref, held, sems):
+    senders = held.shape[0] // groups
+    share = held.shape[3]
+    copies = []
+    for g in range(groups):
+        at = pl.ds(g * senders, senders)
+        copy = pltpu.make_async_copy(back_ref.at[at], held.at[at], sems.at[g])
+        copy.start()
+        copies.append(copy)
+    for g in range(groups):
+        copies[g].wait()
+        rows = held[g * senders : (g + 1) * senders]
+        rows = rows.reshape((-1,) + rows.shape[2:]).reshape(-1, share)
+        mixed_ref[:, g * share : (g + 1) * share] = jnp.dot(
+            combiner_ref[...], rows, preferred_element_type=jnp.float32
+        ).astype(mixed_ref.dtype)
+
+
+def combine(combiner, back, groups):
+    return pl.pallas_call(
+        functools.partial(combine_kernel, groups),
+        in_specs=[pl.BlockSpec(memory_space=pltpu.VMEM), pl.BlockSpec(memory_space=pl.ANY)],
+        out_shape=jax.ShapeDtypeStruct((combiner.shape[0], groups * back.shape[3]), jnp.bfloat16),
+        scratch_shapes=[
+            pltpu.VMEM(back.shape, jnp.bfloat16),
+            pltpu.SemaphoreType.DMA((groups,)),
+        ],
+        compiler_params=pltpu.CompilerParams(vmem_limit_bytes=VMEM_LIMIT),
+        cost_estimate=pl.CostEstimate(flops=1000, bytes_accessed=1000, transcendentals=0),
+        name="combine",
+    )(combiner, back)
 
 
 def relayout_kernel(x_ref, *refs):
@@ -228,24 +269,24 @@
         sent = lax.all_to_all(packed, "ep", split_axis=0, concat_axis=0, tiled=True)
         received.append(sent)
 
+    gate_weight, up_weight, down_weight = (
+        pltpu.with_memory_space_constraint(w, pltpu.HBM)
+        for w in (gate_weight, up_weight, down_weight)
+    )
     me = lax.axis_index("rep").astype(jnp.int32).reshape(1)
     half = slots // 2
-    hidden = []
+    back = None
     for j, sent in enumerate(received):
         mine = relayout(sent, (slots, width + adapters), [])
         before_me, after_me = from_further(mine, -1), from_further(mine, 1)
         across = [from_further(before_me[:half], -1), from_further(after_me[half:], 1)]
         every = [mine, after_me, *across, before_me]
         units = gate_up(every, gate_weight, up_weight, adapter_up_factor, j, [])
-        hidden.append([units] + [from_further(units, s) for s in range(1, groups)])
-    back = down(hidden, down_weight, me, capacity)
+        hidden = [units] + [from_further(units, s) for s in range(1, groups)]
+        back = down(hidden, down_weight, me, j, capacity, back)
     back = lax.all_to_all(back, ("rep", "ep"), split_axis=0, concat_axis=0, tiled=True)
-    back = back.reshape(groups, owners * local_count * capacity, share)
     combiner = jnp.stack([c.reshape(row_count, owners, capacity) for c in combiners], axis=2)
-    total = jnp.einsum(
-        "ri,gid->rgd", combiner.reshape(row_count, -1), back, preferred_element_type=f32
-    )
-    return total.astype(bf16).reshape(row_count, width)
+    return combine(combiner.reshape(row_count, -1), back, groups)
 
 
 def solution(mesh):

time: 216 us -> 209 us (0.968)
  starting transfers between devices: 48.7 us -> 54.2 us
  waiting for transfers between devices: 128 us -> 123 us
  local copies, waits for them, and re-layouts: 11.2 us -> 6.29 us
    ppermute x14, waiting for transfers between devices: 35.2 us -> 29.8 us  [from_further(): return lax.ppermute(x, 'rep', [(i, (i - by) % n) for i in range(n)])]
    pallas_call x1 -> x3, Pallas kernels: 5.9 us -> 10.2 us  [the longest x2 7.64 us: down(): pl.pallas_call(functools.partial(down_kernel, groups, expert), in_specs=[...]
    unnamed x35 -> x9, local copies, waits for them, and re-layouts: 4.55 us -> 0.86 us
    ppermute x14, starting transfers between devices: 16.8 us -> 20.3 us  [from_further(): return lax.ppermute(x, 'rep', [(i, (i - by) % n) for i in range(n)])]
    pallas_call x2, Pallas kernels: 4.51 us -> 1.24 us  [relayout(): pl.pallas_call(relayout_kernel, in_specs=[pl.BlockSpec(memory_space=pltpu...]
    reshape x2 -> x1, local copies, waits for them, and re-layouts: 2.34 us -> 0.06 us  [per_device(): return combine(combiner.reshape(row_count, -1), back, groups)]
  transfers between devices with their start and end apart: 17 -> 17, of which waited for: 10 -> 8; matrix products, arithmetic and copies ran while one was open for 2% -> 2% of each run, Pallas kernels for 7% -> 7%
where the time goes in v4:
time: 209 us
  waiting for transfers between devices  123 us (59%)
  starting transfers between devices  54.2 us (26%)
  Pallas kernels  20.6 us (10%)
  local copies, waits for them, and re-layouts  6.29 us (3%)
  matrix products  2.95 us (1%)
    all_to_all x1, waiting for transfers between devices, per_device(): lax.all_to_all(back, ('rep', 'ep'), split_axis=0, concat_axis=0, tiled=True)  47.2 us
    all_to_all x2, waiting for transfers between devices, per_device(): sent = lax.all_to_all(packed, 'ep', split_axis=0, concat_axis=0, tiled=True)  46.3 us
    ppermute x14, waiting for transfers between devices, from_further(): return lax.ppermute(x, 'rep', [(i, (i - by) % n) for i in range(n)])  29.8 us
    ppermute x14, starting transfers between devices, from_further(): return lax.ppermute(x, 'rep', [(i, (i - by) % n) for i in range(n)])  20.3 us
    all_to_all x2, starting transfers between devices, per_device(): sent = lax.all_to_all(packed, 'ep', split_axis=0, concat_axis=0, tiled=True)  19.4 us
    all_to_all x1, starting transfers between devices, per_device(): lax.all_to_all(back, ('rep', 'ep'), split_axis=0, concat_axis=0, tiled=True)  14.4 us
    pallas_call x2, Pallas kernels, gate_up(): pl.pallas_call(functools.partial(gate_up_kernel, parts, expert, chunks),...  9.16 us
    pallas_call x2, Pallas kernels, down(): pl.pallas_call(functools.partial(down_kernel, groups, expert), in_specs=[...  7.64 us
  transfers between devices with their start and end apart: 17, of which 8 were waited for; matrix products, arithmetic and copies ran while one was open for 2% of the time, Pallas kernels for 7%

profile of v4, /device:TPU:1, one launch (start us, length us, event | category | flops | bytes accessed | tf_op | source)
XLA Modules:
  0.0 208.6 jit_solution(6330435805519862681)
XLA Ops:
  2.8 1.4 convolution_convert_fusion
  4.2 1.4 reshape.60
  5.5 13.0 %all-to-all-start.1 = ((bf16[64,2,3712]{2,1,0:T(2,128)(2,1)}), bf16[64,2,3712]{2,1,0:T(2,128)(2,1)S(1)}, u32[]{:S(2)}, u32[]{:S(2)}) async-start(bf16[64,2,3712]{2,1,0:T(2,128)(2,1)} %reshape.60), calls=%async_computation.1 | async-start | bytes 1900544 | tf_op jit(solution)/shard_map/all_to_all | solution.py:269
  20.3 24.2 %all-to-all-done.1.x_ref = bf16[64,2,3712]{2,1,0:T(2,128)(2,1)S(1)} async-done(((bf16[64,2,3712]{2,1,0:T(2,128)(2,1)}), bf16[64,2,3712]{2,1,0:T(2,128)(2,1)S(1)}, u32[]{:S(2)}, u32[]{:S(2)}) %all-to-all-start.1) | async-done | bytes 950304 | tf_op jit(solution)/shard_map/all_to_all | solution.py:269
  44.5 6.5 %all-to-all-start = ((bf16[64,2,3712]{2,1,0:T(2,128)(2,1)}), bf16[64,2,3712]{2,1,0:T(2,128)(2,1)S(1)}, u32[]{:S(2)}, u32[]{:S(2)}) async-start(bf16[64,2,3712]{2,1,0:T(2,128)(2,1)} %reshape.59), calls=%async_computation | async-start | bytes 1900544 | tf_op jit(solution)/shard_map/all_to_all | solution.py:269
  53.4 1.4 collective-permute-start.7
  54.8 22.1 %all-to-all-done.x_ref = bf16[64,2,3712]{2,1,0:T(2,128)(2,1)S(1)} async-done(((bf16[64,2,3712]{2,1,0:T(2,128)(2,1)}), bf16[64,2,3712]{2,1,0:T(2,128)(2,1)S(1)}, u32[]{:S(2)}, u32[]{:S(2)}) %all-to-all-start) | async-done | bytes 950304 | tf_op jit(solution)/shard_map/all_to_all | solution.py:269
  77.1 1.4 collective-permute-start.1
  78.4 1.5 collective-permute-start
  82.2 2.7 %collective-permute-start.10 = (bf16[64,3712]{1,0:T(8,128)(2,1)S(1)}, bf16[64,3712]{1,0:T(8,128)(2,1)S(1)}, u32[]{:S(2)}, u32[]{:S(2)}) collective-permute-start(bf16[64,3712]{1,0:T(8,128)(2,1)S(1)} %slice.19), channel_id=1, source_target_pairs={{0,192},{64,0},{128,64},{192,128},{1,193},{65,1},{129,65},{193,129... | collective-permute-start | bytes 1425416 | tf_op jit(solution)/shard_map/ppermute | solution.py:216
  84.9 14.8 %collective-permute-done.1.refs_4_ = bf16[128,3712]{1,0:T(8,128)(2,1)S(1)} collective-permute-done((bf16[128,3712]{1,0:T(8,128)(2,1)S(1)}, bf16[128,3712]{1,0:T(8,128)(2,1)S(1)}, u32[]{:S(2)}, u32[]{:S(2)}) %collective-permute-start.1) | collective-permute-done | bytes 950304 | tf_op jit(solution)/shard_map/ppermute | solution.py:216
  99.9 2.9 %collective-permute-start.3 = (bf16[64,3712]{1,0:T(8,128)(2,1)S(1)}, bf16[64,3712]{1,0:T(8,128)(2,1)S(1)}, u32[]{:S(2)}, u32[]{:S(2)}) collective-permute-start(bf16[64,3712]{1,0:T(8,128)(2,1)S(1)} %slice.17), channel_id=1, source_target_pairs={{0,192},{64,0},{128,64},{192,128},{1,193},{65,1},{129,65},{193,129... | collective-permute-start | bytes 1425416 | tf_op jit(solution)/shard_map/ppermute | solution.py:216
  102.9 7.1 %collective-permute-done.9.refs_2_ = bf16[64,3712]{1,0:T(8,128)(2,1)S(1)} collective-permute-done((bf16[64,3712]{1,0:T(8,128)(2,1)S(1)}, bf16[64,3712]{1,0:T(8,128)(2,1)S(1)}, u32[]{:S(2)}, u32[]{:S(2)}) %collective-permute-start.9) | collective-permute-done | bytes 475168 | tf_op jit(solution)/shard_map/ppermute | solution.py:216
  110.0 4.7 %gate_up.3.refs_0_ = bf16[512,256]{1,0:T(8,128)(2,1)S(1)} custom-call(bf16[128,3712]{1,0:T(8,128)(2,1)} %relayout.3.refs_0_, bf16[128,3712]{1,0:T(8,128)(2,1)} %collective-permute-done.7.refs_1_, bf16[64,3712]{1,0:T(8,128)(2,1)S(1)} %collective-permute-done.9.refs_2_, bf16[64,3712]{1,0:T(8,128)(2,1)S(1)} %collective-permute-done.10.refs_3_, ...), custom_call_target="tpu_custom_call" | custom-call | flops 1000 | bytes 1000 | tf_op jit(solution)/shard_map/gate_up/pallas_call | solution.py:57
  115.7 2.8 %collective-permute-start.12 = (bf16[512,256]{1,0:T(8,128)(2,1)S(1)}, bf16[512,256]{1,0:T(8,128)(2,1)S(1)}, u32[]{:S(2)}, u32[]{:S(2)}) collective-permute-start(bf16[512,256]{1,0:T(8,128)(2,1)S(1)} %gate_up.3.refs_0_), channel_id=1, source_target_pairs={{0,128},{64,192},{128,0},{192,64},{1,129},{65,193},{129,1},{193,65... | collective-permute-start | bytes 786440 | tf_op jit(solution)/shard_map/ppermute | solution.py:216
  120.1 4.4 %gate_up.2.refs_0_ = bf16[512,256]{1,0:T(8,128)(2,1)S(1)} custom-call(bf16[128,3712]{1,0:T(8,128)(2,1)S(1)} %relayout.2.refs_0_, bf16[128,3712]{1,0:T(8,128)(2,1)S(1)} %collective-permute-done.refs_1_, bf16[64,3712]{1,0:T(8,128)(2,1)S(1)} %collective-permute-done.2.refs_2_, bf16[64,3712]{1,0:T(8,128)(2,1)S(1)} %collective-permute-done.3.refs_3_, ...), custom_call_target="tpu_custom_call" | custom-call | flops 1000 | bytes 1000 | tf_op jit(solution)/shard_map/gate_up/pallas_call | solution.py:57
  125.6 3.3 %collective-permute-start.5 = (bf16[512,256]{1,0:T(8,128)(2,1)S(1)}, bf16[512,256]{1,0:T(8,128)(2,1)S(1)}, u32[]{:S(2)}, u32[]{:S(2)}) collective-permute-start(bf16[512,256]{1,0:T(8,128)(2,1)S(1)} %gate_up.2.refs_0_), channel_id=1, source_target_pairs={{0,128},{64,192},{128,0},{192,64},{1,129},{65,193},{129,1},{193,65... | collective-permute-start | bytes 786440 | tf_op jit(solution)/shard_map/ppermute | solution.py:216
  129.0 3.5 %collective-permute-done.12.refs_2_ = bf16[512,256]{1,0:T(8,128)(2,1)S(1)} collective-permute-done((bf16[512,256]{1,0:T(8,128)(2,1)S(1)}, bf16[512,256]{1,0:T(8,128)(2,1)S(1)}, u32[]{:S(2)}, u32[]{:S(2)}) %collective-permute-start.12) | collective-permute-done | bytes 262176 | tf_op jit(solution)/shard_map/ppermute | solution.py:216
  132.5 3.8 %down.2.refs_5_ = bf16[256,2,2,896]{3,2,1,0:T(2,128)(2,1)} custom-call(s32[1]{0:T(128)} %bitcast.3.me_ref, bf16[512,256]{1,0:T(8,128)(2,1)S(1)} %gate_up.3.refs_0_, bf16[512,256]{1,0:T(8,128)(2,1)S(1)} %collective-permute-done.11.refs_1_, bf16[512,256]{1,0:T(8,128)(2,1)S(1)} %collective-permute-done.12.refs_2_, ...), custom_call_target="tpu_custom_call" | custom-call | flops 1000 | bytes 1000 | tf_op jit(solution)/shard_map/down/pallas_call | solution.py:126
  136.4 3.3 %collective-permute-done.5.refs_2_ = bf16[512,256]{1,0:T(8,128)(2,1)S(1)} collective-permute-done((bf16[512,256]{1,0:T(8,128)(2,1)S(1)}, bf16[512,256]{1,0:T(8,128)(2,1)S(1)}, u32[]{:S(2)}, u32[]{:S(2)}) %collective-permute-start.5) | collective-permute-done | bytes 262176 | tf_op jit(solution)/shard_map/ppermute | solution.py:216
  139.7 3.8 %down.3 = bf16[256,2,2,896]{3,2,1,0:T(2,128)(2,1)} custom-call(s32[1]{0:T(128)} %bitcast.3.me_ref, bf16[512,256]{1,0:T(8,128)(2,1)S(1)} %gate_up.2.refs_0_, bf16[512,256]{1,0:T(8,128)(2,1)S(1)} %collective-permute-done.4.refs_1_, bf16[512,256]{1,0:T(8,128)(2,1)S(1)} %collective-permute-done.5.refs_2_, ...), custom_call_target="tpu_custom_call", output_to_operand_aliasing={{}: (6, {})} | custom-call | flops 1000 | bytes 1000 | tf_op jit(solution)/shard_map/down/pallas_call | solution.py:126
  143.5 14.4 %all-to-all-start.2 = ((bf16[256,2,2,896]{3,2,1,0:T(2,128)(2,1)}), bf16[256,2,2,896]{3,2,1,0:T(2,128)(2,1)S(1)}, u32[]{:S(2)}, u32[]{:S(2)}) async-start(bf16[256,2,2,896]{3,2,1,0:T(2,128)(2,1)} %down.3), calls=%async_computation.2 | async-start | bytes 3670016 | tf_op jit(solution)/shard_map/all_to_all | solution.py:287
  158.7 47.2 %all-to-all-done.2.back_ref = bf16[256,2,2,896]{3,2,1,0:T(2,128)(2,1)S(1)} async-done(((bf16[256,2,2,896]{3,2,1,0:T(2,128)(2,1)}), bf16[256,2,2,896]{3,2,1,0:T(2,128)(2,1)S(1)}, u32[]{:S(2)}, u32[]{:S(2)}) %all-to-all-start.2) | async-done | bytes 1835040 | tf_op jit(solution)/shard_map/all_to_all | solution.py:287
  205.9 2.5 %combine.1 = bf16[16,3584]{1,0:T(8,128)(2,1)} custom-call(bf16[16,256]{1,0:T(8,128)(2,1)S(1)} %copy.44.combiner_ref, bf16[256,2,2,896]{3,2,1,0:T(2,128)(2,1)S(1)} %all-to-all-done.2.back_ref), custom_call_target="tpu_custom_call" | custom-call | flops 1000 | bytes 1000 | tf_op jit(solution)/shard_map/combine/pallas_call | solution.py:164
  (51 shorter events, 14.0 us)
Async XLA Ops:
  0.0 1.6 copy-start
  4.2 14.4 %copy-start.2 = (bf16[16,3584]{1,0:T(8,128)(2,1)S(1)}, bf16[16,3584]{1,0:T(8,128)(2,1)}, u32[]{:S(2)}) copy-start(bf16[16,3584]{1,0:T(8,128)(2,1)} %param.9) | copy-start | bytes 344068
  5.5 39.0 %all-to-all-start.1 = ((bf16[64,2,3712]{2,1,0:T(2,128)(2,1)}), bf16[64,2,3712]{2,1,0:T(2,128)(2,1)S(1)}, u32[]{:S(2)}, u32[]{:S(2)}) async-start(bf16[64,2,3712]{2,1,0:T(2,128)(2,1)} %reshape.60), calls=%async_computation.1 | async-start | bytes 1900544 | tf_op jit(solution)/shard_map/all_to_all | solution.py:269
  44.5 32.4 %all-to-all-start = ((bf16[64,2,3712]{2,1,0:T(2,128)(2,1)}), bf16[64,2,3712]{2,1,0:T(2,128)(2,1)S(1)}, u32[]{:S(2)}, u32[]{:S(2)}) async-start(bf16[64,2,3712]{2,1,0:T(2,128)(2,1)} %reshape.59), calls=%async_computation | async-start | bytes 1900544 | tf_op jit(solution)/shard_map/all_to_all | solution.py:269
  52.1 27.9 %collective-permute-start.8 = (bf16[128,3712]{1,0:T(8,128)(2,1)}, bf16[128,3712]{1,0:T(8,128)(2,1)}, u32[]{:S(2)}, u32[]{:S(2)}) collective-permute-start(bf16[128,3712]{1,0:T(8,128)(2,1)} %relayout.3.refs_0_), channel_id=1, source_target_pairs={{0,64},{64,128},{128,192},{192,0},{1,65},{65,129},{129,193},{193,1... | collective-permute-start | bytes 2850824 | tf_op jit(solution)/shard_map/ppermute | solution.py:216
  53.4 27.8 %collective-permute-start.7 = (bf16[128,3712]{1,0:T(8,128)(2,1)}, bf16[128,3712]{1,0:T(8,128)(2,1)}, u32[]{:S(2)}, u32[]{:S(2)}) collective-permute-start(bf16[128,3712]{1,0:T(8,128)(2,1)} %relayout.3.refs_0_), channel_id=1, source_target_pairs={{0,192},{64,0},{128,64},{192,128},{1,193},{65,1},{129,65},{193,129... | collective-permute-start | bytes 2850824 | tf_op jit(solution)/shard_map/ppermute | solution.py:216
  77.1 32.9 %copy-start.1 = (bf16[128,256]{1,0:T(8,128)(2,1)S(1)}, bf16[128,256]{1,0:T(8,128)(2,1)}, u32[]{:S(2)}) copy-start(bf16[128,256]{1,0:T(8,128)(2,1)} %refs_7_.3) | copy-start | bytes 196612
  77.1 22.7 %collective-permute-start.1 = (bf16[128,3712]{1,0:T(8,128)(2,1)S(1)}, bf16[128,3712]{1,0:T(8,128)(2,1)S(1)}, u32[]{:S(2)}, u32[]{:S(2)}) collective-permute-start(bf16[128,3712]{1,0:T(8,128)(2,1)S(1)} %relayout.2.refs_0_), channel_id=1, source_target_pairs={{0,64},{64,128},{128,192},{192,0},{1,65},{65,129},{129,193},{193,1... | collective-permute-start | bytes 2850824 | tf_op jit(solution)/shard_map/ppermute | solution.py:216
  78.4 21.5 %collective-permute-start = (bf16[128,3712]{1,0:T(8,128)(2,1)S(1)}, bf16[128,3712]{1,0:T(8,128)(2,1)S(1)}, u32[]{:S(2)}, u32[]{:S(2)}) collective-permute-start(bf16[128,3712]{1,0:T(8,128)(2,1)S(1)} %relayout.2.refs_0_), channel_id=1, source_target_pairs={{0,192},{64,0},{128,64},{192,128},{1,193},{65,1},{129,65},{193,129... | collective-permute-start | bytes 2850824 | tf_op jit(solution)/shard_map/ppermute | solution.py:216
  81.0 28.9 %collective-permute-start.9 = (bf16[64,3712]{1,0:T(8,128)(2,1)S(1)}, bf16[64,3712]{1,0:T(8,128)(2,1)S(1)}, u32[]{:S(2)}, u32[]{:S(2)}) collective-permute-start(bf16[64,3712]{1,0:T(8,128)(2,1)S(1)} %slice.18), channel_id=1, source_target_pairs={{0,64},{64,128},{128,192},{192,0},{1,65},{65,129},{129,193},{193,1... | collective-permute-start | bytes 1425416 | tf_op jit(solution)/shard_map/ppermute | solution.py:216
  82.2 27.8 %collective-permute-start.10 = (bf16[64,3712]{1,0:T(8,128)(2,1)S(1)}, bf16[64,3712]{1,0:T(8,128)(2,1)S(1)}, u32[]{:S(2)}, u32[]{:S(2)}) collective-permute-start(bf16[64,3712]{1,0:T(8,128)(2,1)S(1)} %slice.19), channel_id=1, source_target_pairs={{0,192},{64,0},{128,64},{192,128},{1,193},{65,1},{129,65},{193,129... | collective-permute-start | bytes 1425416 | tf_op jit(solution)/shard_map/ppermute | solution.py:216
  99.8 20.3 %collective-permute-start.2 = (bf16[64,3712]{1,0:T(8,128)(2,1)S(1)}, bf16[64,3712]{1,0:T(8,128)(2,1)S(1)}, u32[]{:S(2)}, u32[]{:S(2)}) collective-permute-start(bf16[64,3712]{1,0:T(8,128)(2,1)S(1)} %slice.16), channel_id=1, source_target_pairs={{0,64},{64,128},{128,192},{192,0},{1,65},{65,129},{129,193},{193,1... | collective-permute-start | bytes 1425416 | tf_op jit(solution)/shard_map/ppermute | solution.py:216
  99.9 20.2 %collective-permute-start.3 = (bf16[64,3712]{1,0:T(8,128)(2,1)S(1)}, bf16[64,3712]{1,0:T(8,128)(2,1)S(1)}, u32[]{:S(2)}, u32[]{:S(2)}) collective-permute-start(bf16[64,3712]{1,0:T(8,128)(2,1)S(1)} %slice.17), channel_id=1, source_target_pairs={{0,192},{64,0},{128,64},{192,128},{1,193},{65,1},{129,65},{193,129... | collective-permute-start | bytes 1425416 | tf_op jit(solution)/shard_map/ppermute | solution.py:216
  114.7 14.2 %collective-permute-start.13 = (bf16[512,256]{1,0:T(8,128)(2,1)S(1)}, bf16[512,256]{1,0:T(8,128)(2,1)S(1)}, u32[]{:S(2)}, u32[]{:S(2)}) collective-permute-start(bf16[512,256]{1,0:T(8,128)(2,1)S(1)} %gate_up.3.refs_0_), channel_id=1, source_target_pairs={{0,64},{64,128},{128,192},{192,0},{1,65},{65,129},{129,193},{193,1... | collective-permute-start | bytes 786440 | tf_op jit(solution)/shard_map/ppermute | solution.py:216
  115.7 16.8 %collective-permute-start.12 = (bf16[512,256]{1,0:T(8,128)(2,1)S(1)}, bf16[512,256]{1,0:T(8,128)(2,1)S(1)}, u32[]{:S(2)}, u32[]{:S(2)}) collective-permute-start(bf16[512,256]{1,0:T(8,128)(2,1)S(1)} %gate_up.3.refs_0_), channel_id=1, source_target_pairs={{0,128},{64,192},{128,0},{192,64},{1,129},{65,193},{129,1},{193,65... | collective-permute-start | bytes 786440 | tf_op jit(solution)/shard_map/ppermute | solution.py:216
  118.5 14.0 %collective-permute-start.11 = (bf16[512,256]{1,0:T(8,128)(2,1)S(1)}, bf16[512,256]{1,0:T(8,128)(2,1)S(1)}, u32[]{:S(2)}, u32[]{:S(2)}) collective-permute-start(bf16[512,256]{1,0:T(8,128)(2,1)S(1)} %gate_up.3.refs_0_), channel_id=1, source_target_pairs={{0,192},{64,0},{128,64},{192,128},{1,193},{65,1},{129,65},{193,129... | collective-permute-start | bytes 786440 | tf_op jit(solution)/shard_map/ppermute | solution.py:216
  124.6 11.8 %collective-permute-start.6 = (bf16[512,256]{1,0:T(8,128)(2,1)S(1)}, bf16[512,256]{1,0:T(8,128)(2,1)S(1)}, u32[]{:S(2)}, u32[]{:S(2)}) collective-permute-start(bf16[512,256]{1,0:T(8,128)(2,1)S(1)} %gate_up.2.refs_0_), channel_id=1, source_target_pairs={{0,64},{64,128},{128,192},{192,0},{1,65},{65,129},{129,193},{193,1... | collective-permute-start | bytes 786440 | tf_op jit(solution)/shard_map/ppermute | solution.py:216
  125.6 14.1 %collective-permute-start.5 = (bf16[512,256]{1,0:T(8,128)(2,1)S(1)}, bf16[512,256]{1,0:T(8,128)(2,1)S(1)}, u32[]{:S(2)}, u32[]{:S(2)}) collective-permute-start(bf16[512,256]{1,0:T(8,128)(2,1)S(1)} %gate_up.2.refs_0_), channel_id=1, source_target_pairs={{0,128},{64,192},{128,0},{192,64},{1,129},{65,193},{129,1},{193,65... | collective-permute-start | bytes 786440 | tf_op jit(solution)/shard_map/ppermute | solution.py:216
  128.9 10.8 %collective-permute-start.4 = (bf16[512,256]{1,0:T(8,128)(2,1)S(1)}, bf16[512,256]{1,0:T(8,128)(2,1)S(1)}, u32[]{:S(2)}, u32[]{:S(2)}) collective-permute-start(bf16[512,256]{1,0:T(8,128)(2,1)S(1)} %gate_up.2.refs_0_), channel_id=1, source_target_pairs={{0,192},{64,0},{128,64},{192,128},{1,193},{65,1},{129,65},{193,129... | collective-permute-start | bytes 786440 | tf_op jit(solution)/shard_map/ppermute | solution.py:216
  143.5 14.4 %copy-start.3 = (bf16[16,8]{0,1:T(8,128)(2,1)S(1)}, bf16[16,8]{0,1:T(8,128)(2,1)}, u32[]{:S(2)}) copy-start(bf16[16,8]{0,1:T(8,128)(2,1)} %param.11) | copy-start | bytes 772
  143.5 62.3 %all-to-all-start.2 = ((bf16[256,2,2,896]{3,2,1,0:T(2,128)(2,1)}), bf16[256,2,2,896]{3,2,1,0:T(2,128)(2,1)S(1)}, u32[]{:S(2)}, u32[]{:S(2)}) async-start(bf16[256,2,2,896]{3,2,1,0:T(2,128)(2,1)} %down.3), calls=%async_computation.2 | async-start | bytes 3670016 | tf_op jit(solution)/shard_map/all_to_all | solution.py:287

commit v5 on v4

v5 whole, which is shorter than its diff:
```python
import functools

import jax
import jax.numpy as jnp
from jax import lax
from jax.experimental import pallas as pl
from jax.experimental.pallas import tpu as pltpu
from jax.sharding import PartitionSpec as P

ADAPTER_RANK = 16
VMEM_LIMIT = 16 * 1024 * 1024


def in_vmem(x):
    return pltpu.with_memory_space_constraint(x, pltpu.VMEM)


def in_hbm(x):
    return pltpu.with_memory_space_constraint(x, pltpu.HBM)


def gate_up_kernel(parts, expert, chunks, *refs):
    rows = refs[:parts]
    gate_ref, up_ref, factor_ref, hidden_ref = refs[parts:]
    width = gate_ref.shape[1]
    depth = width // chunks
    low = jnp.concatenate([r[:, width:] for r in rows], axis=0)
    up = jnp.dot(low, factor_ref[...], preferred_element_type=jnp.float32)
    gate = 0.0
    for c in range(chunks):
        here = slice(c * depth, (c + 1) * depth)
        x = jnp.concatenate([r[:, here] for r in rows], axis=0)
        gate += jnp.dot(x, gate_ref[expert, here], preferred_element_type=jnp.float32)
        up += jnp.dot(x, up_ref[expert, here], preferred_element_type=jnp.float32)
    hidden_ref[...] = (gate / (1.0 + jnp.exp(-gate)) * up).astype(hidden_ref.dtype)


def gate_up(rows, gate_weight, up_weight, factor, expert, chunks=7):
    units = gate_weight.shape[2]
    parts = len(rows)
    count = sum(r.shape[0] for r in rows)
    vmem = pl.BlockSpec(memory_space=pltpu.VMEM)
    return pl.pallas_call(
        functools.partial(gate_up_kernel, parts, expert, chunks),
        in_specs=[vmem] * (parts + 3),
        out_specs=vmem,
        out_shape=jax.ShapeDtypeStruct((count, units), jnp.bfloat16),
        compiler_params=pltpu.CompilerParams(vmem_limit_bytes=VMEM_LIMIT),
        cost_estimate=pl.CostEstimate(flops=1000, bytes_accessed=1000, transcendentals=0),
        name="gate_up",
    )(*(in_vmem(x) for x in (*rows, gate_weight, up_weight)), factor)


def down_kernel(groups, expert, me_ref, *refs):
    hidden, weight_ref = refs[:groups], refs[groups]
    out_ref, made, sems = refs[-3:]
    count, units = hidden[0].shape
    block = count // groups
    me = me_ref[0]
    weights, columns = [], []
    for s in range(groups):
        at = pl.multiple_of(lax.rem(me + s, groups) * units, units)
        weights.append(weight_ref[expert, pl.ds(at, units)])
        turned = [(i - s) % groups * block for i in range(groups)]
        columns.append(jnp.concatenate([hidden[s][t : t + block] for t in turned], axis=0))
    out = jnp.dot(
        jnp.concatenate(columns, axis=1),
        jnp.concatenate(weights, axis=0),
        preferred_element_type=jnp.float32,
    )
    out = out.astype(made.dtype)
    stored = []
    for i in range(groups):
        senders = block // made.shape[1]
        made[i * senders : (i + 1) * senders] = out[i * block : (i + 1) * block].reshape(
            (senders,) + made.shape[1:]
        )
        to = pl.ds(lax.rem(me + i, groups) * senders, senders)
        copy = pltpu.make_async_copy(
            made.at[pl.ds(i * senders, senders)], out_ref.at[to, expert], sems.at[i]
        )
        copy.start()
        stored.append(copy)
    for copy in stored:
        copy.wait()


def down(hidden, down_weight, me, expert, capacity, outputs):
    groups = len(hidden)
    count, units = hidden[0].shape
    experts, share = down_weight.shape[0], down_weight.shape[2]
    anywhere = pl.BlockSpec(memory_space=pl.ANY)
    vmem = pl.BlockSpec(memory_space=pltpu.VMEM)
    held = [] if outputs is None else [outputs]
    return pl.pallas_call(
        functools.partial(down_kernel, groups, expert),
        in_specs=[pl.BlockSpec(memory_space=pltpu.SMEM)]
        + [vmem] * (groups + 1)
        + [anywhere] * len(held),
        out_specs=anywhere,
        out_shape=jax.ShapeDtypeStruct((count // capacity, experts, capacity, share), jnp.bfloat16),
        scratch_shapes=[
            pltpu.VMEM((count // capacity, capacity, share), jnp.bfloat16),
            pltpu.SemaphoreType.DMA((groups,)),
        ],
        input_output_aliases={groups + 2: 0} if held else {},
        compiler_params=pltpu.CompilerParams(vmem_limit_bytes=VMEM_LIMIT),
        cost_estimate=pl.CostEstimate(flops=1000, bytes_accessed=1000, transcendentals=0),
        name="down",
    )(me, *(in_vmem(x) for x in (*hidden, down_weight)), *held)


def combine_kernel(groups, combiner_ref, back_ref, mixed_ref):
    senders = back_ref.shape[0] // groups
    share = back_ref.shape[3]
    for g in range(groups):
        rows = back_ref[g * senders : (g + 1) * senders]
        rows = rows.reshape((-1,) + rows.shape[2:]).reshape(-1, share)
        mixed_ref[:, g * share : (g + 1) * share] = jnp.dot(
            combiner_ref[...], rows, preferred_element_type=jnp.float32
        ).astype(mixed_ref.dtype)


def combine(combiner, back, groups):
    vmem = pl.BlockSpec(memory_space=pltpu.VMEM)
    return pl.pallas_call(
        functools.partial(combine_kernel, groups),
        in_specs=[vmem, vmem],
        out_shape=jax.ShapeDtypeStruct((combiner.shape[0], groups * back.shape[3]), jnp.bfloat16),
        compiler_params=pltpu.CompilerParams(vmem_limit_bytes=VMEM_LIMIT),
        cost_estimate=pl.CostEstimate(flops=1000, bytes_accessed=1000, transcendentals=0),
        name="combine",
    )(combiner, in_vmem(back))


def relayout_kernel(x_ref, *refs):
    refs[-1][...] = x_ref[...].reshape(refs[-1].shape)


def relayout(x, shape, after):
    return pl.pallas_call(
        relayout_kernel,
        in_specs=[pl.BlockSpec(memory_space=pltpu.VMEM)]
        + [pl.BlockSpec(memory_space=pl.ANY)] * len(after),
        out_shape=jax.ShapeDtypeStruct(shape, x.dtype),
        compiler_params=pltpu.CompilerParams(vmem_limit_bytes=VMEM_LIMIT),
        cost_estimate=pl.CostEstimate(flops=1000, bytes_accessed=1000, transcendentals=0),
        name="relayout",
    )(x, *after)


def halves_kernel(half, before_ref, after_ref, *refs):
    top_ref, bottom_ref = refs[-2:]
    top_ref[...] = before_ref[:half]
    bottom_ref[...] = after_ref[half:]


def halves(before_me, after_me, after):
    count, width = before_me.shape
    half = count // 2
    vmem = pl.BlockSpec(memory_space=pltpu.VMEM)
    return pl.pallas_call(
        functools.partial(halves_kernel, half),
        in_specs=[vmem, vmem] + [pl.BlockSpec(memory_space=pl.ANY)] * len(after),
        out_shape=[jax.ShapeDtypeStruct((half, width), before_me.dtype)] * 2,
        compiler_params=pltpu.CompilerParams(vmem_limit_bytes=VMEM_LIMIT),
        cost_estimate=pl.CostEstimate(flops=1000, bytes_accessed=1000, transcendentals=0),
        name="halves",
    )(before_me, after_me, *after)


def pack_kernel(routing_ref, tokens_ref, down_ref, mask_ref, out_ref):
    tokens = tokens_ref[...]
    low = jnp.dot(tokens, down_ref[...], preferred_element_type=jnp.float32) * mask_ref[...]
    width = tokens.shape[1]
    share = width // 4
    for c in range(4):
        here = slice(c * share, (c + 1) * share)
        picked = jnp.dot(routing_ref[...], tokens[:, here], preferred_element_type=jnp.float32)
        out_ref[:, :, here] = picked.astype(out_ref.dtype).reshape(out_ref.shape[:2] + (share,))
    picked = jnp.dot(
        routing_ref[...], low.astype(out_ref.dtype), preferred_element_type=jnp.float32
    )
    out_ref[:, :, width:] = picked.astype(out_ref.dtype).reshape(
        out_ref.shape[:2] + (low.shape[1],)
    )


def pack(routing, tokens, adapter_down_factor, mask, owners):
    slots, adapters = routing.shape[0], mask.shape[1]
    vmem = pl.BlockSpec(memory_space=pltpu.VMEM)
    return pl.pallas_call(
        pack_kernel,
        in_specs=[vmem] * 4,
        out_shape=jax.ShapeDtypeStruct(
            (owners, slots // owners, tokens.shape[1] + adapters), jnp.bfloat16
        ),
        compiler_params=pltpu.CompilerParams(vmem_limit_bytes=VMEM_LIMIT),
        cost_estimate=pl.CostEstimate(flops=1000, bytes_accessed=1000, transcendentals=0),
        name="pack",
    )(routing, in_hbm(tokens), in_hbm(adapter_down_factor), mask)


def from_further(x, by):
    n = lax.axis_size("rep")
    return lax.ppermute(x, "rep", [(i, (i - by) % n) for i in range(n)])


def per_device(
    tokens,
    chosen_expert_index,
    expert_mixing_weight,
    row_adapter_index,
    gate_weight,
    up_weight,
    down_weight,
    adapter_down_factor,
    adapter_up_factor,
):
    row_count, width = tokens.shape
    owners = lax.axis_size("ep")
    groups = lax.axis_size("rep")
    local_count = gate_weight.shape[0]
    experts = local_count * owners
    capacity = 2
    share = down_weight.shape[2]
    f32 = jnp.float32
    bf16 = jnp.bfloat16

    flat_ids = chosen_expert_index.reshape(-1)
    one_hot = (flat_ids[:, None] == lax.iota(jnp.int32, experts)[None, :]).astype(jnp.int32)
    before = jnp.cumsum(one_hot, axis=0) - one_hot
    position = jnp.sum(before * one_hot, axis=1).reshape(chosen_expert_index.shape)
    local = chosen_expert_index % local_count
    owner = chosen_expert_index // local_count

    adapters = adapter_down_factor.shape[1]
    lane_adapter = lax.iota(jnp.int32, adapters) // ADAPTER_RANK
    adapter_mask = (row_adapter_index[:, None] == lane_adapter[None, :]).astype(f32)
    slots = owners * capacity
    slot = owner * capacity + position
    mixing = expert_mixing_weight.astype(f32)
    received, combiners = [], []
    for j in range(local_count):
        matches = (slot[:, :, None] == lax.iota(jnp.int32, slots)[None, None, :]) & (
            local == j
        )[:, :, None]
        routing = (
            (slot[None, :, :] == lax.iota(jnp.int32, slots)[:, None, None])
            & (local == j)[None, :, :]
        )
        routing = jnp.any(routing, axis=2).astype(bf16)
        combiners.append(
            jnp.sum(jnp.where(matches, mixing[:, :, None], f32(0.0)), axis=1).astype(bf16)
        )
        packed = pack(
            routing, tokens, adapter_down_factor, adapter_mask, owners
        )
        sent = lax.all_to_all(packed, "ep", split_axis=0, concat_axis=0, tiled=True)
        received.append(sent)

    me = lax.axis_index("rep").astype(jnp.int32).reshape(1)
    half = slots // 2
    back = None
    for j, sent in enumerate(received):
        mine = relayout(sent, (slots, width + adapters), [])
        before_me, after_me = from_further(mine, -1), from_further(mine, 1)
        across = [from_further(before_me[:half], -1), from_further(after_me[half:], 1)]
        every = [mine, after_me, *across, before_me]
        units = gate_up(every, gate_weight, up_weight, adapter_up_factor, j)
        hidden = [units] + [from_further(units, s) for s in range(1, groups)]
        back = down(hidden, down_weight, me, j, capacity, back)
    back = lax.all_to_all(back, ("rep", "ep"), split_axis=0, concat_axis=0, tiled=True)
    combiner = jnp.stack([c.reshape(row_count, owners, capacity) for c in combiners], axis=2)
    return combine(combiner.reshape(row_count, -1), back, groups)


def solution(mesh):
    placed = (
        P(("rep", "ep"), None),
        P(("rep", "ep"), None),
        P(("rep", "ep"), None),
        P(("rep", "ep")),
        P("ep", None, "rep"),
        P("ep", None, "rep"),
        P("ep", None, "rep"),
        P(),
        P(None, "rep"),
    )
    return jax.shard_map(
        per_device, mesh=mesh, in_specs=placed, out_specs=P(("rep", "ep"), None), check_vma=False
    )
```

time: 209 us -> 204 us (0.976)
  waiting for transfers between devices: 123 us -> 129 us
  starting transfers between devices: 54.2 us -> 49.4 us
  Pallas kernels: 20.6 us -> 16.8 us
  matrix products: 2.95 us -> 0 us
    ppermute x14, waiting for transfers between devices: 29.8 us -> 35.7 us  [from_further(): return lax.ppermute(x, 'rep', [(i, (i - by) % n) for i in range(n)])]
    all_to_all x1, starting transfers between devices: 14.4 us -> 9.66 us  [per_device(): lax.all_to_all(back, ('rep', 'ep'), split_axis=0, concat_axis=0, tiled=True)]
    pallas_call x1 -> x3, Pallas kernels: 2.53 us -> 6.55 us  [the longest x2 5.49 us: pack(): pl.pallas_call(pack_kernel, in_specs=[vmem] * 4, out_shape=jax.ShapeDtype...]
    unnamed x9 -> x15, local copies, waits for them, and re-layouts: 0.86 us -> 4.85 us
    pallas_call x2, Pallas kernels: 9.16 us -> 5.61 us  [gate_up(): pl.pallas_call(functools.partial(gate_up_kernel, parts, expert, chunks),...]
    pallas_call x2, Pallas kernels: 7.64 us -> 4.36 us  [down(): pl.pallas_call(functools.partial(down_kernel, groups, expert), in_specs=[...]
    dot_general x3 -> x0, matrix products: 2.95 us -> none  [the longest x2 1.82 us: per_device(): jnp.einsum('ri,rd->id', routing, rows, preferred_element_type=f32)]
    reshape x2 -> x0, local copies, waits for them, and re-layouts: 2.65 us -> none  [per_device(): packed = packed.reshape(owners, capacity, width + adapters)]
  transfers between devices with their start and end apart: 17 -> 17, of which waited for: 8 -> 9; matrix products, arithmetic and copies ran while one was open for 2% -> 1% of each run, Pallas kernels for 7% -> 5%
where the time goes in v5:
time: 204 us
  waiting for transfers between devices  129 us (63%)
  starting transfers between devices  49.4 us (24%)
  Pallas kernels  16.8 us (8%)
  local copies, waits for them, and re-layouts  6.86 us (3%)
    all_to_all x1, waiting for transfers between devices, per_device(): lax.all_to_all(back, ('rep', 'ep'), split_axis=0, concat_axis=0, tiled=True)  47.2 us
    all_to_all x2, waiting for transfers between devices, per_device(): sent = lax.all_to_all(packed, 'ep', split_axis=0, concat_axis=0, tiled=True)  46.1 us
    ppermute x14, waiting for transfers between devices, from_further(): return lax.ppermute(x, 'rep', [(i, (i - by) % n) for i in range(n)])  35.7 us
    ppermute x14, starting transfers between devices, from_further(): return lax.ppermute(x, 'rep', [(i, (i - by) % n) for i in range(n)])  20.3 us
    all_to_all x2, starting transfers between devices, per_device(): sent = lax.all_to_all(packed, 'ep', split_axis=0, concat_axis=0, tiled=True)  19.4 us
    all_to_all x1, starting transfers between devices, per_device(): lax.all_to_all(back, ('rep', 'ep'), split_axis=0, concat_axis=0, tiled=True)  9.66 us
    pallas_call x2, Pallas kernels, gate_up(): pl.pallas_call(functools.partial(gate_up_kernel, parts, expert, chunks),...  5.61 us
    pallas_call x2, Pallas kernels, pack(): pl.pallas_call(pack_kernel, in_specs=[vmem] * 4, out_shape=jax.ShapeDtype...  5.49 us
  transfers between devices with their start and end apart: 17, of which 9 were waited for; matrix products, arithmetic and copies ran while one was open for 1% of the time, Pallas kernels for 5%

profile of v5, /device:TPU:1, one launch (start us, length us, event | category | flops | bytes accessed | tf_op | source)
XLA Modules:
  0.0 203.8 jit_solution(18165872663527176680)
XLA Ops:
  2.4 2.8 %pack.3 = bf16[64,2,3712]{2,1,0:T(2,128)(2,1)} custom-call(bf16[128,16]{1,0:T(8,128)(2,1)S(1)} %copy.57.routing_ref, bf16[16,3584]{1,0:T(8,128)(2,1)} %tokens_ref.3, bf16[3584,128]{1,0:T(8,128)(2,1)} %down_ref.3, f32[16,128]{1,0:T(8,128)S(1)} %compare_convert_fusion.mask_ref), custom_call_target="tpu_custom_call" | custom-call | flops 1000 | bytes 1000 | tf_op jit(solution)/shard_map/pack/pallas_call | solution.py:192
  5.2 13.0 %all-to-all-start.1 = ((bf16[64,2,3712]{2,1,0:T(2,128)(2,1)}), bf16[64,2,3712]{2,1,0:T(2,128)(2,1)S(1)}, u32[]{:S(2)}, u32[]{:S(2)}) async-start(bf16[64,2,3712]{2,1,0:T(2,128)(2,1)} %pack.3), calls=%async_computation.1 | async-start | bytes 1900544 | tf_op jit(solution)/shard_map/all_to_all | solution.py:259
  18.3 2.7 %pack.2 = bf16[64,2,3712]{2,1,0:T(2,128)(2,1)} custom-call(bf16[128,16]{1,0:T(8,128)(2,1)S(1)} %copy.56.routing_ref, bf16[16,3584]{1,0:T(8,128)(2,1)} %tokens_ref.3, bf16[3584,128]{1,0:T(8,128)(2,1)} %down_ref.3, f32[16,128]{1,0:T(8,128)S(1)} %compare_convert_fusion.mask_ref), custom_call_target="tpu_custom_call" | custom-call | flops 1000 | bytes 1000 | tf_op jit(solution)/shard_map/pack/pallas_call | solution.py:192
  21.0 23.1 %all-to-all-done.1.x_ref = bf16[64,2,3712]{2,1,0:T(2,128)(2,1)S(1)} async-done(((bf16[64,2,3712]{2,1,0:T(2,128)(2,1)}), bf16[64,2,3712]{2,1,0:T(2,128)(2,1)S(1)}, u32[]{:S(2)}, u32[]{:S(2)}) %all-to-all-start.1) | async-done | bytes 950304 | tf_op jit(solution)/shard_map/all_to_all | solution.py:259
  44.2 6.5 %all-to-all-start = ((bf16[64,2,3712]{2,1,0:T(2,128)(2,1)}), bf16[64,2,3712]{2,1,0:T(2,128)(2,1)S(1)}, u32[]{:S(2)}, u32[]{:S(2)}) async-start(bf16[64,2,3712]{2,1,0:T(2,128)(2,1)} %pack.2), calls=%async_computation | async-start | bytes 1900544 | tf_op jit(solution)/shard_map/all_to_all | solution.py:259
  52.2 1.5 collective-permute-start.7
  53.7 22.9 %all-to-all-done.x_ref = bf16[64,2,3712]{2,1,0:T(2,128)(2,1)S(1)} async-done(((bf16[64,2,3712]{2,1,0:T(2,128)(2,1)}), bf16[64,2,3712]{2,1,0:T(2,128)(2,1)S(1)}, u32[]{:S(2)}, u32[]{:S(2)}) %all-to-all-start) | async-done | bytes 950304 | tf_op jit(solution)/shard_map/all_to_all | solution.py:259
  78.1 1.5 collective-permute-start
  80.9 2.7 %collective-permute-start.10 = (bf16[64,3712]{1,0:T(8,128)(2,1)S(1)}, bf16[64,3712]{1,0:T(8,128)(2,1)S(1)}, u32[]{:S(2)}, u32[]{:S(2)}) collective-permute-start(bf16[64,3712]{1,0:T(8,128)(2,1)S(1)} %slice.19), channel_id=1, source_target_pairs={{0,192},{64,0},{128,64},{192,128},{1,193},{65,1},{129,65},{193,129... | collective-permute-start | bytes 1425416 | tf_op jit(solution)/shard_map/ppermute | solution.py:206
  83.6 15.9 %collective-permute-done.1.refs_4_ = bf16[128,3712]{1,0:T(8,128)(2,1)S(1)} collective-permute-done((bf16[128,3712]{1,0:T(8,128)(2,1)S(1)}, bf16[128,3712]{1,0:T(8,128)(2,1)S(1)}, u32[]{:S(2)}, u32[]{:S(2)}) %collective-permute-start.1) | collective-permute-done | bytes 950304 | tf_op jit(solution)/shard_map/ppermute | solution.py:206
  99.6 2.7 %collective-permute-start.3 = (bf16[64,3712]{1,0:T(8,128)(2,1)S(1)}, bf16[64,3712]{1,0:T(8,128)(2,1)S(1)}, u32[]{:S(2)}, u32[]{:S(2)}) collective-permute-start(bf16[64,3712]{1,0:T(8,128)(2,1)S(1)} %slice.17), channel_id=1, source_target_pairs={{0,192},{64,0},{128,64},{192,128},{1,193},{65,1},{129,65},{193,129... | collective-permute-start | bytes 1425416 | tf_op jit(solution)/shard_map/ppermute | solution.py:206
  102.4 7.3 %collective-permute-done.9.refs_2_ = bf16[64,3712]{1,0:T(8,128)(2,1)S(1)} collective-permute-done((bf16[64,3712]{1,0:T(8,128)(2,1)S(1)}, bf16[64,3712]{1,0:T(8,128)(2,1)S(1)}, u32[]{:S(2)}, u32[]{:S(2)}) %collective-permute-start.9) | collective-permute-done | bytes 475168 | tf_op jit(solution)/shard_map/ppermute | solution.py:206
  109.7 2.0 copy-done.1
  111.7 3.5 %gate_up.3.refs_0_ = bf16[512,256]{1,0:T(8,128)(2,1)S(1)} custom-call(bf16[128,3712]{1,0:T(8,128)(2,1)S(1)} %relayout.3.refs_0_, bf16[128,3712]{1,0:T(8,128)(2,1)} %collective-permute-done.7.refs_1_, bf16[64,3712]{1,0:T(8,128)(2,1)S(1)} %collective-permute-done.9.refs_2_, bf16[64,3712]{1,0:T(8,128)(2,1)S(1)} %collective-permute-done.10.refs_3_, ...), custom_call_target="tpu_custom_call" | custom-call | flops 1000 | bytes 1000 | tf_op jit(solution)/shard_map/gate_up/pallas_call | solution.py:43
  116.2 2.8 %collective-permute-start.12 = (bf16[512,256]{1,0:T(8,128)(2,1)S(1)}, bf16[512,256]{1,0:T(8,128)(2,1)S(1)}, u32[]{:S(2)}, u32[]{:S(2)}) collective-permute-start(bf16[512,256]{1,0:T(8,128)(2,1)S(1)} %gate_up.3.refs_0_), channel_id=1, source_target_pairs={{0,128},{64,192},{128,0},{192,64},{1,129},{65,193},{129,1},{193,65... | collective-permute-start | bytes 786440 | tf_op jit(solution)/shard_map/ppermute | solution.py:206
  119.8 2.1 %gate_up.2.refs_0_ = bf16[512,256]{1,0:T(8,128)(2,1)S(1)} custom-call(bf16[128,3712]{1,0:T(8,128)(2,1)S(1)} %relayout.2.refs_0_, bf16[128,3712]{1,0:T(8,128)(2,1)S(1)} %collective-permute-done.refs_1_, bf16[64,3712]{1,0:T(8,128)(2,1)S(1)} %collective-permute-done.2.refs_2_, bf16[64,3712]{1,0:T(8,128)(2,1)S(1)} %collective-permute-done.3.refs_3_, ...), custom_call_target="tpu_custom_call" | custom-call | flops 1000 | bytes 1000 | tf_op jit(solution)/shard_map/gate_up/pallas_call | solution.py:43
  123.0 2.8 %collective-permute-start.5 = (bf16[512,256]{1,0:T(8,128)(2,1)S(1)}, bf16[512,256]{1,0:T(8,128)(2,1)S(1)}, u32[]{:S(2)}, u32[]{:S(2)}) collective-permute-start(bf16[512,256]{1,0:T(8,128)(2,1)S(1)} %gate_up.2.refs_0_), channel_id=1, source_target_pairs={{0,128},{64,192},{128,0},{192,64},{1,129},{65,193},{129,1},{193,65... | collective-permute-start | bytes 786440 | tf_op jit(solution)/shard_map/ppermute | solution.py:206
  126.4 5.3 %collective-permute-done.12.refs_2_ = bf16[512,256]{1,0:T(8,128)(2,1)S(1)} collective-permute-done((bf16[512,256]{1,0:T(8,128)(2,1)S(1)}, bf16[512,256]{1,0:T(8,128)(2,1)S(1)}, u32[]{:S(2)}, u32[]{:S(2)}) %collective-permute-start.12) | collective-permute-done | bytes 262176 | tf_op jit(solution)/shard_map/ppermute | solution.py:206
  132.5 2.0 copy-done.3
  134.5 2.1 %down.2.refs_5_ = bf16[256,2,2,896]{3,2,1,0:T(2,128)(2,1)} custom-call(s32[1]{0:T(128)} %bitcast.3.me_ref, bf16[512,256]{1,0:T(8,128)(2,1)S(1)} %gate_up.3.refs_0_, bf16[512,256]{1,0:T(8,128)(2,1)S(1)} %collective-permute-done.11.refs_1_, bf16[512,256]{1,0:T(8,128)(2,1)S(1)} %collective-permute-done.12.refs_2_, ...), custom_call_target="tpu_custom_call" | custom-call | flops 1000 | bytes 1000 | tf_op jit(solution)/shard_map/down/pallas_call | solution.py:95
  136.7 6.3 %collective-permute-done.5.refs_2_ = bf16[512,256]{1,0:T(8,128)(2,1)S(1)} collective-permute-done((bf16[512,256]{1,0:T(8,128)(2,1)S(1)}, bf16[512,256]{1,0:T(8,128)(2,1)S(1)}, u32[]{:S(2)}, u32[]{:S(2)}) %collective-permute-start.5) | collective-permute-done | bytes 262176 | tf_op jit(solution)/shard_map/ppermute | solution.py:206
  143.0 2.2 %down.3 = bf16[256,2,2,896]{3,2,1,0:T(2,128)(2,1)} custom-call(s32[1]{0:T(128)} %bitcast.3.me_ref, bf16[512,256]{1,0:T(8,128)(2,1)S(1)} %gate_up.2.refs_0_, bf16[512,256]{1,0:T(8,128)(2,1)S(1)} %collective-permute-done.4.refs_1_, bf16[512,256]{1,0:T(8,128)(2,1)S(1)} %collective-permute-done.5.refs_2_, ...), custom_call_target="tpu_custom_call", output_to_operand_aliasing={{}: (6, {})} | custom-call | flops 1000 | bytes 1000 | tf_op jit(solution)/shard_map/down/pallas_call | solution.py:95
  145.2 9.7 %all-to-all-start.2 = ((bf16[256,2,2,896]{3,2,1,0:T(2,128)(2,1)}), bf16[256,2,2,896]{3,2,1,0:T(2,128)(2,1)S(1)}, u32[]{:S(2)}, u32[]{:S(2)}) async-start(bf16[256,2,2,896]{3,2,1,0:T(2,128)(2,1)} %down.3), calls=%async_computation.2 | async-start | bytes 3670016 | tf_op jit(solution)/shard_map/all_to_all | solution.py:273
  155.6 47.2 %all-to-all-done.2.back_ref = bf16[256,2,2,896]{3,2,1,0:T(2,128)(2,1)S(1)} async-done(((bf16[256,2,2,896]{3,2,1,0:T(2,128)(2,1)}), bf16[256,2,2,896]{3,2,1,0:T(2,128)(2,1)S(1)}, u32[]{:S(2)}, u32[]{:S(2)}) %all-to-all-start.2) | async-done | bytes 1835040 | tf_op jit(solution)/shard_map/all_to_all | solution.py:273
  (59 shorter events, 12.9 us)
Async XLA Ops:
  5.2 39.0 %all-to-all-start.1 = ((bf16[64,2,3712]{2,1,0:T(2,128)(2,1)}), bf16[64,2,3712]{2,1,0:T(2,128)(2,1)S(1)}, u32[]{:S(2)}, u32[]{:S(2)}) async-start(bf16[64,2,3712]{2,1,0:T(2,128)(2,1)} %pack.3), calls=%async_computation.1 | async-start | bytes 1900544 | tf_op jit(solution)/shard_map/all_to_all | solution.py:259
  44.2 32.4 %all-to-all-start = ((bf16[64,2,3712]{2,1,0:T(2,128)(2,1)}), bf16[64,2,3712]{2,1,0:T(2,128)(2,1)S(1)}, u32[]{:S(2)}, u32[]{:S(2)}) async-start(bf16[64,2,3712]{2,1,0:T(2,128)(2,1)} %pack.2), calls=%async_computation | async-start | bytes 1900544 | tf_op jit(solution)/shard_map/all_to_all | solution.py:259
  50.6 59.0 %copy-start.5 = (bf16[128,256]{1,0:T(8,128)(2,1)S(1)}, bf16[128,256]{1,0:T(8,128)(2,1)}, u32[]{:S(2)}) copy-start(bf16[128,256]{1,0:T(8,128)(2,1)} %refs_7_.3) | copy-start | bytes 196612
  50.8 28.9 %collective-permute-start.8 = (bf16[128,3712]{1,0:T(8,128)(2,1)S(1)}, bf16[128,3712]{1,0:T(8,128)(2,1)S(1)}, u32[]{:S(2)}, u32[]{:S(2)}) collective-permute-start(bf16[128,3712]{1,0:T(8,128)(2,1)S(1)} %relayout.3.refs_0_), channel_id=1, source_target_pairs={{0,64},{64,128},{128,192},{192,0},{1,65},{65,129},{129,193},{193,1... | collective-permute-start | bytes 2850824 | tf_op jit(solution)/shard_map/ppermute | solution.py:206
  52.2 27.6 %collective-permute-start.7 = (bf16[128,3712]{1,0:T(8,128)(2,1)S(1)}, bf16[128,3712]{1,0:T(8,128)(2,1)}, u32[]{:S(2)}, u32[]{:S(2)}) collective-permute-start(bf16[128,3712]{1,0:T(8,128)(2,1)S(1)} %relayout.3.refs_0_), channel_id=1, source_target_pairs={{0,192},{64,0},{128,64},{192,128},{1,193},{65,1},{129,65},{193,129... | collective-permute-start | bytes 2850824 | tf_op jit(solution)/shard_map/ppermute | solution.py:206
  76.6 33.0 %copy-start = (bf16[2,3584,256]{2,1,0:T(8,128)(2,1)S(1)}, bf16[2,3584,256]{2,1,0:T(8,128)(2,1)}, u32[]{:S(2)}) copy-start(bf16[2,3584,256]{2,1,0:T(8,128)(2,1)} %refs_5_.3) | copy-start | bytes 11010052
  76.7 22.7 %collective-permute-start.1 = (bf16[128,3712]{1,0:T(8,128)(2,1)S(1)}, bf16[128,3712]{1,0:T(8,128)(2,1)S(1)}, u32[]{:S(2)}, u32[]{:S(2)}) collective-permute-start(bf16[128,3712]{1,0:T(8,128)(2,1)S(1)} %relayout.2.refs_0_), channel_id=1, source_target_pairs={{0,64},{64,128},{128,192},{192,0},{1,65},{65,129},{129,193},{193,1... | collective-permute-start | bytes 2850824 | tf_op jit(solution)/shard_map/ppermute | solution.py:206
  78.1 21.5 %collective-permute-start = (bf16[128,3712]{1,0:T(8,128)(2,1)S(1)}, bf16[128,3712]{1,0:T(8,128)(2,1)S(1)}, u32[]{:S(2)}, u32[]{:S(2)}) collective-permute-start(bf16[128,3712]{1,0:T(8,128)(2,1)S(1)} %relayout.2.refs_0_), channel_id=1, source_target_pairs={{0,192},{64,0},{128,64},{192,128},{1,193},{65,1},{129,65},{193,129... | collective-permute-start | bytes 2850824 | tf_op jit(solution)/shard_map/ppermute | solution.py:206
  79.7 29.9 %collective-permute-start.9 = (bf16[64,3712]{1,0:T(8,128)(2,1)S(1)}, bf16[64,3712]{1,0:T(8,128)(2,1)S(1)}, u32[]{:S(2)}, u32[]{:S(2)}) collective-permute-start(bf16[64,3712]{1,0:T(8,128)(2,1)S(1)} %slice.18), channel_id=1, source_target_pairs={{0,64},{64,128},{128,192},{192,0},{1,65},{65,129},{129,193},{193,1... | collective-permute-start | bytes 1425416 | tf_op jit(solution)/shard_map/ppermute | solution.py:206
  80.9 28.8 %collective-permute-start.10 = (bf16[64,3712]{1,0:T(8,128)(2,1)S(1)}, bf16[64,3712]{1,0:T(8,128)(2,1)S(1)}, u32[]{:S(2)}, u32[]{:S(2)}) collective-permute-start(bf16[64,3712]{1,0:T(8,128)(2,1)S(1)} %slice.19), channel_id=1, source_target_pairs={{0,192},{64,0},{128,64},{192,128},{1,193},{65,1},{129,65},{193,129... | collective-permute-start | bytes 1425416 | tf_op jit(solution)/shard_map/ppermute | solution.py:206
  99.5 20.3 %collective-permute-start.2 = (bf16[64,3712]{1,0:T(8,128)(2,1)S(1)}, bf16[64,3712]{1,0:T(8,128)(2,1)S(1)}, u32[]{:S(2)}, u32[]{:S(2)}) collective-permute-start(bf16[64,3712]{1,0:T(8,128)(2,1)S(1)} %slice.16), channel_id=1, source_target_pairs={{0,64},{64,128},{128,192},{192,0},{1,65},{65,129},{129,193},{193,1... | collective-permute-start | bytes 1425416 | tf_op jit(solution)/shard_map/ppermute | solution.py:206
  99.6 20.2 %collective-permute-start.3 = (bf16[64,3712]{1,0:T(8,128)(2,1)S(1)}, bf16[64,3712]{1,0:T(8,128)(2,1)S(1)}, u32[]{:S(2)}, u32[]{:S(2)}) collective-permute-start(bf16[64,3712]{1,0:T(8,128)(2,1)S(1)} %slice.17), channel_id=1, source_target_pairs={{0,192},{64,0},{128,64},{192,128},{1,193},{65,1},{129,65},{193,129... | collective-permute-start | bytes 1425416 | tf_op jit(solution)/shard_map/ppermute | solution.py:206
  109.6 2.0 %copy-start.1 = (bf16[2,3584,256]{2,1,0:T(8,128)(2,1)S(1)}, bf16[2,3584,256]{2,1,0:T(8,128)(2,1)}, u32[]{:S(2)}) copy-start(bf16[2,3584,256]{2,1,0:T(8,128)(2,1)} %refs_6_.3) | copy-start | bytes 11010052
  111.7 8.1 %copy-start.2 = (bf16[2,3584,256]{2,1,0:T(8,128)(2,1)S(1)}, bf16[2,3584,256]{2,1,0:T(8,128)(2,1)}, u32[]{:S(2)}) copy-start(bf16[2,3584,256]{2,1,0:T(8,128)(2,1)} %refs_6_.3) | copy-start | bytes 11010052
  115.2 10.6 %collective-permute-start.13 = (bf16[512,256]{1,0:T(8,128)(2,1)S(1)}, bf16[512,256]{1,0:T(8,128)(2,1)S(1)}, u32[]{:S(2)}, u32[]{:S(2)}) collective-permute-start(bf16[512,256]{1,0:T(8,128)(2,1)S(1)} %gate_up.3.refs_0_), channel_id=1, source_target_pairs={{0,64},{64,128},{128,192},{192,0},{1,65},{65,129},{129,193},{193,1... | collective-permute-start | bytes 786440 | tf_op jit(solution)/shard_map/ppermute | solution.py:206
  116.2 15.5 %collective-permute-start.12 = (bf16[512,256]{1,0:T(8,128)(2,1)S(1)}, bf16[512,256]{1,0:T(8,128)(2,1)S(1)}, u32[]{:S(2)}, u32[]{:S(2)}) collective-permute-start(bf16[512,256]{1,0:T(8,128)(2,1)S(1)} %gate_up.3.refs_0_), channel_id=1, source_target_pairs={{0,128},{64,192},{128,0},{192,64},{1,129},{65,193},{129,1},{193,65... | collective-permute-start | bytes 786440 | tf_op jit(solution)/shard_map/ppermute | solution.py:206
  119.0 13.5 %collective-permute-start.11 = (bf16[512,256]{1,0:T(8,128)(2,1)S(1)}, bf16[512,256]{1,0:T(8,128)(2,1)S(1)}, u32[]{:S(2)}, u32[]{:S(2)}) collective-permute-start(bf16[512,256]{1,0:T(8,128)(2,1)S(1)} %gate_up.3.refs_0_), channel_id=1, source_target_pairs={{0,192},{64,0},{128,64},{192,128},{1,193},{65,1},{129,65},{193,129... | collective-permute-start | bytes 786440 | tf_op jit(solution)/shard_map/ppermute | solution.py:206
  122.0 14.7 %collective-permute-start.6 = (bf16[512,256]{1,0:T(8,128)(2,1)S(1)}, bf16[512,256]{1,0:T(8,128)(2,1)S(1)}, u32[]{:S(2)}, u32[]{:S(2)}) collective-permute-start(bf16[512,256]{1,0:T(8,128)(2,1)S(1)} %gate_up.2.refs_0_), channel_id=1, source_target_pairs={{0,64},{64,128},{128,192},{192,0},{1,65},{65,129},{129,193},{193,1... | collective-permute-start | bytes 786440 | tf_op jit(solution)/shard_map/ppermute | solution.py:206
  123.0 20.0 %collective-permute-start.5 = (bf16[512,256]{1,0:T(8,128)(2,1)S(1)}, bf16[512,256]{1,0:T(8,128)(2,1)S(1)}, u32[]{:S(2)}, u32[]{:S(2)}) collective-permute-start(bf16[512,256]{1,0:T(8,128)(2,1)S(1)} %gate_up.2.refs_0_), channel_id=1, source_target_pairs={{0,128},{64,192},{128,0},{192,64},{1,129},{65,193},{129,1},{193,65... | collective-permute-start | bytes 786440 | tf_op jit(solution)/shard_map/ppermute | solution.py:206
  125.8 17.2 %collective-permute-start.4 = (bf16[512,256]{1,0:T(8,128)(2,1)S(1)}, bf16[512,256]{1,0:T(8,128)(2,1)S(1)}, u32[]{:S(2)}, u32[]{:S(2)}) collective-permute-start(bf16[512,256]{1,0:T(8,128)(2,1)S(1)} %gate_up.2.refs_0_), channel_id=1, source_target_pairs={{0,192},{64,0},{128,64},{192,128},{1,193},{65,1},{129,65},{193,129... | collective-permute-start | bytes 786440 | tf_op jit(solution)/shard_map/ppermute | solution.py:206
  132.5 2.0 %copy-start.3 = (bf16[2,1024,896]{2,1,0:T(8,128)(2,1)S(1)}, bf16[2,1024,896]{2,1,0:T(8,128)(2,1)}, u32[]{:S(2)}) copy-start(bf16[2,1024,896]{2,1,0:T(8,128)(2,1)} %refs_4_.3) | copy-start | bytes 11010052
  134.5 8.4 %copy-start.4 = (bf16[2,1024,896]{2,1,0:T(8,128)(2,1)S(1)}, bf16[2,1024,896]{2,1,0:T(8,128)(2,1)}, u32[]{:S(2)}) copy-start(bf16[2,1024,896]{2,1,0:T(8,128)(2,1)} %refs_4_.3) | copy-start | bytes 11010052
  145.2 9.7 %copy-start.6 = (bf16[16,8]{0,1:T(8,128)(2,1)S(1)}, bf16[16,8]{0,1:T(8,128)(2,1)}, u32[]{:S(2)}) copy-start(bf16[16,8]{0,1:T(8,128)(2,1)} %param.11) | copy-start | bytes 772
  145.2 57.6 %all-to-all-start.2 = ((bf16[256,2,2,896]{3,2,1,0:T(2,128)(2,1)}), bf16[256,2,2,896]{3,2,1,0:T(2,128)(2,1)S(1)}, u32[]{:S(2)}, u32[]{:S(2)}) async-start(bf16[256,2,2,896]{3,2,1,0:T(2,128)(2,1)} %down.3), calls=%async_computation.2 | async-start | bytes 3670016 | tf_op jit(solution)/shard_map/all_to_all | solution.py:273

commit v6 on v5

--- a/solution.py
+++ b/solution.py
@@ -75,9 +75,10 @@
         made[i * senders : (i + 1) * senders] = out[i * block : (i + 1) * block].reshape(
             (senders,) + made.shape[1:]
         )
-        to = pl.ds(lax.rem(me + i, groups) * senders, senders)
         copy = pltpu.make_async_copy(
-            made.at[pl.ds(i * senders, senders)], out_ref.at[to, expert], sems.at[i]
+            made.at[pl.ds(i * senders, senders)],
+            out_ref.at[:, lax.rem(me + i, groups), expert],
+            sems.at[i],
         )
         copy.start()
         stored.append(copy)
@@ -98,7 +99,9 @@
         + [vmem] * (groups + 1)
         + [anywhere] * len(held),
         out_specs=anywhere,
-        out_shape=jax.ShapeDtypeStruct((count // capacity, experts, capacity, share), jnp.bfloat16),
+        out_shape=jax.ShapeDtypeStruct(
+            (count // (groups * capacity), groups, experts, capacity, share), jnp.bfloat16
+        ),
         scratch_shapes=[
             pltpu.VMEM((count // capacity, capacity, share), jnp.bfloat16),
             pltpu.SemaphoreType.DMA((groups,)),
@@ -111,10 +114,9 @@
 
 
 def combine_kernel(groups, combiner_ref, back_ref, mixed_ref):
-    senders = back_ref.shape[0] // groups
-    share = back_ref.shape[3]
+    share = back_ref.shape[4]
     for g in range(groups):
-        rows = back_ref[g * senders : (g + 1) * senders]
+        rows = back_ref[:, g]
         rows = rows.reshape((-1,) + rows.shape[2:]).reshape(-1, share)
         mixed_ref[:, g * share : (g + 1) * share] = jnp.dot(
             combiner_ref[...], rows, preferred_element_type=jnp.float32
@@ -126,7 +128,7 @@
     return pl.pallas_call(
         functools.partial(combine_kernel, groups),
         in_specs=[vmem, vmem],
-        out_shape=jax.ShapeDtypeStruct((combiner.shape[0], groups * back.shape[3]), jnp.bfloat16),
+        out_shape=jax.ShapeDtypeStruct((combiner.shape[0], groups * back.shape[4]), jnp.bfloat16),
         compiler_params=pltpu.CompilerParams(vmem_limit_bytes=VMEM_LIMIT),
         cost_estimate=pl.CostEstimate(flops=1000, bytes_accessed=1000, transcendentals=0),
         name="combine",
@@ -147,26 +149,6 @@
         cost_estimate=pl.CostEstimate(flops=1000, bytes_accessed=1000, transcendentals=0),
         name="relayout",
     )(x, *after)
-
-
-def halves_kernel(half, before_ref, after_ref, *refs):
-    top_ref, bottom_ref = refs[-2:]
-    top_ref[...] = before_ref[:half]
-    bottom_ref[...] = after_ref[half:]
-
-
-def halves(before_me, after_me, after):
-    count, width = before_me.shape
-    half = count // 2
-    vmem = pl.BlockSpec(memory_space=pltpu.VMEM)
-    return pl.pallas_call(
-        functools.partial(halves_kernel, half),
-        in_specs=[vmem, vmem] + [pl.BlockSpec(memory_space=pl.ANY)] * len(after),
-        out_shape=[jax.ShapeDtypeStruct((half, width), before_me.dtype)] * 2,
-        compiler_params=pltpu.CompilerParams(vmem_limit_bytes=VMEM_LIMIT),
-        cost_estimate=pl.CostEstimate(flops=1000, bytes_accessed=1000, transcendentals=0),
-        name="halves",
-    )(before_me, after_me, *after)
 
 
 def pack_kernel(routing_ref, tokens_ref, down_ref, mask_ref, out_ref):
@@ -270,7 +252,10 @@
         units = gate_up(every, gate_weight, up_weight, adapter_up_factor, j)
         hidden = [units] + [from_further(units, s) for s in range(1, groups)]
         back = down(hidden, down_weight, me, j, capacity, back)
-    back = lax.all_to_all(back, ("rep", "ep"), split_axis=0, concat_axis=0, tiled=True)
+    shape = back.shape
+    back = back.reshape((owners * groups,) + shape[2:])
+    back = lax.all_to_all(back, ("ep", "rep"), split_axis=0, concat_axis=0, tiled=True)
+    back = back.reshape(shape)
     combiner = jnp.stack([c.reshape(row_count, owners, capacity) for c in combiners], axis=2)
     return combine(combiner.reshape(row_count, -1), back, groups)
 

time: 204 us -> 204 us (level)
  no operation moved by 1% of the time
where the time goes in v6:
time: 204 us
  waiting for transfers between devices  129 us (63%)
  starting transfers between devices  49.4 us (24%)
  Pallas kernels  16.8 us (8%)
  local copies, waits for them, and re-layouts  6.86 us (3%)
    all_to_all x1, waiting for transfers between devices, per_device(): lax.all_to_all(back, ('ep', 'rep'), split_axis=0, concat_axis=0, tiled=True)  47 us
    all_to_all x2, waiting for transfers between devices, per_device(): sent = lax.all_to_all(packed, 'ep', split_axis=0, concat_axis=0, tiled=True)  46.1 us
    ppermute x14, waiting for transfers between devices, from_further(): return lax.ppermute(x, 'rep', [(i, (i - by) % n) for i in range(n)])  35.7 us
    ppermute x14, starting transfers between devices, from_further(): return lax.ppermute(x, 'rep', [(i, (i - by) % n) for i in range(n)])  20.3 us
    all_to_all x2, starting transfers between devices, per_device(): sent = lax.all_to_all(packed, 'ep', split_axis=0, concat_axis=0, tiled=True)  19.4 us
    all_to_all x1, starting transfers between devices, per_device(): lax.all_to_all(back, ('ep', 'rep'), split_axis=0, concat_axis=0, tiled=True)  9.66 us
    pallas_call x2, Pallas kernels, gate_up(): pl.pallas_call(functools.partial(gate_up_kernel, parts, expert, chunks),...  5.61 us
    pallas_call x2, Pallas kernels, pack(): pl.pallas_call(pack_kernel, in_specs=[vmem] * 4, out_shape=jax.ShapeDtype...  5.49 us
  transfers between devices with their start and end apart: 17, of which 9 were waited for; matrix products, arithmetic and copies ran while one was open for 1% of the time, Pallas kernels for 5%

profile of v6, /device:TPU:1, one launch (start us, length us, event | category | flops | bytes accessed | tf_op | source)
XLA Modules:
  0.0 203.7 jit_solution(4184860781208361918)
XLA Ops:
  2.4 2.8 %pack.3 = bf16[64,2,3712]{2,1,0:T(2,128)(2,1)} custom-call(bf16[128,16]{1,0:T(8,128)(2,1)S(1)} %copy.57.routing_ref, bf16[16,3584]{1,0:T(8,128)(2,1)} %tokens_ref.3, bf16[3584,128]{1,0:T(8,128)(2,1)} %down_ref.3, f32[16,128]{1,0:T(8,128)S(1)} %compare_convert_fusion.mask_ref), custom_call_target="tpu_custom_call" | custom-call | flops 1000 | bytes 1000 | tf_op jit(solution)/shard_map/pack/pallas_call | solution.py:174
  5.2 13.0 %all-to-all-start.1 = ((bf16[64,2,3712]{2,1,0:T(2,128)(2,1)}), bf16[64,2,3712]{2,1,0:T(2,128)(2,1)S(1)}, u32[]{:S(2)}, u32[]{:S(2)}) async-start(bf16[64,2,3712]{2,1,0:T(2,128)(2,1)} %pack.3), calls=%async_computation.1 | async-start | bytes 1900544 | tf_op jit(solution)/shard_map/all_to_all | solution.py:241
  18.3 2.7 %pack.2 = bf16[64,2,3712]{2,1,0:T(2,128)(2,1)} custom-call(bf16[128,16]{1,0:T(8,128)(2,1)S(1)} %copy.56.routing_ref, bf16[16,3584]{1,0:T(8,128)(2,1)} %tokens_ref.3, bf16[3584,128]{1,0:T(8,128)(2,1)} %down_ref.3, f32[16,128]{1,0:T(8,128)S(1)} %compare_convert_fusion.mask_ref), custom_call_target="tpu_custom_call" | custom-call | flops 1000 | bytes 1000 | tf_op jit(solution)/shard_map/pack/pallas_call | solution.py:174
  21.0 23.1 %all-to-all-done.1.x_ref = bf16[64,2,3712]{2,1,0:T(2,128)(2,1)S(1)} async-done(((bf16[64,2,3712]{2,1,0:T(2,128)(2,1)}), bf16[64,2,3712]{2,1,0:T(2,128)(2,1)S(1)}, u32[]{:S(2)}, u32[]{:S(2)}) %all-to-all-start.1) | async-done | bytes 950304 | tf_op jit(solution)/shard_map/all_to_all | solution.py:241
  44.2 6.5 %all-to-all-start = ((bf16[64,2,3712]{2,1,0:T(2,128)(2,1)}), bf16[64,2,3712]{2,1,0:T(2,128)(2,1)S(1)}, u32[]{:S(2)}, u32[]{:S(2)}) async-start(bf16[64,2,3712]{2,1,0:T(2,128)(2,1)} %pack.2), calls=%async_computation | async-start | bytes 1900544 | tf_op jit(solution)/shard_map/all_to_all | solution.py:241
  52.2 1.5 collective-permute-start.7
  53.7 22.9 %all-to-all-done.x_ref = bf16[64,2,3712]{2,1,0:T(2,128)(2,1)S(1)} async-done(((bf16[64,2,3712]{2,1,0:T(2,128)(2,1)}), bf16[64,2,3712]{2,1,0:T(2,128)(2,1)S(1)}, u32[]{:S(2)}, u32[]{:S(2)}) %all-to-all-start) | async-done | bytes 950304 | tf_op jit(solution)/shard_map/all_to_all | solution.py:241
  78.1 1.5 collective-permute-start
  80.9 2.7 %collective-permute-start.10 = (bf16[64,3712]{1,0:T(8,128)(2,1)S(1)}, bf16[64,3712]{1,0:T(8,128)(2,1)S(1)}, u32[]{:S(2)}, u32[]{:S(2)}) collective-permute-start(bf16[64,3712]{1,0:T(8,128)(2,1)S(1)} %slice.19), channel_id=1, source_target_pairs={{0,192},{64,0},{128,64},{192,128},{1,193},{65,1},{129,65},{193,129... | collective-permute-start | bytes 1425416 | tf_op jit(solution)/shard_map/ppermute | solution.py:188
  83.6 15.9 %collective-permute-done.1.refs_4_ = bf16[128,3712]{1,0:T(8,128)(2,1)S(1)} collective-permute-done((bf16[128,3712]{1,0:T(8,128)(2,1)S(1)}, bf16[128,3712]{1,0:T(8,128)(2,1)S(1)}, u32[]{:S(2)}, u32[]{:S(2)}) %collective-permute-start.1) | collective-permute-done | bytes 950304 | tf_op jit(solution)/shard_map/ppermute | solution.py:188
  99.6 2.7 %collective-permute-start.3 = (bf16[64,3712]{1,0:T(8,128)(2,1)S(1)}, bf16[64,3712]{1,0:T(8,128)(2,1)S(1)}, u32[]{:S(2)}, u32[]{:S(2)}) collective-permute-start(bf16[64,3712]{1,0:T(8,128)(2,1)S(1)} %slice.17), channel_id=1, source_target_pairs={{0,192},{64,0},{128,64},{192,128},{1,193},{65,1},{129,65},{193,129... | collective-permute-start | bytes 1425416 | tf_op jit(solution)/shard_map/ppermute | solution.py:188
  102.4 7.3 %collective-permute-done.9.refs_2_ = bf16[64,3712]{1,0:T(8,128)(2,1)S(1)} collective-permute-done((bf16[64,3712]{1,0:T(8,128)(2,1)S(1)}, bf16[64,3712]{1,0:T(8,128)(2,1)S(1)}, u32[]{:S(2)}, u32[]{:S(2)}) %collective-permute-start.9) | collective-permute-done | bytes 475168 | tf_op jit(solution)/shard_map/ppermute | solution.py:188
  109.7 2.0 copy-done.1
  111.7 3.5 %gate_up.3.refs_0_ = bf16[512,256]{1,0:T(8,128)(2,1)S(1)} custom-call(bf16[128,3712]{1,0:T(8,128)(2,1)S(1)} %relayout.3.refs_0_, bf16[128,3712]{1,0:T(8,128)(2,1)} %collective-permute-done.7.refs_1_, bf16[64,3712]{1,0:T(8,128)(2,1)S(1)} %collective-permute-done.9.refs_2_, bf16[64,3712]{1,0:T(8,128)(2,1)S(1)} %collective-permute-done.10.refs_3_, ...), custom_call_target="tpu_custom_call" | custom-call | flops 1000 | bytes 1000 | tf_op jit(solution)/shard_map/gate_up/pallas_call | solution.py:43
  116.2 2.8 %collective-permute-start.12 = (bf16[512,256]{1,0:T(8,128)(2,1)S(1)}, bf16[512,256]{1,0:T(8,128)(2,1)S(1)}, u32[]{:S(2)}, u32[]{:S(2)}) collective-permute-start(bf16[512,256]{1,0:T(8,128)(2,1)S(1)} %gate_up.3.refs_0_), channel_id=1, source_target_pairs={{0,128},{64,192},{128,0},{192,64},{1,129},{65,193},{129,1},{193,65... | collective-permute-start | bytes 786440 | tf_op jit(solution)/shard_map/ppermute | solution.py:188
  119.8 2.1 %gate_up.2.refs_0_ = bf16[512,256]{1,0:T(8,128)(2,1)S(1)} custom-call(bf16[128,3712]{1,0:T(8,128)(2,1)S(1)} %relayout.2.refs_0_, bf16[128,3712]{1,0:T(8,128)(2,1)S(1)} %collective-permute-done.refs_1_, bf16[64,3712]{1,0:T(8,128)(2,1)S(1)} %collective-permute-done.2.refs_2_, bf16[64,3712]{1,0:T(8,128)(2,1)S(1)} %collective-permute-done.3.refs_3_, ...), custom_call_target="tpu_custom_call" | custom-call | flops 1000 | bytes 1000 | tf_op jit(solution)/shard_map/gate_up/pallas_call | solution.py:43
  123.0 2.8 %collective-permute-start.5 = (bf16[512,256]{1,0:T(8,128)(2,1)S(1)}, bf16[512,256]{1,0:T(8,128)(2,1)S(1)}, u32[]{:S(2)}, u32[]{:S(2)}) collective-permute-start(bf16[512,256]{1,0:T(8,128)(2,1)S(1)} %gate_up.2.refs_0_), channel_id=1, source_target_pairs={{0,128},{64,192},{128,0},{192,64},{1,129},{65,193},{129,1},{193,65... | collective-permute-start | bytes 786440 | tf_op jit(solution)/shard_map/ppermute | solution.py:188
  126.4 5.3 %collective-permute-done.12.refs_2_ = bf16[512,256]{1,0:T(8,128)(2,1)S(1)} collective-permute-done((bf16[512,256]{1,0:T(8,128)(2,1)S(1)}, bf16[512,256]{1,0:T(8,128)(2,1)S(1)}, u32[]{:S(2)}, u32[]{:S(2)}) %collective-permute-start.12) | collective-permute-done | bytes 262176 | tf_op jit(solution)/shard_map/ppermute | solution.py:188
  132.5 2.0 copy-done.3
  134.5 2.2 %down.2.refs_5_ = bf16[64,4,2,2,896]{4,3,2,1,0:T(2,128)(2,1)} custom-call(s32[1]{0:T(128)} %bitcast.3.me_ref, bf16[512,256]{1,0:T(8,128)(2,1)S(1)} %gate_up.3.refs_0_, bf16[512,256]{1,0:T(8,128)(2,1)S(1)} %collective-permute-done.11.refs_1_, bf16[512,256]{1,0:T(8,128)(2,1)S(1)} %collective-permute-done.12.refs_2_, ...), custom_call_target="tpu_custom_call" | custom-call | flops 1000 | bytes 1000 | tf_op jit(solution)/shard_map/down/pallas_call | solution.py:96
  136.7 6.2 %collective-permute-done.5.refs_2_ = bf16[512,256]{1,0:T(8,128)(2,1)S(1)} collective-permute-done((bf16[512,256]{1,0:T(8,128)(2,1)S(1)}, bf16[512,256]{1,0:T(8,128)(2,1)S(1)}, u32[]{:S(2)}, u32[]{:S(2)}) %collective-permute-start.5) | collective-permute-done | bytes 262176 | tf_op jit(solution)/shard_map/ppermute | solution.py:188
  143.0 2.2 %down.3 = bf16[64,4,2,2,896]{4,3,2,1,0:T(2,128)(2,1)} custom-call(s32[1]{0:T(128)} %bitcast.3.me_ref, bf16[512,256]{1,0:T(8,128)(2,1)S(1)} %gate_up.2.refs_0_, bf16[512,256]{1,0:T(8,128)(2,1)S(1)} %collective-permute-done.4.refs_1_, bf16[512,256]{1,0:T(8,128)(2,1)S(1)} %collective-permute-done.5.refs_2_, ...), custom_call_target="tpu_custom_call", output_to_operand_aliasing={{}: (6, {})} | custom-call | flops 1000 | bytes 1000 | tf_op jit(solution)/shard_map/down/pallas_call | solution.py:96
  145.2 9.7 %all-to-all-start.2 = ((bf16[256,2,2,896]{3,2,1,0:T(2,128)(2,1)}), bf16[256,2,2,896]{3,2,1,0:T(2,128)(2,1)S(1)}, u32[]{:S(2)}, u32[]{:S(2)}) async-start(bf16[256,2,2,896]{3,2,1,0:T(2,128)(2,1)} %bitcast.4), calls=%async_computation.2 | async-start | bytes 3670016 | tf_op jit(solution)/shard_map/all_to_all | solution.py:257
  155.6 47.0 %all-to-all-done.2 = bf16[256,2,2,896]{3,2,1,0:T(2,128)(2,1)S(1)} async-done(((bf16[256,2,2,896]{3,2,1,0:T(2,128)(2,1)}), bf16[256,2,2,896]{3,2,1,0:T(2,128)(2,1)S(1)}, u32[]{:S(2)}, u32[]{:S(2)}) %all-to-all-start.2) | async-done | bytes 1835040 | tf_op jit(solution)/shard_map/all_to_all | solution.py:257
  (59 shorter events, 12.9 us)
Async XLA Ops:
  5.2 39.0 %all-to-all-start.1 = ((bf16[64,2,3712]{2,1,0:T(2,128)(2,1)}), bf16[64,2,3712]{2,1,0:T(2,128)(2,1)S(1)}, u32[]{:S(2)}, u32[]{:S(2)}) async-start(bf16[64,2,3712]{2,1,0:T(2,128)(2,1)} %pack.3), calls=%async_computation.1 | async-start | bytes 1900544 | tf_op jit(solution)/shard_map/all_to_all | solution.py:241
  44.2 32.4 %all-to-all-start = ((bf16[64,2,3712]{2,1,0:T(2,128)(2,1)}), bf16[64,2,3712]{2,1,0:T(2,128)(2,1)S(1)}, u32[]{:S(2)}, u32[]{:S(2)}) async-start(bf16[64,2,3712]{2,1,0:T(2,128)(2,1)} %pack.2), calls=%async_computation | async-start | bytes 1900544 | tf_op jit(solution)/shard_map/all_to_all | solution.py:241
  50.6 59.0 %copy-start.5 = (bf16[128,256]{1,0:T(8,128)(2,1)S(1)}, bf16[128,256]{1,0:T(8,128)(2,1)}, u32[]{:S(2)}) copy-start(bf16[128,256]{1,0:T(8,128)(2,1)} %refs_7_.3) | copy-start | bytes 196612
  50.8 28.9 %collective-permute-start.8 = (bf16[128,3712]{1,0:T(8,128)(2,1)S(1)}, bf16[128,3712]{1,0:T(8,128)(2,1)S(1)}, u32[]{:S(2)}, u32[]{:S(2)}) collective-permute-start(bf16[128,3712]{1,0:T(8,128)(2,1)S(1)} %relayout.3.refs_0_), channel_id=1, source_target_pairs={{0,64},{64,128},{128,192},{192,0},{1,65},{65,129},{129,193},{193,1... | collective-permute-start | bytes 2850824 | tf_op jit(solution)/shard_map/ppermute | solution.py:188
  52.2 27.6 %collective-permute-start.7 = (bf16[128,3712]{1,0:T(8,128)(2,1)S(1)}, bf16[128,3712]{1,0:T(8,128)(2,1)}, u32[]{:S(2)}, u32[]{:S(2)}) collective-permute-start(bf16[128,3712]{1,0:T(8,128)(2,1)S(1)} %relayout.3.refs_0_), channel_id=1, source_target_pairs={{0,192},{64,0},{128,64},{192,128},{1,193},{65,1},{129,65},{193,129... | collective-permute-start | bytes 2850824 | tf_op jit(solution)/shard_map/ppermute | solution.py:188
  76.6 33.0 %copy-start = (bf16[2,3584,256]{2,1,0:T(8,128)(2,1)S(1)}, bf16[2,3584,256]{2,1,0:T(8,128)(2,1)}, u32[]{:S(2)}) copy-start(bf16[2,3584,256]{2,1,0:T(8,128)(2,1)} %refs_5_.3) | copy-start | bytes 11010052
  76.7 22.7 %collective-permute-start.1 = (bf16[128,3712]{1,0:T(8,128)(2,1)S(1)}, bf16[128,3712]{1,0:T(8,128)(2,1)S(1)}, u32[]{:S(2)}, u32[]{:S(2)}) collective-permute-start(bf16[128,3712]{1,0:T(8,128)(2,1)S(1)} %relayout.2.refs_0_), channel_id=1, source_target_pairs={{0,64},{64,128},{128,192},{192,0},{1,65},{65,129},{129,193},{193,1... | collective-permute-start | bytes 2850824 | tf_op jit(solution)/shard_map/ppermute | solution.py:188
  78.1 21.5 %collective-permute-start = (bf16[128,3712]{1,0:T(8,128)(2,1)S(1)}, bf16[128,3712]{1,0:T(8,128)(2,1)S(1)}, u32[]{:S(2)}, u32[]{:S(2)}) collective-permute-start(bf16[128,3712]{1,0:T(8,128)(2,1)S(1)} %relayout.2.refs_0_), channel_id=1, source_target_pairs={{0,192},{64,0},{128,64},{192,128},{1,193},{65,1},{129,65},{193,129... | collective-permute-start | bytes 2850824 | tf_op jit(solution)/shard_map/ppermute | solution.py:188
  79.7 29.9 %collective-permute-start.9 = (bf16[64,3712]{1,0:T(8,128)(2,1)S(1)}, bf16[64,3712]{1,0:T(8,128)(2,1)S(1)}, u32[]{:S(2)}, u32[]{:S(2)}) collective-permute-start(bf16[64,3712]{1,0:T(8,128)(2,1)S(1)} %slice.18), channel_id=1, source_target_pairs={{0,64},{64,128},{128,192},{192,0},{1,65},{65,129},{129,193},{193,1... | collective-permute-start | bytes 1425416 | tf_op jit(solution)/shard_map/ppermute | solution.py:188
  80.9 28.8 %collective-permute-start.10 = (bf16[64,3712]{1,0:T(8,128)(2,1)S(1)}, bf16[64,3712]{1,0:T(8,128)(2,1)S(1)}, u32[]{:S(2)}, u32[]{:S(2)}) collective-permute-start(bf16[64,3712]{1,0:T(8,128)(2,1)S(1)} %slice.19), channel_id=1, source_target_pairs={{0,192},{64,0},{128,64},{192,128},{1,193},{65,1},{129,65},{193,129... | collective-permute-start | bytes 1425416 | tf_op jit(solution)/shard_map/ppermute | solution.py:188
  99.5 20.3 %collective-permute-start.2 = (bf16[64,3712]{1,0:T(8,128)(2,1)S(1)}, bf16[64,3712]{1,0:T(8,128)(2,1)S(1)}, u32[]{:S(2)}, u32[]{:S(2)}) collective-permute-start(bf16[64,3712]{1,0:T(8,128)(2,1)S(1)} %slice.16), channel_id=1, source_target_pairs={{0,64},{64,128},{128,192},{192,0},{1,65},{65,129},{129,193},{193,1... | collective-permute-start | bytes 1425416 | tf_op jit(solution)/shard_map/ppermute | solution.py:188
  99.6 20.2 %collective-permute-start.3 = (bf16[64,3712]{1,0:T(8,128)(2,1)S(1)}, bf16[64,3712]{1,0:T(8,128)(2,1)S(1)}, u32[]{:S(2)}, u32[]{:S(2)}) collective-permute-start(bf16[64,3712]{1,0:T(8,128)(2,1)S(1)} %slice.17), channel_id=1, source_target_pairs={{0,192},{64,0},{128,64},{192,128},{1,193},{65,1},{129,65},{193,129... | collective-permute-start | bytes 1425416 | tf_op jit(solution)/shard_map/ppermute | solution.py:188
  109.6 2.0 %copy-start.1 = (bf16[2,3584,256]{2,1,0:T(8,128)(2,1)S(1)}, bf16[2,3584,256]{2,1,0:T(8,128)(2,1)}, u32[]{:S(2)}) copy-start(bf16[2,3584,256]{2,1,0:T(8,128)(2,1)} %refs_6_.3) | copy-start | bytes 11010052
  111.7 8.1 %copy-start.2 = (bf16[2,3584,256]{2,1,0:T(8,128)(2,1)S(1)}, bf16[2,3584,256]{2,1,0:T(8,128)(2,1)}, u32[]{:S(2)}) copy-start(bf16[2,3584,256]{2,1,0:T(8,128)(2,1)} %refs_6_.3) | copy-start | bytes 11010052
  115.2 10.6 %collective-permute-start.13 = (bf16[512,256]{1,0:T(8,128)(2,1)S(1)}, bf16[512,256]{1,0:T(8,128)(2,1)S(1)}, u32[]{:S(2)}, u32[]{:S(2)}) collective-permute-start(bf16[512,256]{1,0:T(8,128)(2,1)S(1)} %gate_up.3.refs_0_), channel_id=1, source_target_pairs={{0,64},{64,128},{128,192},{192,0},{1,65},{65,129},{129,193},{193,1... | collective-permute-start | bytes 786440 | tf_op jit(solution)/shard_map/ppermute | solution.py:188
  116.2 15.5 %collective-permute-start.12 = (bf16[512,256]{1,0:T(8,128)(2,1)S(1)}, bf16[512,256]{1,0:T(8,128)(2,1)S(1)}, u32[]{:S(2)}, u32[]{:S(2)}) collective-permute-start(bf16[512,256]{1,0:T(8,128)(2,1)S(1)} %gate_up.3.refs_0_), channel_id=1, source_target_pairs={{0,128},{64,192},{128,0},{192,64},{1,129},{65,193},{129,1},{193,65... | collective-permute-start | bytes 786440 | tf_op jit(solution)/shard_map/ppermute | solution.py:188
  119.0 13.5 %collective-permute-start.11 = (bf16[512,256]{1,0:T(8,128)(2,1)S(1)}, bf16[512,256]{1,0:T(8,128)(2,1)S(1)}, u32[]{:S(2)}, u32[]{:S(2)}) collective-permute-start(bf16[512,256]{1,0:T(8,128)(2,1)S(1)} %gate_up.3.refs_0_), channel_id=1, source_target_pairs={{0,192},{64,0},{128,64},{192,128},{1,193},{65,1},{129,65},{193,129... | collective-permute-start | bytes 786440 | tf_op jit(solution)/shard_map/ppermute | solution.py:188
  122.0 14.7 %collective-permute-start.6 = (bf16[512,256]{1,0:T(8,128)(2,1)S(1)}, bf16[512,256]{1,0:T(8,128)(2,1)S(1)}, u32[]{:S(2)}, u32[]{:S(2)}) collective-permute-start(bf16[512,256]{1,0:T(8,128)(2,1)S(1)} %gate_up.2.refs_0_), channel_id=1, source_target_pairs={{0,64},{64,128},{128,192},{192,0},{1,65},{65,129},{129,193},{193,1... | collective-permute-start | bytes 786440 | tf_op jit(solution)/shard_map/ppermute | solution.py:188
  123.0 20.0 %collective-permute-start.5 = (bf16[512,256]{1,0:T(8,128)(2,1)S(1)}, bf16[512,256]{1,0:T(8,128)(2,1)S(1)}, u32[]{:S(2)}, u32[]{:S(2)}) collective-permute-start(bf16[512,256]{1,0:T(8,128)(2,1)S(1)} %gate_up.2.refs_0_), channel_id=1, source_target_pairs={{0,128},{64,192},{128,0},{192,64},{1,129},{65,193},{129,1},{193,65... | collective-permute-start | bytes 786440 | tf_op jit(solution)/shard_map/ppermute | solution.py:188
  125.8 17.2 %collective-permute-start.4 = (bf16[512,256]{1,0:T(8,128)(2,1)S(1)}, bf16[512,256]{1,0:T(8,128)(2,1)S(1)}, u32[]{:S(2)}, u32[]{:S(2)}) collective-permute-start(bf16[512,256]{1,0:T(8,128)(2,1)S(1)} %gate_up.2.refs_0_), channel_id=1, source_target_pairs={{0,192},{64,0},{128,64},{192,128},{1,193},{65,1},{129,65},{193,129... | collective-permute-start | bytes 786440 | tf_op jit(solution)/shard_map/ppermute | solution.py:188
  132.5 2.0 %copy-start.3 = (bf16[2,1024,896]{2,1,0:T(8,128)(2,1)S(1)}, bf16[2,1024,896]{2,1,0:T(8,128)(2,1)}, u32[]{:S(2)}) copy-start(bf16[2,1024,896]{2,1,0:T(8,128)(2,1)} %refs_4_.3) | copy-start | bytes 11010052
  134.5 8.4 %copy-start.4 = (bf16[2,1024,896]{2,1,0:T(8,128)(2,1)S(1)}, bf16[2,1024,896]{2,1,0:T(8,128)(2,1)}, u32[]{:S(2)}) copy-start(bf16[2,1024,896]{2,1,0:T(8,128)(2,1)} %refs_4_.3) | copy-start | bytes 11010052
  145.2 9.7 %copy-start.6 = (bf16[16,8]{0,1:T(8,128)(2,1)S(1)}, bf16[16,8]{0,1:T(8,128)(2,1)}, u32[]{:S(2)}) copy-start(bf16[16,8]{0,1:T(8,128)(2,1)} %param.11) | copy-start | bytes 772
  145.2 57.4 %all-to-all-start.2 = ((bf16[256,2,2,896]{3,2,1,0:T(2,128)(2,1)}), bf16[256,2,2,896]{3,2,1,0:T(2,128)(2,1)S(1)}, u32[]{:S(2)}, u32[]{:S(2)}) async-start(bf16[256,2,2,896]{3,2,1,0:T(2,128)(2,1)} %bitcast.4), calls=%async_computation.2 | async-start | bytes 3670016 | tf_op jit(solution)/shard_map/all_to_all | solution.py:257

commit v7 on v5

--- a/solution.py
+++ b/solution.py
@@ -21,7 +21,9 @@
 
 def gate_up_kernel(parts, expert, chunks, *refs):
     rows = refs[:parts]
-    gate_ref, up_ref, factor_ref, hidden_ref = refs[parts:]
+    gate_ref, up_ref, factor_ref, hidden_ref, up_at, sem = refs[parts:]
+    fetch = pltpu.make_async_copy(up_ref.at[expert], up_at, sem)
+    fetch.start()
     width = gate_ref.shape[1]
     depth = width // chunks
     low = jnp.concatenate([r[:, width:] for r in rows], axis=0)
@@ -31,7 +33,11 @@
         here = slice(c * depth, (c + 1) * depth)
         x = jnp.concatenate([r[:, here] for r in rows], axis=0)
         gate += jnp.dot(x, gate_ref[expert, here], preferred_element_type=jnp.float32)
-        up += jnp.dot(x, up_ref[expert, here], preferred_element_type=jnp.float32)
+    fetch.wait()
+    for c in range(chunks):
+        here = slice(c * depth, (c + 1) * depth)
+        x = jnp.concatenate([r[:, here] for r in rows], axis=0)
+        up += jnp.dot(x, up_at[here], preferred_element_type=jnp.float32)
     hidden_ref[...] = (gate / (1.0 + jnp.exp(-gate)) * up).astype(hidden_ref.dtype)
 
 
@@ -42,13 +48,17 @@
     vmem = pl.BlockSpec(memory_space=pltpu.VMEM)
     return pl.pallas_call(
         functools.partial(gate_up_kernel, parts, expert, chunks),
-        in_specs=[vmem] * (parts + 3),
+        in_specs=[vmem] * (parts + 1) + [pl.BlockSpec(memory_space=pl.ANY), vmem],
         out_specs=vmem,
         out_shape=jax.ShapeDtypeStruct((count, units), jnp.bfloat16),
+        scratch_shapes=[
+            pltpu.VMEM(up_weight.shape[1:], jnp.bfloat16),
+            pltpu.SemaphoreType.DMA,
+        ],
         compiler_params=pltpu.CompilerParams(vmem_limit_bytes=VMEM_LIMIT),
         cost_estimate=pl.CostEstimate(flops=1000, bytes_accessed=1000, transcendentals=0),
         name="gate_up",
-    )(*(in_vmem(x) for x in (*rows, gate_weight, up_weight)), factor)
+    )(*(in_vmem(x) for x in (*rows, gate_weight)), in_hbm(up_weight), factor)
 
 
 def down_kernel(groups, expert, me_ref, *refs):

time: 204 us -> 204 us (level)
  Pallas kernels: 16.8 us -> 20.7 us
  waiting for transfers between devices: 129 us -> 126 us
  local copies, waits for them, and re-layouts: 6.86 us -> 4.82 us
    pallas_call x2, Pallas kernels: 5.61 us -> 9.52 us  [gate_up(): pl.pallas_call(functools.partial(gate_up_kernel, parts, expert, chunks),...]
    ppermute x14, waiting for transfers between devices: 35.7 us -> 32.6 us  [from_further(): return lax.ppermute(x, 'rep', [(i, (i - by) % n) for i in range(n)])]
    unnamed x15 -> x11, local copies, waits for them, and re-layouts: 4.85 us -> 2.81 us
  transfers between devices with their start and end apart: 17 -> 17, of which waited for: 9 -> 10; matrix products, arithmetic and copies ran while one was open for 1% -> 1% of each run, Pallas kernels for 5% -> 7%
where the time goes in v7:
time: 204 us
  waiting for transfers between devices  126 us (62%)
  starting transfers between devices  50.7 us (25%)
  Pallas kernels  20.7 us (10%)
  local copies, waits for them, and re-layouts  4.82 us (2%)
    all_to_all x1, waiting for transfers between devices, per_device(): lax.all_to_all(back, ('rep', 'ep'), split_axis=0, concat_axis=0, tiled=True)  47.2 us
    all_to_all x2, waiting for transfers between devices, per_device(): sent = lax.all_to_all(packed, 'ep', split_axis=0, concat_axis=0, tiled=True)  46.1 us
    ppermute x14, waiting for transfers between devices, from_further(): return lax.ppermute(x, 'rep', [(i, (i - by) % n) for i in range(n)])  32.6 us
    ppermute x14, starting transfers between devices, from_further(): return lax.ppermute(x, 'rep', [(i, (i - by) % n) for i in range(n)])  20.5 us
    all_to_all x2, starting transfers between devices, per_device(): sent = lax.all_to_all(packed, 'ep', split_axis=0, concat_axis=0, tiled=True)  19.4 us
    all_to_all x1, starting transfers between devices, per_device(): lax.all_to_all(back, ('rep', 'ep'), split_axis=0, concat_axis=0, tiled=True)  10.8 us
    pallas_call x2, Pallas kernels, gate_up(): pl.pallas_call(functools.partial(gate_up_kernel, parts, expert, chunks),...  9.52 us
    pallas_call x2, Pallas kernels, pack(): pl.pallas_call(pack_kernel, in_specs=[vmem] * 4, out_shape=jax.ShapeDtype...  5.49 us
  transfers between devices with their start and end apart: 17, of which 10 were waited for; matrix products, arithmetic and copies ran while one was open for 1% of the time, Pallas kernels for 7%

profile of v7, /device:TPU:1, one launch (start us, length us, event | category | flops | bytes accessed | tf_op | source)
XLA Modules:
  0.0 203.9 jit_solution(9454019352484153179)
XLA Ops:
  2.4 2.8 %pack.3 = bf16[64,2,3712]{2,1,0:T(2,128)(2,1)} custom-call(bf16[128,16]{1,0:T(8,128)(2,1)S(1)} %copy.57.routing_ref, bf16[16,3584]{1,0:T(8,128)(2,1)} %tokens_ref.3, bf16[3584,128]{1,0:T(8,128)(2,1)} %down_ref.3, f32[16,128]{1,0:T(8,128)S(1)} %compare_convert_fusion.mask_ref), custom_call_target="tpu_custom_call" | custom-call | flops 1000 | bytes 1000 | tf_op jit(solution)/shard_map/pack/pallas_call | solution.py:202
  5.2 13.0 %all-to-all-start.1 = ((bf16[64,2,3712]{2,1,0:T(2,128)(2,1)}), bf16[64,2,3712]{2,1,0:T(2,128)(2,1)S(1)}, u32[]{:S(2)}, u32[]{:S(2)}) async-start(bf16[64,2,3712]{2,1,0:T(2,128)(2,1)} %pack.3), calls=%async_computation.1 | async-start | bytes 1900544 | tf_op jit(solution)/shard_map/all_to_all | solution.py:269
  18.3 2.7 %pack.2 = bf16[64,2,3712]{2,1,0:T(2,128)(2,1)} custom-call(bf16[128,16]{1,0:T(8,128)(2,1)S(1)} %copy.56.routing_ref, bf16[16,3584]{1,0:T(8,128)(2,1)} %tokens_ref.3, bf16[3584,128]{1,0:T(8,128)(2,1)} %down_ref.3, f32[16,128]{1,0:T(8,128)S(1)} %compare_convert_fusion.mask_ref), custom_call_target="tpu_custom_call" | custom-call | flops 1000 | bytes 1000 | tf_op jit(solution)/shard_map/pack/pallas_call | solution.py:202
  21.0 23.1 %all-to-all-done.1.x_ref = bf16[64,2,3712]{2,1,0:T(2,128)(2,1)S(1)} async-done(((bf16[64,2,3712]{2,1,0:T(2,128)(2,1)}), bf16[64,2,3712]{2,1,0:T(2,128)(2,1)S(1)}, u32[]{:S(2)}, u32[]{:S(2)}) %all-to-all-start.1) | async-done | bytes 950304 | tf_op jit(solution)/shard_map/all_to_all | solution.py:269
  44.2 6.5 %all-to-all-start = ((bf16[64,2,3712]{2,1,0:T(2,128)(2,1)}), bf16[64,2,3712]{2,1,0:T(2,128)(2,1)S(1)}, u32[]{:S(2)}, u32[]{:S(2)}) async-start(bf16[64,2,3712]{2,1,0:T(2,128)(2,1)} %pack.2), calls=%async_computation | async-start | bytes 1900544 | tf_op jit(solution)/shard_map/all_to_all | solution.py:269
  50.8 1.4 collective-permute-start.8
  52.2 1.5 collective-permute-start.7
  53.7 22.9 %all-to-all-done.x_ref = bf16[64,2,3712]{2,1,0:T(2,128)(2,1)S(1)} async-done(((bf16[64,2,3712]{2,1,0:T(2,128)(2,1)}), bf16[64,2,3712]{2,1,0:T(2,128)(2,1)S(1)}, u32[]{:S(2)}, u32[]{:S(2)}) %all-to-all-start) | async-done | bytes 950304 | tf_op jit(solution)/shard_map/all_to_all | solution.py:269
  78.1 1.5 collective-permute-start
  80.9 2.7 %collective-permute-start.10 = (bf16[64,3712]{1,0:T(8,128)(2,1)S(1)}, bf16[64,3712]{1,0:T(8,128)(2,1)S(1)}, u32[]{:S(2)}, u32[]{:S(2)}) collective-permute-start(bf16[64,3712]{1,0:T(8,128)(2,1)S(1)} %slice.19), channel_id=1, source_target_pairs={{0,192},{64,0},{128,64},{192,128},{1,193},{65,1},{129,65},{193,129... | collective-permute-start | bytes 1425416 | tf_op jit(solution)/shard_map/ppermute | solution.py:216
  83.6 15.9 %collective-permute-done.1.refs_4_ = bf16[128,3712]{1,0:T(8,128)(2,1)S(1)} collective-permute-done((bf16[128,3712]{1,0:T(8,128)(2,1)S(1)}, bf16[128,3712]{1,0:T(8,128)(2,1)S(1)}, u32[]{:S(2)}, u32[]{:S(2)}) %collective-permute-start.1) | collective-permute-done | bytes 950304 | tf_op jit(solution)/shard_map/ppermute | solution.py:216
  99.6 2.7 %collective-permute-start.3 = (bf16[64,3712]{1,0:T(8,128)(2,1)S(1)}, bf16[64,3712]{1,0:T(8,128)(2,1)S(1)}, u32[]{:S(2)}, u32[]{:S(2)}) collective-permute-start(bf16[64,3712]{1,0:T(8,128)(2,1)S(1)} %slice.17), channel_id=1, source_target_pairs={{0,192},{64,0},{128,64},{192,128},{1,193},{65,1},{129,65},{193,129... | collective-permute-start | bytes 1425416 | tf_op jit(solution)/shard_map/ppermute | solution.py:216
  102.4 7.3 %collective-permute-done.9.refs_2_ = bf16[64,3712]{1,0:T(8,128)(2,1)S(1)} collective-permute-done((bf16[64,3712]{1,0:T(8,128)(2,1)S(1)}, bf16[64,3712]{1,0:T(8,128)(2,1)S(1)}, u32[]{:S(2)}, u32[]{:S(2)}) %collective-permute-start.9) | collective-permute-done | bytes 475168 | tf_op jit(solution)/shard_map/ppermute | solution.py:216
  109.7 5.4 %gate_up.3.refs_0_ = bf16[512,256]{1,0:T(8,128)(2,1)S(1)} custom-call(bf16[128,3712]{1,0:T(8,128)(2,1)S(1)} %relayout.3.refs_0_, bf16[128,3712]{1,0:T(8,128)(2,1)} %collective-permute-done.7.refs_1_, bf16[64,3712]{1,0:T(8,128)(2,1)S(1)} %collective-permute-done.9.refs_2_, bf16[64,3712]{1,0:T(8,128)(2,1)S(1)} %collective-permute-done.10.refs_3_, ...), custom_call_target="tpu_custom_call" | custom-call | flops 1000 | bytes 1000 | tf_op jit(solution)/shard_map/gate_up/pallas_call | solution.py:49
  116.2 2.8 %collective-permute-start.12 = (bf16[512,256]{1,0:T(8,128)(2,1)S(1)}, bf16[512,256]{1,0:T(8,128)(2,1)S(1)}, u32[]{:S(2)}, u32[]{:S(2)}) collective-permute-start(bf16[512,256]{1,0:T(8,128)(2,1)S(1)} %gate_up.3.refs_0_), channel_id=1, source_target_pairs={{0,128},{64,192},{128,0},{192,64},{1,129},{65,193},{129,1},{193,65... | collective-permute-start | bytes 786440 | tf_op jit(solution)/shard_map/ppermute | solution.py:216
  119.8 4.2 %gate_up.2.refs_0_ = bf16[512,256]{1,0:T(8,128)(2,1)S(1)} custom-call(bf16[128,3712]{1,0:T(8,128)(2,1)S(1)} %relayout.2.refs_0_, bf16[128,3712]{1,0:T(8,128)(2,1)S(1)} %collective-permute-done.refs_1_, bf16[64,3712]{1,0:T(8,128)(2,1)S(1)} %collective-permute-done.2.refs_2_, bf16[64,3712]{1,0:T(8,128)(2,1)S(1)} %collective-permute-done.3.refs_3_, ...), custom_call_target="tpu_custom_call" | custom-call | flops 1000 | bytes 1000 | tf_op jit(solution)/shard_map/gate_up/pallas_call | solution.py:49
  125.0 2.9 %collective-permute-start.5 = (bf16[512,256]{1,0:T(8,128)(2,1)S(1)}, bf16[512,256]{1,0:T(8,128)(2,1)S(1)}, u32[]{:S(2)}, u32[]{:S(2)}) collective-permute-start(bf16[512,256]{1,0:T(8,128)(2,1)S(1)} %gate_up.2.refs_0_), channel_id=1, source_target_pairs={{0,128},{64,192},{128,0},{192,64},{1,129},{65,193},{129,1},{193,65... | collective-permute-start | bytes 786440 | tf_op jit(solution)/shard_map/ppermute | solution.py:216
  128.4 3.3 %collective-permute-done.12.refs_2_ = bf16[512,256]{1,0:T(8,128)(2,1)S(1)} collective-permute-done((bf16[512,256]{1,0:T(8,128)(2,1)S(1)}, bf16[512,256]{1,0:T(8,128)(2,1)S(1)}, u32[]{:S(2)}, u32[]{:S(2)}) %collective-permute-start.12) | collective-permute-done | bytes 262176 | tf_op jit(solution)/shard_map/ppermute | solution.py:216
  132.4 2.0 copy-done.1
  134.5 2.2 %down.2.refs_5_ = bf16[256,2,2,896]{3,2,1,0:T(2,128)(2,1)} custom-call(s32[1]{0:T(128)} %bitcast.3.me_ref, bf16[512,256]{1,0:T(8,128)(2,1)S(1)} %gate_up.3.refs_0_, bf16[512,256]{1,0:T(8,128)(2,1)S(1)} %collective-permute-done.11.refs_1_, bf16[512,256]{1,0:T(8,128)(2,1)S(1)} %collective-permute-done.12.refs_2_, ...), custom_call_target="tpu_custom_call" | custom-call | flops 1000 | bytes 1000 | tf_op jit(solution)/shard_map/down/pallas_call | solution.py:105
  136.6 5.0 %collective-permute-done.5.refs_2_ = bf16[512,256]{1,0:T(8,128)(2,1)S(1)} collective-permute-done((bf16[512,256]{1,0:T(8,128)(2,1)S(1)}, bf16[512,256]{1,0:T(8,128)(2,1)S(1)}, u32[]{:S(2)}, u32[]{:S(2)}) %collective-permute-start.5) | collective-permute-done | bytes 262176 | tf_op jit(solution)/shard_map/ppermute | solution.py:216
  141.9 2.2 %down.3 = bf16[256,2,2,896]{3,2,1,0:T(2,128)(2,1)} custom-call(s32[1]{0:T(128)} %bitcast.3.me_ref, bf16[512,256]{1,0:T(8,128)(2,1)S(1)} %gate_up.2.refs_0_, bf16[512,256]{1,0:T(8,128)(2,1)S(1)} %collective-permute-done.4.refs_1_, bf16[512,256]{1,0:T(8,128)(2,1)S(1)} %collective-permute-done.5.refs_2_, ...), custom_call_target="tpu_custom_call", output_to_operand_aliasing={{}: (6, {})} | custom-call | flops 1000 | bytes 1000 | tf_op jit(solution)/shard_map/down/pallas_call | solution.py:105
  144.1 10.8 %all-to-all-start.2 = ((bf16[256,2,2,896]{3,2,1,0:T(2,128)(2,1)}), bf16[256,2,2,896]{3,2,1,0:T(2,128)(2,1)S(1)}, u32[]{:S(2)}, u32[]{:S(2)}) async-start(bf16[256,2,2,896]{3,2,1,0:T(2,128)(2,1)} %down.3), calls=%async_computation.2 | async-start | bytes 3670016 | tf_op jit(solution)/shard_map/all_to_all | solution.py:283
  155.7 47.2 %all-to-all-done.2.back_ref = bf16[256,2,2,896]{3,2,1,0:T(2,128)(2,1)S(1)} async-done(((bf16[256,2,2,896]{3,2,1,0:T(2,128)(2,1)}), bf16[256,2,2,896]{3,2,1,0:T(2,128)(2,1)S(1)}, u32[]{:S(2)}, u32[]{:S(2)}) %all-to-all-start.2) | async-done | bytes 1835040 | tf_op jit(solution)/shard_map/all_to_all | solution.py:283
  (55 shorter events, 11.8 us)
Async XLA Ops:
  5.2 39.0 %all-to-all-start.1 = ((bf16[64,2,3712]{2,1,0:T(2,128)(2,1)}), bf16[64,2,3712]{2,1,0:T(2,128)(2,1)S(1)}, u32[]{:S(2)}, u32[]{:S(2)}) async-start(bf16[64,2,3712]{2,1,0:T(2,128)(2,1)} %pack.3), calls=%async_computation.1 | async-start | bytes 1900544 | tf_op jit(solution)/shard_map/all_to_all | solution.py:269
  44.2 32.4 %all-to-all-start = ((bf16[64,2,3712]{2,1,0:T(2,128)(2,1)}), bf16[64,2,3712]{2,1,0:T(2,128)(2,1)S(1)}, u32[]{:S(2)}, u32[]{:S(2)}) async-start(bf16[64,2,3712]{2,1,0:T(2,128)(2,1)} %pack.2), calls=%async_computation | async-start | bytes 1900544 | tf_op jit(solution)/shard_map/all_to_all | solution.py:269
  50.6 59.0 %copy-start.3 = (bf16[128,256]{1,0:T(8,128)(2,1)S(1)}, bf16[128,256]{1,0:T(8,128)(2,1)}, u32[]{:S(2)}) copy-start(bf16[128,256]{1,0:T(8,128)(2,1)} %refs_7_.3) | copy-start | bytes 196612
  50.8 28.9 %collective-permute-start.8 = (bf16[128,3712]{1,0:T(8,128)(2,1)S(1)}, bf16[128,3712]{1,0:T(8,128)(2,1)S(1)}, u32[]{:S(2)}, u32[]{:S(2)}) collective-permute-start(bf16[128,3712]{1,0:T(8,128)(2,1)S(1)} %relayout.3.refs_0_), channel_id=1, source_target_pairs={{0,64},{64,128},{128,192},{192,0},{1,65},{65,129},{129,193},{193,1... | collective-permute-start | bytes 2850824 | tf_op jit(solution)/shard_map/ppermute | solution.py:216
  52.2 27.6 %collective-permute-start.7 = (bf16[128,3712]{1,0:T(8,128)(2,1)S(1)}, bf16[128,3712]{1,0:T(8,128)(2,1)}, u32[]{:S(2)}, u32[]{:S(2)}) collective-permute-start(bf16[128,3712]{1,0:T(8,128)(2,1)S(1)} %relayout.3.refs_0_), channel_id=1, source_target_pairs={{0,192},{64,0},{128,64},{192,128},{1,193},{65,1},{129,65},{193,129... | collective-permute-start | bytes 2850824 | tf_op jit(solution)/shard_map/ppermute | solution.py:216
  76.6 33.0 %copy-start = (bf16[2,3584,256]{2,1,0:T(8,128)(2,1)S(1)}, bf16[2,3584,256]{2,1,0:T(8,128)(2,1)}, u32[]{:S(2)}) copy-start(bf16[2,3584,256]{2,1,0:T(8,128)(2,1)} %refs_5_.3) | copy-start | bytes 11010052
  76.8 22.7 %collective-permute-start.1 = (bf16[128,3712]{1,0:T(8,128)(2,1)S(1)}, bf16[128,3712]{1,0:T(8,128)(2,1)S(1)}, u32[]{:S(2)}, u32[]{:S(2)}) collective-permute-start(bf16[128,3712]{1,0:T(8,128)(2,1)S(1)} %relayout.2.refs_0_), channel_id=1, source_target_pairs={{0,64},{64,128},{128,192},{192,0},{1,65},{65,129},{129,193},{193,1... | collective-permute-start | bytes 2850824 | tf_op jit(solution)/shard_map/ppermute | solution.py:216
  78.1 21.5 %collective-permute-start = (bf16[128,3712]{1,0:T(8,128)(2,1)S(1)}, bf16[128,3712]{1,0:T(8,128)(2,1)S(1)}, u32[]{:S(2)}, u32[]{:S(2)}) collective-permute-start(bf16[128,3712]{1,0:T(8,128)(2,1)S(1)} %relayout.2.refs_0_), channel_id=1, source_target_pairs={{0,192},{64,0},{128,64},{192,128},{1,193},{65,1},{129,65},{193,129... | collective-permute-start | bytes 2850824 | tf_op jit(solution)/shard_map/ppermute | solution.py:216
  79.7 29.9 %collective-permute-start.9 = (bf16[64,3712]{1,0:T(8,128)(2,1)S(1)}, bf16[64,3712]{1,0:T(8,128)(2,1)S(1)}, u32[]{:S(2)}, u32[]{:S(2)}) collective-permute-start(bf16[64,3712]{1,0:T(8,128)(2,1)S(1)} %slice.18), channel_id=1, source_target_pairs={{0,64},{64,128},{128,192},{192,0},{1,65},{65,129},{129,193},{193,1... | collective-permute-start | bytes 1425416 | tf_op jit(solution)/shard_map/ppermute | solution.py:216
  80.9 28.8 %collective-permute-start.10 = (bf16[64,3712]{1,0:T(8,128)(2,1)S(1)}, bf16[64,3712]{1,0:T(8,128)(2,1)S(1)}, u32[]{:S(2)}, u32[]{:S(2)}) collective-permute-start(bf16[64,3712]{1,0:T(8,128)(2,1)S(1)} %slice.19), channel_id=1, source_target_pairs={{0,192},{64,0},{128,64},{192,128},{1,193},{65,1},{129,65},{193,129... | collective-permute-start | bytes 1425416 | tf_op jit(solution)/shard_map/ppermute | solution.py:216
  99.5 20.3 %collective-permute-start.2 = (bf16[64,3712]{1,0:T(8,128)(2,1)S(1)}, bf16[64,3712]{1,0:T(8,128)(2,1)S(1)}, u32[]{:S(2)}, u32[]{:S(2)}) collective-permute-start(bf16[64,3712]{1,0:T(8,128)(2,1)S(1)} %slice.16), channel_id=1, source_target_pairs={{0,64},{64,128},{128,192},{192,0},{1,65},{65,129},{129,193},{193,1... | collective-permute-start | bytes 1425416 | tf_op jit(solution)/shard_map/ppermute | solution.py:216
  99.6 20.2 %collective-permute-start.3 = (bf16[64,3712]{1,0:T(8,128)(2,1)S(1)}, bf16[64,3712]{1,0:T(8,128)(2,1)S(1)}, u32[]{:S(2)}, u32[]{:S(2)}) collective-permute-start(bf16[64,3712]{1,0:T(8,128)(2,1)S(1)} %slice.17), channel_id=1, source_target_pairs={{0,192},{64,0},{128,64},{192,128},{1,193},{65,1},{129,65},{193,129... | collective-permute-start | bytes 1425416 | tf_op jit(solution)/shard_map/ppermute | solution.py:216
  115.0 12.9 %collective-permute-start.13 = (bf16[512,256]{1,0:T(8,128)(2,1)S(1)}, bf16[512,256]{1,0:T(8,128)(2,1)S(1)}, u32[]{:S(2)}, u32[]{:S(2)}) collective-permute-start(bf16[512,256]{1,0:T(8,128)(2,1)S(1)} %gate_up.3.refs_0_), channel_id=1, source_target_pairs={{0,64},{64,128},{128,192},{192,0},{1,65},{65,129},{129,193},{193,1... | collective-permute-start | bytes 786440 | tf_op jit(solution)/shard_map/ppermute | solution.py:216
  116.2 15.5 %collective-permute-start.12 = (bf16[512,256]{1,0:T(8,128)(2,1)S(1)}, bf16[512,256]{1,0:T(8,128)(2,1)S(1)}, u32[]{:S(2)}, u32[]{:S(2)}) collective-permute-start(bf16[512,256]{1,0:T(8,128)(2,1)S(1)} %gate_up.3.refs_0_), channel_id=1, source_target_pairs={{0,128},{64,192},{128,0},{192,64},{1,129},{65,193},{129,1},{193,65... | collective-permute-start | bytes 786440 | tf_op jit(solution)/shard_map/ppermute | solution.py:216
  119.0 13.4 %collective-permute-start.11 = (bf16[512,256]{1,0:T(8,128)(2,1)S(1)}, bf16[512,256]{1,0:T(8,128)(2,1)S(1)}, u32[]{:S(2)}, u32[]{:S(2)}) collective-permute-start(bf16[512,256]{1,0:T(8,128)(2,1)S(1)} %gate_up.3.refs_0_), channel_id=1, source_target_pairs={{0,192},{64,0},{128,64},{192,128},{1,193},{65,1},{129,65},{193,129... | collective-permute-start | bytes 786440 | tf_op jit(solution)/shard_map/ppermute | solution.py:216
  124.0 12.6 %collective-permute-start.6 = (bf16[512,256]{1,0:T(8,128)(2,1)S(1)}, bf16[512,256]{1,0:T(8,128)(2,1)S(1)}, u32[]{:S(2)}, u32[]{:S(2)}) collective-permute-start(bf16[512,256]{1,0:T(8,128)(2,1)S(1)} %gate_up.2.refs_0_), channel_id=1, source_target_pairs={{0,64},{64,128},{128,192},{192,0},{1,65},{65,129},{129,193},{193,1... | collective-permute-start | bytes 786440 | tf_op jit(solution)/shard_map/ppermute | solution.py:216
  125.0 16.6 %collective-permute-start.5 = (bf16[512,256]{1,0:T(8,128)(2,1)S(1)}, bf16[512,256]{1,0:T(8,128)(2,1)S(1)}, u32[]{:S(2)}, u32[]{:S(2)}) collective-permute-start(bf16[512,256]{1,0:T(8,128)(2,1)S(1)} %gate_up.2.refs_0_), channel_id=1, source_target_pairs={{0,128},{64,192},{128,0},{192,64},{1,129},{65,193},{129,1},{193,65... | collective-permute-start | bytes 786440 | tf_op jit(solution)/shard_map/ppermute | solution.py:216
  128.0 14.0 %collective-permute-start.4 = (bf16[512,256]{1,0:T(8,128)(2,1)S(1)}, bf16[512,256]{1,0:T(8,128)(2,1)S(1)}, u32[]{:S(2)}, u32[]{:S(2)}) collective-permute-start(bf16[512,256]{1,0:T(8,128)(2,1)S(1)} %gate_up.2.refs_0_), channel_id=1, source_target_pairs={{0,192},{64,0},{128,64},{192,128},{1,193},{65,1},{129,65},{193,129... | collective-permute-start | bytes 786440 | tf_op jit(solution)/shard_map/ppermute | solution.py:216
  132.4 2.0 copy-start.1
  134.4 7.5 %copy-start.2 = (bf16[2,1024,896]{2,1,0:T(8,128)(2,1)S(1)}, bf16[2,1024,896]{2,1,0:T(8,128)(2,1)}, u32[]{:S(2)}) copy-start(bf16[2,1024,896]{2,1,0:T(8,128)(2,1)} %refs_4_.3) | copy-start | bytes 11010052
  144.1 10.8 %copy-start.4 = (bf16[16,8]{0,1:T(8,128)(2,1)S(1)}, bf16[16,8]{0,1:T(8,128)(2,1)}, u32[]{:S(2)}) copy-start(bf16[16,8]{0,1:T(8,128)(2,1)} %param.11) | copy-start | bytes 772
  144.1 58.7 %all-to-all-start.2 = ((bf16[256,2,2,896]{3,2,1,0:T(2,128)(2,1)}), bf16[256,2,2,896]{3,2,1,0:T(2,128)(2,1)S(1)}, u32[]{:S(2)}, u32[]{:S(2)}) async-start(bf16[256,2,2,896]{3,2,1,0:T(2,128)(2,1)} %down.3), calls=%async_computation.2 | async-start | bytes 3670016 | tf_op jit(solution)/shard_map/all_to_all | solution.py:283
